TPU v7x, 32 devices: a whole 2x2x4 slice. The times are simulated.
32 devices in a mesh: seq: 8 (over z, x), fsdp: 4 (over y, core).
Axes of the slice: x: 2, y: 2, z: 4, core: 2. Of those that a mesh axis runs over, the one named last changes fastest.
Arguments:
- tokens: bfloat16 [4, 1024, 2048], P('fsdp', 'seq'), may hold values from -6 to 6
- block_pos: int32 [4, 8], P('fsdp'), may hold values from 0 to 7, each once within a row
- w_query: bfloat16 [2048, 2048], P(('seq', 'fsdp')), may hold values from -0.125 to 0.125
- key_weight: bfloat16 [2048, 1024], P(('seq', 'fsdp')), may hold values from -0.125 to 0.125
- value_weight: bfloat16 [2048, 1024], P(('seq', 'fsdp')), may hold values from -0.125 to 0.125
- w_out: bfloat16 [2048, 2048], P(('seq', 'fsdp')), may hold values from -0.375 to 0.375
- w_gate: bfloat16 [2048, 6144], P(('seq', 'fsdp')), may hold values from -0.125 to 0.125
- w_up: bfloat16 [2048, 6144], P(('seq', 'fsdp')), may hold values from -0.125 to 0.125
- w_down: bfloat16 [2048, 6144], P(('seq', 'fsdp')), may hold values from -0.15625 to 0.15625
- attn_gain: bfloat16 [2048], P(('seq', 'fsdp')), may hold values from 0.099609375 to 1.8984375
- mlp_gain: bfloat16 [2048], P(('seq', 'fsdp')), may hold values from 0.099609375 to 1.8984375
- qk_gain: bfloat16 [2, 128], P(None, ('seq', 'fsdp')), may hold values from 0.099609375 to 1.8984375
- grad_out: bfloat16 [4, 1024, 2048], P('fsdp', 'seq'), may hold values from -6 to 6
Outputs:
- output: bfloat16 [4, 1024, 2048], P('fsdp', 'seq')
- grad_tokens: float32 [4, 1024, 2048], P('fsdp', 'seq')
- grad_query: float32 [2048, 2048], P(('seq', 'fsdp'))
- grad_key: float32 [2048, 1024], P(('seq', 'fsdp'))
- grad_value: float32 [2048, 1024], P(('seq', 'fsdp'))
- grad_outproj: float32 [2048, 2048], P(('seq', 'fsdp'))
- grad_gate: float32 [2048, 6144], P(('seq', 'fsdp'))
- grad_up: float32 [2048, 6144], P(('seq', 'fsdp'))
- grad_down: float32 [2048, 6144], P(('seq', 'fsdp'))
- grad_attn_gain: float32 [2048], P(('seq', 'fsdp'))
- grad_mlp_gain: float32 [2048], P(('seq', 'fsdp'))
- grad_qk_gain: float32 [2, 128], P(None, ('seq', 'fsdp'))
Inputs may be any that keep to these rules, and one draw needn't show every extreme that they name: Each row of block_pos is a permutation: index s of seq holds positions block_pos[f, s] * 128 to block_pos[f, s] * 128 + 127 of sequence f.
All inputs are finite; a program needn't handle non-finite values.
Results may differ from a plain program's by a relative error of at most 0.02.
Values may be sent and summed in bfloat16 or wider, within the bound.
No kernel may reach another device: no remote copies, remote signals or barrier semaphores. Data moves between devices by JAX's collectives and lax.ppermute only.
A program may use at most 640 MiB of HBM per device.

v0:
```python
import jax
import jax.numpy as jnp
from jax import lax
from jax.sharding import PartitionSpec as P

QUERY_HEADS = 16
KEY_VALUE_HEADS = 8
HEAD_SIZE = 128
FF = 6144


rope_base = 1000000.0
norm_eps = 1e-06


def from_behind(block, axis, distance):
    devices = range(lax.axis_size(axis))
    route = [((i - distance) % len(devices), i) for i in devices]
    return lax.ppermute(block, axis, route)


def matrix_product(left, right):
    return jnp.dot(left, right, preferred_element_type=jnp.float32)


def matmul_t(left, right):
    return lax.dot_general(
        left, right, (((1,), (1,)), ((), ())), preferred_element_type=jnp.float32
    )


def matmul_tn(left, right):
    return lax.dot_general(
        left, right, (((0,), (0,)), ((), ())), preferred_element_type=jnp.float32
    )


def rms_norm(tensor, gain):
    return tensor * lax.rsqrt(jnp.mean(tensor * tensor, axis=-1, keepdims=True) + norm_eps) * gain


def norm_back(tensor, gain, incoming):
    inv_root = lax.rsqrt(jnp.mean(tensor * tensor, axis=-1, keepdims=True) + norm_eps)
    scaled = gain * incoming
    grad_tensor = inv_root * scaled - tensor * (inv_root * inv_root * inv_root) * jnp.mean(
        scaled * tensor, axis=-1, keepdims=True
    )
    return (grad_tensor, incoming * tensor * inv_root)


def rope_angles(positions):
    exponent = jnp.arange(HEAD_SIZE // 2, dtype=jnp.float32) * (-2.0 / HEAD_SIZE)
    frequency = rope_base**exponent
    return positions.astype(jnp.float32)[:, None] * frequency[None, :]


def rotate(tensor, angles):
    half_width = tensor.shape[-1] // 2
    cosine = jnp.cos(angles)[:, None, :]
    sine_part = jnp.sin(angles)[:, None, :]
    front_half = tensor[..., :half_width]
    back_half = tensor[..., half_width:]
    return jnp.concatenate(
        [front_half * cosine - back_half * sine_part, back_half * cosine + front_half * sine_part],
        axis=-1,
    )


def unrotate(tensor, angles):
    half_width = tensor.shape[-1] // 2
    cosine = jnp.cos(angles)[:, None, :]
    sine_part = jnp.sin(angles)[:, None, :]
    front_half = tensor[..., :half_width]
    back_half = tensor[..., half_width:]
    return jnp.concatenate(
        [front_half * cosine + back_half * sine_part, back_half * cosine - front_half * sine_part],
        axis=-1,
    )


def on_device(
    tokens,
    block_pos,
    w_query,
    key_weight,
    value_weight,
    w_out,
    w_gate,
    w_up,
    w_down,
    attn_gain,
    mlp_gain,
    qk_gain,
    grad_out,
):
    cycle_size = lax.axis_size("seq")
    cycle_index = lax.axis_index("seq")
    token_rows = tokens.shape[1]
    queries_per_group = QUERY_HEADS // KEY_VALUE_HEADS
    score_scale = HEAD_SIZE ** (-0.5)
    order = block_pos[0]
    own_block = order[cycle_index]
    row_offsets = jnp.arange(token_rows, dtype=jnp.int32)
    local_pos = own_block * token_rows + row_offsets
    angles = rope_angles(local_pos)
    inputs = tokens[0].astype(jnp.float32)
    attn_full = (
        lax.all_gather(w_query, ("seq", "fsdp"), axis=0, tiled=True),
        lax.all_gather(key_weight, ("seq", "fsdp"), axis=0, tiled=True),
        lax.all_gather(value_weight, ("seq", "fsdp"), axis=0, tiled=True),
        lax.all_gather(w_out, ("seq", "fsdp"), axis=0, tiled=True),
        lax.all_gather(attn_gain, ("seq", "fsdp"), axis=0, tiled=True),
        lax.all_gather(qk_gain, ("seq", "fsdp"), axis=1, tiled=True),
    )
    wq_all, key_weight_gathered, wv_all, wo_all, gain_all, qkg_all = attn_full
    first_gain = gain_all.astype(jnp.float32)
    query_gain = qkg_all[0].astype(jnp.float32)
    key_gain = qkg_all[1].astype(jnp.float32)
    normalized_input = rms_norm(inputs, first_gain).astype(jnp.bfloat16)
    q_heads = matrix_product(normalized_input, wq_all).reshape(token_rows, QUERY_HEADS, HEAD_SIZE)
    key_head_rows = matrix_product(normalized_input, key_weight_gathered).reshape(
        token_rows, KEY_VALUE_HEADS, HEAD_SIZE
    )
    value_matrix_rows = matrix_product(normalized_input, wv_all).astype(jnp.bfloat16)
    query_rows = rotate(rms_norm(q_heads, query_gain), angles).astype(jnp.bfloat16)
    rotated_keys = rotate(rms_norm(key_head_rows, key_gain), angles).astype(jnp.bfloat16)
    diagonal_block_pair = jnp.stack(
        [rotated_keys, value_matrix_rows.reshape(token_rows, KEY_VALUE_HEADS, HEAD_SIZE)]
    )
    grouped_queries = query_rows.reshape(token_rows, KEY_VALUE_HEADS, queries_per_group, HEAD_SIZE)

    def attend(carry, pair, key_pos):
        row_top, totals, accum = carry
        scores = (
            jnp.einsum(
                "qkgd,tkd->kgqt", grouped_queries, pair[0], preferred_element_type=jnp.float32
            )
            * score_scale
        )
        visible = local_pos[:, None] >= key_pos[None, :]
        scores = jnp.where(visible, scores, -1e30)
        new_top = jnp.maximum(row_top, jnp.max(scores, axis=-1))
        weights = jnp.exp(scores - new_top[..., None])
        factor = jnp.exp(row_top - new_top)
        totals = factor * totals + jnp.sum(weights, axis=-1)
        accum = factor[..., None] * accum + jnp.einsum(
            "kgqt,tkd->kgqd",
            weights.astype(jnp.bfloat16),
            pair[1],
            preferred_element_type=jnp.float32,
        )
        return (new_top, totals, accum)

    def forward_turn(turn_index, state):
        pair, carry = state
        source = (cycle_index - turn_index) % cycle_size
        key_start = order[source]
        key_pos = key_start * token_rows + row_offsets

        def forward_take_block(carry_in):
            return attend(carry_in, pair, key_pos)

        def forward_skip_block(carry_in):
            return carry_in

        carry = lax.cond(key_start <= own_block, forward_take_block, forward_skip_block, carry)
        pair = from_behind(pair, "seq", 1)
        return (pair, carry)

    start_carry = (
        jnp.full((KEY_VALUE_HEADS, queries_per_group, token_rows), -1e30, jnp.float32),
        jnp.zeros((KEY_VALUE_HEADS, queries_per_group, token_rows), jnp.float32),
        jnp.zeros((KEY_VALUE_HEADS, queries_per_group, token_rows, HEAD_SIZE), jnp.float32),
    )
    ignored, (row_top, totals, accum) = lax.fori_loop(
        0, cycle_size, forward_turn, (diagonal_block_pair, start_carry)
    )
    log_total = row_top + jnp.log(totals)
    attended_heads = accum / totals[..., None]
    attended = (
        jnp.transpose(attended_heads, (2, 0, 1, 3))
        .reshape(token_rows, QUERY_HEADS * HEAD_SIZE)
        .astype(jnp.bfloat16)
    )
    mlp_full = (
        lax.all_gather(w_gate, ("seq", "fsdp"), axis=0, tiled=True),
        lax.all_gather(w_up, ("seq", "fsdp"), axis=0, tiled=True),
        lax.all_gather(w_down, ("seq", "fsdp"), axis=0, tiled=True),
        lax.all_gather(mlp_gain, ("seq", "fsdp"), axis=0, tiled=True),
    )
    wg_all, wu_all, wd_all, gain_two = mlp_full
    second_gain = gain_two.astype(jnp.float32)
    middle = inputs + matmul_t(attended, wo_all)
    normed2 = rms_norm(middle, second_gain).astype(jnp.bfloat16)
    gate_act = matrix_product(normed2, wg_all)
    up_act = matrix_product(normed2, wu_all)
    inner = (jax.nn.silu(gate_act) * up_act).astype(jnp.bfloat16)
    result = (middle + matmul_t(inner, wd_all)).astype(jnp.bfloat16)
    wg_back, wu_back, wd_back, gain_back = (
        lax.all_gather(w_gate, ("seq", "fsdp"), axis=0, tiled=True),
        lax.all_gather(w_up, ("seq", "fsdp"), axis=0, tiled=True),
        lax.all_gather(w_down, ("seq", "fsdp"), axis=0, tiled=True),
        lax.all_gather(mlp_gain, ("seq", "fsdp"), axis=0, tiled=True),
    )
    grad_rows = grad_out[0]
    grad_inner = matrix_product(grad_rows, wd_back)
    sigmoid_gate = jax.nn.sigmoid(gate_act)
    d_gate = (grad_inner * up_act * sigmoid_gate * (1.0 + gate_act * (1.0 - sigmoid_gate))).astype(
        jnp.bfloat16
    )
    d_up = (grad_inner * gate_act * sigmoid_gate).astype(jnp.bfloat16)
    grad_normed2 = matmul_t(d_gate, wg_back) + matmul_t(d_up, wu_back)
    grad_mid_norm, mlp_gain_terms = norm_back(middle, second_gain, grad_normed2)
    grad_middle = grad_rows.astype(jnp.float32) + grad_mid_norm
    mlp_gain_grad = jnp.sum(mlp_gain_terms, axis=0)
    gate_and_up = jnp.concatenate([d_gate, d_up], axis=1)
    left_norm = normed2
    mlp_grads = lax.psum_scatter(
        jnp.concatenate([matmul_tn(left_norm, gate_and_up), matmul_tn(grad_rows, inner)], axis=1),
        ("seq", "fsdp"),
        scatter_dimension=0,
        tiled=True,
    )
    wq_back, wk_back, wv_back, wo_back, gain_one, qkg_back = (
        lax.all_gather(w_query, ("seq", "fsdp"), axis=0, tiled=True),
        lax.all_gather(key_weight, ("seq", "fsdp"), axis=0, tiled=True),
        lax.all_gather(value_weight, ("seq", "fsdp"), axis=0, tiled=True),
        lax.all_gather(w_out, ("seq", "fsdp"), axis=0, tiled=True),
        lax.all_gather(attn_gain, ("seq", "fsdp"), axis=0, tiled=True),
        lax.all_gather(qk_gain, ("seq", "fsdp"), axis=1, tiled=True),
    )
    d_branch = grad_middle.astype(jnp.bfloat16)
    attended_gradient = matrix_product(d_branch, wo_back).astype(jnp.bfloat16)
    grouped_gradient = attended_gradient.reshape(
        token_rows, KEY_VALUE_HEADS, queries_per_group, HEAD_SIZE
    )
    delta = jnp.sum(
        jnp.transpose(grouped_gradient, (1, 2, 0, 3)).astype(jnp.float32) * attended_heads, axis=-1
    )

    def gradient_block(state, pair, key_pos):
        grad_query, key_value_gradients = state
        scores = (
            jnp.einsum(
                "qkgd,tkd->kgqt", grouped_queries, pair[0], preferred_element_type=jnp.float32
            )
            * score_scale
        )
        visible = local_pos[:, None] >= key_pos[None, :]
        scores = jnp.where(visible, scores, -1e30)
        weights = jnp.exp(scores - log_total[..., None])
        grad_weights = jnp.einsum(
            "qkgd,tkd->kgqt", grouped_gradient, pair[1], preferred_element_type=jnp.float32
        )
        d_scores = (weights * (grad_weights - delta[..., None])).astype(jnp.bfloat16)
        grad_query = grad_query + jnp.einsum(
            "kgqt,tkd->kgqd", d_scores, pair[0], preferred_element_type=jnp.float32
        )
        key_part = jnp.einsum(
            "kgqt,qkgd->tkd", d_scores, grouped_queries, preferred_element_type=jnp.float32
        )
        value_part = jnp.einsum(
            "kgqt,qkgd->tkd",
            weights.astype(jnp.bfloat16),
            grouped_gradient,
            preferred_element_type=jnp.float32,
        )
        return (grad_query, key_value_gradients + jnp.stack([key_part, value_part]))

    def backward_turn(turn_index, state):
        pair, key_value_gradients, grad_query = state
        source = (cycle_index + turn_index) % cycle_size
        key_start = order[source]
        key_pos = key_start * token_rows + row_offsets

        def backward_take_block(inner_state):
            return gradient_block(inner_state, pair, key_pos)

        def backward_skip_block(inner_state):
            return inner_state

        grad_query, key_value_gradients = lax.cond(
            key_start <= own_block,
            backward_take_block,
            backward_skip_block,
            (grad_query, key_value_gradients),
        )
        key_value_gradients = from_behind(
            key_value_gradients.astype(jnp.bfloat16), "seq", -1
        ).astype(key_value_gradients.dtype)
        pair = from_behind(pair, "seq", -1)
        return (pair, key_value_gradients, grad_query)

    start_state = (
        diagonal_block_pair,
        jnp.zeros((2, token_rows, KEY_VALUE_HEADS, HEAD_SIZE), jnp.float32),
        jnp.zeros((KEY_VALUE_HEADS, queries_per_group, token_rows, HEAD_SIZE), jnp.float32),
    )
    ignored_pair, key_value_gradients, grad_query = lax.fori_loop(
        0, cycle_size, backward_turn, start_state
    )
    grad_queries = jnp.transpose(grad_query * score_scale, (2, 0, 1, 3)).reshape(
        token_rows, QUERY_HEADS, HEAD_SIZE
    )
    grad_keys = key_value_gradients[0] * score_scale
    value_gradient = (
        key_value_gradients[1].reshape(token_rows, KEY_VALUE_HEADS * HEAD_SIZE).astype(jnp.bfloat16)
    )
    grad_q_heads, query_gain_terms = norm_back(q_heads, query_gain, unrotate(grad_queries, angles))
    key_heads_gradient, key_gain_terms = norm_back(
        key_head_rows, key_gain, unrotate(grad_keys, angles)
    )
    d_q_pre = grad_q_heads.reshape(token_rows, QUERY_HEADS * HEAD_SIZE).astype(jnp.bfloat16)
    key_before_rotation_gradient = key_heads_gradient.reshape(
        token_rows, KEY_VALUE_HEADS * HEAD_SIZE
    ).astype(jnp.bfloat16)
    qk_gain_grad = jnp.stack(
        [jnp.sum(query_gain_terms, axis=(0, 1)), jnp.sum(key_gain_terms, axis=(0, 1))]
    )
    grad_normed = (
        matmul_t(d_q_pre, wq_back)
        + matmul_t(key_before_rotation_gradient, wk_back)
        + matmul_t(value_gradient, wv_back)
    )
    grad_in_norm, attn_gain_terms = norm_back(inputs, first_gain, grad_normed)
    grad_input = grad_middle + grad_in_norm
    attn_gain_grad = jnp.sum(attn_gain_terms, axis=0)
    projections = jnp.concatenate([d_q_pre, key_before_rotation_gradient, value_gradient], axis=1)
    left_norm = normalized_input
    attn_grads = lax.psum_scatter(
        jnp.concatenate([matmul_tn(left_norm, projections), matmul_tn(d_branch, attended)], axis=1),
        ("seq", "fsdp"),
        scatter_dimension=0,
        tiled=True,
    )
    gains_done = (
        lax.psum_scatter(attn_gain_grad, ("seq", "fsdp"), scatter_dimension=0, tiled=True),
        lax.psum_scatter(mlp_gain_grad, ("seq", "fsdp"), scatter_dimension=0, tiled=True),
        lax.psum_scatter(qk_gain_grad, ("seq", "fsdp"), scatter_dimension=1, tiled=True),
    )
    query_cols = QUERY_HEADS * HEAD_SIZE
    key_value_columns = KEY_VALUE_HEADS * HEAD_SIZE
    grad_wq = attn_grads[:, :query_cols]
    grad_wk = attn_grads[:, query_cols : query_cols + key_value_columns]
    grad_wv = attn_grads[:, query_cols + key_value_columns : query_cols + 2 * key_value_columns]
    grad_wo = attn_grads[:, query_cols + 2 * key_value_columns :]
    grad_wg = mlp_grads[:, :FF]
    grad_wu = mlp_grads[:, FF : 2 * FF]
    grad_wd = mlp_grads[:, 2 * FF :]
    return (
        result[None],
        grad_input[None],
        grad_wq,
        grad_wk,
        grad_wv,
        grad_wo,
        grad_wg,
        grad_wu,
        grad_wd,
        gains_done[0],
        gains_done[1],
        gains_done[2],
    )


def solution(mesh):
    placed = (
        P("fsdp", "seq", None),
        P("fsdp", None),
        P(("seq", "fsdp"), None),
        P(("seq", "fsdp"), None),
        P(("seq", "fsdp"), None),
        P(("seq", "fsdp"), None),
        P(("seq", "fsdp"), None),
        P(("seq", "fsdp"), None),
        P(("seq", "fsdp"), None),
        P(("seq", "fsdp")),
        P(("seq", "fsdp")),
        P(None, ("seq", "fsdp")),
        P("fsdp", "seq", None),
    )
    return jax.shard_map(
        on_device,
        mesh=mesh,
        in_specs=placed,
        out_specs=(
            P("fsdp", "seq", None),
            P("fsdp", "seq", None),
            P(("seq", "fsdp"), None),
            P(("seq", "fsdp"), None),
            P(("seq", "fsdp"), None),
            P(("seq", "fsdp"), None),
            P(("seq", "fsdp"), None),
            P(("seq", "fsdp"), None),
            P(("seq", "fsdp"), None),
            P(("seq", "fsdp")),
            P(("seq", "fsdp")),
            P(None, ("seq", "fsdp")),
        ),
        check_vma=False,
    )
```

profile of v0, /device:TPU:0, one launch (start us, length us, event | category | flops | bytes accessed | tf_op | source)
XLA Modules:
  0.0 2911.7 jit_solution(11071426926747302599)
XLA Ops:
  13.7 42.4 %all-reduce.6 = (bf16[2048]{0:T(1024)(128)(2,1)S(1)}, bf16[2048]{0:T(1024)(128)(2,1)S(1)}) all-reduce(bf16[2048]{0:T(1024)(128)(2,1)S(1)} %dynamic-update-slice, bf16[2048]{0:T(1024)(128)(2,1)S(1)} %dynamic-update-slice.1), channel_id=1, replica_groups=mesh['seq'=8,'fsdp'=4] {'seq','fsdp'}, use_global_device_ids=true, to_apply=%add | all-reduce | flops 4096 | bytes 16384
  56.1 40.1 %all-gather = bf16[32,4,2]{1,2,0:T(2,128)(2,1)S(1)} all-gather(bf16[1,4,2]{1,2,0:T(2,128)(2,1)} %bitcast.241), channel_id=1, replica_groups=mesh['seq'=8,'fsdp'=4] {'seq','fsdp'}, dimensions={0}, use_global_device_ids=true | all-gather | bytes 528 | tf_op jit(solution)/shard_map/all_gather | solution.py:113
  103.5 35.8 %all-gather.9.cloned.1.call-done = bf16[2048,1024]{1,0:T(8,128)(2,1)} async-done(((bf16[64,1024]{1,0:T(8,128)(2,1)}), bf16[2048,1024]{1,0:T(8,128)(2,1)}) %all-gather.9.cloned.1.call-update) | async-done | bytes 4194320 | tf_op jit(solution)/shard_map/all_gather | solution.py:109
  150.5 67.8 %all-gather.13.cloned.1.call-done = bf16[2048,2048]{1,0:T(8,128)(2,1)} async-done(((bf16[64,2048]{1,0:T(8,128)(2,1)}), bf16[2048,2048]{1,0:T(8,128)(2,1)}) %all-gather.13.cloned.1.call-update) | async-done | bytes 8388624 | tf_op jit(solution)/shard_map/all_gather | solution.py:108
  238.9 185.5 %while.42 = (s32[]{:T(128)}, bf16[2,128,8,128]{3,1,2,0:T(8,128)(2,1)S(1)}, f32[8,2,128]{2,1,0:T(2,128)S(1)}, f32[8,2,128]{2,1,0:T(2,128)S(1)}, f32[8,2,128,128]{...) while((s32[]{:T(128)}, ...), condition=%wide.region_8.9_spmd.clone, body=%wide.region_3.8_spmd.clone.sunk | while | flops 136597776 | bytes 9605110 | solution.py:175
  247.0 16.1 collective-permute-done
  265.8 16.9 collective-permute-done
  285.4 25.7 collective-permute-done
  328.5 15.9 collective-permute-done
  347.1 23.7 collective-permute-done
  377.4 20.8 collective-permute-done
  404.9 19.4 collective-permute-done
  432.6 77.0 %all-gather.19.cloned.1.call-done = bf16[2048,6144]{1,0:T(8,128)(2,1)} async-done(((bf16[64,6144]{1,0:T(8,128)(2,1)}), bf16[2048,6144]{1,0:T(8,128)(2,1)}) %all-gather.19.cloned.1.call-update) | async-done | bytes 25165840 | tf_op jit(solution)/shard_map/all_gather | solution.py:187
  509.7 13.3 fusion.86
  522.9 142.3 %all-gather.17.cloned.1.call-done = bf16[2048,6144]{1,0:T(8,128)(2,1)} async-done(((bf16[64,6144]{1,0:T(8,128)(2,1)}), bf16[2048,6144]{1,0:T(8,128)(2,1)}) %all-gather.17.cloned.1.call-update) | async-done | bytes 25165840 | tf_op jit(solution)/shard_map/all_gather | solution.py:186
  665.3 13.2 fusion.85
  678.5 142.5 %all-gather.21.cloned.1.call-done = bf16[2048,6144]{1,0:T(8,128)(2,1)} async-done(((bf16[64,6144]{1,0:T(8,128)(2,1)}), bf16[2048,6144]{1,0:T(8,128)(2,1)}) %all-gather.21.cloned.1.call-update) | async-done | bytes 25165840 | tf_op jit(solution)/shard_map/all_gather | solution.py:188
  821.0 15.3 multiply_convert_fusion
  836.3 13.5 fusion.87
  849.8 15.1 multiply_reduce_fusion.1
  877.1 248.9 %while.43 = (s32[]{:T(128)}, bf16[2,128,8,128]{3,1,2,0:T(8,128)(2,1)S(1)}, f32[2,128,8,128]{3,1,2,0:T(8,128)}, f32[8,2,128,128]{3,2,1,0:T(8,128)}, s32[]{:T(128)...) while((s32[]{:T(128)}, ...), condition=%wide.region_15.16_spmd.clone, body=%wide.region_12.15_spmd.clone.sunk | while | flops 338968864 | bytes 32821360 | solution.py:299
  922.5 12.7 collective-permute-done.2
  957.8 12.7 collective-permute-done.2
  1142.6 14.0 fusion.55
  1156.6 33.6 %pad_maximum_fusion.1 = f32[2048,6144]{1,0:T(8,128)} fusion(f32[2048,2048]{1,0:T(8,128)} %fusion.68, f32[2048,4096]{1,0:T(8,128)} %fusion.55), kind=kLoop, calls=%fused_computation.46 | loop fusion | flops 12582912 | bytes 100663296 | tf_op jit(solution)/shard_map/concatenate | solution.py:331
  1191.6 28.2 convolution_bitcast_fusion.3
  1219.9 53.1 %fusion.32 = f32[2048,12288]{1,0:T(8,128)} fusion(bf16[128,2048]{1,0:T(8,128)(2,1)} %copy-done.19, bf16[128,6144]{1,0:T(8,128)(2,1)} %get-tuple-element.937, bf16[128,6144]{1,0:T(8,128)(2,1)S(1)} %copy-done.18), kind=kOutput, calls=%fused_computation.48 | convolution fusion | flops 6448742400 | bytes 104333312 | tf_op jit(solution)/shard_map/dot_general | solution.py:33
  1273.0 100.8 %pad_maximum_fusion = f32[2048,18432]{1,0:T(8,128)} fusion(f32[2048,6144]{1,0:T(8,128)} %convolution_bitcast_fusion.3, f32[2048,12288]{1,0:T(8,128)} %fusion.32), kind=kLoop, calls=%fused_computation.45 | loop fusion | flops 37748736 | bytes 301989888 | tf_op jit(solution)/shard_map/concatenate | solution.py:219
  1387.1 47.0 %all-reduce.5 = (f32[2048]{0:T(1024)S(1)}, f32[2048]{0:T(1024)S(1)}, f32[2,128]{1,0:T(2,128)S(1)}) all-reduce(f32[2048]{0:T(1024)S(1)} %get-tuple-element.876, f32[2048]{0:T(1024)S(1)} %copy-done.36, f32[2,128]{1,0:T(2,128)S(1)} %pad_maximum_fusion.6), channel_id=4, replica_groups=mesh['seq'=8,'fsdp'=4] {'seq','fsdp'}, use_global_device_ids=true, to_apply=%region_22.23.clone | all-reduce | flops 4352 | bytes 34816
  1438.5 14.6 fusion.37
  1453.2 176.2 %reduce-scatter.4.cloned.1.call-done = f32[64,6144]{1,0:T(8,128)} async-done(((f32[2048,6144]{1,0:T(8,128)}), f32[64,6144]{1,0:T(8,128)}) %reduce-scatter.4.cloned.1.call-update) | async-done | bytes 1572880 | tf_op jit(solution)/shard_map/reduce_scatter | solution.py:330
  1633.6 1266.5 %reduce-scatter.6.cloned.1.call-done = f32[64,18432]{1,0:T(8,128)} async-done(((f32[2048,18432]{1,0:T(8,128)}), f32[64,18432]{1,0:T(8,128)}) %reduce-scatter.6.cloned.1.call-update) | async-done | bytes 4718608 | tf_op jit(solution)/shard_map/reduce_scatter | solution.py:218
  (385 shorter events, 383.3 us)
Async XLA Ops:
  7.2 93.0 %all-gather.11.cloned.1.call-start = ((), (), s32[]{:S(2)}) async-start(), calls=%async_computation.3 | async-start | bytes 4325376 | tf_op jit(solution)/shard_map/all_gather | solution.py:110
  7.9 131.4 %all-gather.9.cloned.1.call-start = ((), (), s32[]{:S(2)}) async-start(), calls=%async_computation.2 | async-start | bytes 4325376 | tf_op jit(solution)/shard_map/all_gather | solution.py:109
  8.7 209.7 %all-gather.13.cloned.1.call-start = ((), (), s32[]{:S(2)}) async-start(), calls=%async_computation.4 | async-start | bytes 8650752 | tf_op jit(solution)/shard_map/all_gather | solution.py:108
  9.4 416.5 %all-gather.15.cloned.1.call-start = ((), (), s32[]{:S(2)}) async-start(), calls=%async_computation.5 | async-start | bytes 8650752 | tf_op jit(solution)/shard_map/all_gather | solution.py:111
  10.0 499.7 %all-gather.19.cloned.1.call-start = ((), (), s32[]{:S(2)}) async-start(), calls=%async_computation.7 | async-start | bytes 25952256 | tf_op jit(solution)/shard_map/all_gather | solution.py:187
  10.6 654.7 %all-gather.17.cloned.1.call-start = ((), (), s32[]{:S(2)}) async-start(), calls=%async_computation.6 | async-start | bytes 25952256 | tf_op jit(solution)/shard_map/all_gather | solution.py:186
  11.1 809.9 %all-gather.21.cloned.1.call-start = ((), (), s32[]{:S(2)}) async-start(), calls=%async_computation.8 | async-start | bytes 25952256 | tf_op jit(solution)/shard_map/all_gather | solution.py:188
  11.9 1617.5 %reduce-scatter.4.cloned.1.call-start = ((), (), s32[]{:S(2)}) async-start(), calls=%async_computation.9 | async-start | bytes 51904512 | tf_op jit(solution)/shard_map/reduce_scatter | solution.py:330
  239.8 23.4 collective-permute-start
  263.9 18.8 collective-permute-start
  283.5 27.6 collective-permute-start
  311.9 13.9 collective-permute-start
  326.6 17.8 collective-permute-start
  345.2 25.6 collective-permute-start
  371.6 26.7 collective-permute-start
  399.1 25.2 collective-permute-start
  884.0 15.0 collective-permute-start.2
  886.3 23.3 collective-permute-start.1
  917.5 17.6 collective-permute-start.2
  922.4 22.2 collective-permute-start.1
  952.6 17.9 collective-permute-start.2
  957.8 21.3 collective-permute-start.1
  983.3 21.6 collective-permute-start.2
  992.2 20.4 collective-permute-start.1
  1016.8 19.1 collective-permute-start.2
  1025.7 15.7 collective-permute-start.1
  1054.6 13.2 collective-permute-start.1
  1071.9 16.5 collective-permute-start.2
  1080.2 13.7 collective-permute-start.1
  1098.1 22.4 collective-permute-start.2
  1108.0 18.1 collective-permute-start.1
  1190.2 1709.8 %reduce-scatter.6.cloned.1.call-start = ((), (), s32[]{:S(2)}) async-start(), calls=%async_computation.10 | async-start | bytes 155713536 | tf_op jit(solution)/shard_map/reduce_scatter | solution.py:218
  (50 other events, 3503.1 us)
Sparse Core Ops, SparseCore 0:
  10.9 64.9 all-gather.10
  78.7 60.5 all-gather.8
  142.2 76.0 all-gather.12
  221.0 93.2 all-gather.14
  317.0 192.5 all-gather.18
  512.4 152.7 all-gather.16
  668.2 152.8 all-gather.20
  1190.4 439.0 reduce-scatter.3
  1635.9 1264.1 reduce-scatter.5
where the time goes:
time: 2920 us; the launch traced here: 2910 us
  waiting for transfers between devices  2190 us (75%)
  matrix products  244 us (8%)
  other arithmetic  176 us (6%)
  blocking collectives  129 us (4%)
  local copies, waits for them, and re-layouts  66 us (2%)
  starting transfers between devices  61.1 us (2%)
    reduce_scatter x1, waiting for transfers between devices, on_device(): lax.psum_scatter(jnp.concatenate([matmul_tn(left_norm, gate_and_up), matm...  1270 us
    ppermute x24, waiting for transfers between devices, from_behind(): return lax.ppermute(block, axis, route)  280 us
    reduce_scatter x1, waiting for transfers between devices, on_device(): lax.psum_scatter(jnp.concatenate([matmul_tn(left_norm, projections), matm...  176 us
    all_gather x1, waiting for transfers between devices, on_device(): lax.all_gather(w_down, ('seq', 'fsdp'), axis=0, tiled=True)  143 us
    all_gather x1, waiting for transfers between devices, on_device(): lax.all_gather(w_gate, ('seq', 'fsdp'), axis=0, tiled=True)  142 us
    dot_general x4, matrix products, matmul_tn(): lax.dot_general(left, right, (((0,), (0,)), ((), ())), preferred_element_...  105 us
    concatenate x1, other arithmetic, on_device(): jnp.concatenate([matmul_tn(left_norm, gate_and_up), matmul_tn(grad_rows,...  101 us
    unnamed x2, blocking collectives  89.4 us
  transfers between devices with their start and end apart: 33, of which 31 were waited for; matrix products, arithmetic and copies ran while one was open for 11% of the time, Pallas kernels for 0%

commit v1 on v0

v1 whole, which is shorter than its diff:
```python
import jax
import jax.numpy as jnp
from jax import lax
from jax.sharding import PartitionSpec as P

QUERY_HEADS = 16
KEY_VALUE_HEADS = 8
HEAD_SIZE = 128
FF = 6144

rope_base = 1000000.0
norm_eps = 1e-06
BOTH = ("seq", "fsdp")
bf16 = jnp.bfloat16
f32 = jnp.float32

PARTS = KEY_VALUE_HEADS // 2
GROUP = QUERY_HEADS // KEY_VALUE_HEADS


def dot(left, right):
    return jnp.dot(left, right, preferred_element_type=f32)


def dot_t(left, right):
    return lax.dot_general(left, right, (((1,), (1,)), ((), ())), preferred_element_type=f32)


def dot_tn(left, right):
    return lax.dot_general(left, right, (((0,), (0,)), ((), ())), preferred_element_type=f32)


def inv_rms(tensor):
    return lax.rsqrt(jnp.mean(tensor * tensor, axis=-1, keepdims=True) + norm_eps)


def norm_back(tensor, root, gain, incoming):
    scaled = gain * incoming
    return root * scaled - tensor * (root * root * root) * jnp.mean(
        scaled * tensor, axis=-1, keepdims=True
    )


def halves(tensor):
    half_width = tensor.shape[-1] // 2
    return tensor[..., :half_width], tensor[..., half_width:]


def rotate(tensor, cosine, sine):
    front, back = halves(tensor)
    return jnp.concatenate([front * cosine - back * sine, back * cosine + front * sine], axis=-1)


def unrotate(tensor, cosine, sine):
    front, back = halves(tensor)
    return jnp.concatenate([front * cosine + back * sine, back * cosine - front * sine], axis=-1)


class Grid:
    def __init__(self):
        self.seq = lax.axis_size("seq")
        self.fsdp = lax.axis_size("fsdp")
        self.A = PARTS
        self.R = self.seq // self.A
        self.Y = self.fsdp // 2
        s, f = lax.axis_index("seq"), lax.axis_index("fsdp")
        self.a, self.b = s // self.R, s % self.R
        self.y, self.c = f // 2, f % 2
        self.places = [
            (a, b, y, c)
            for a in range(self.A)
            for b in range(self.R)
            for y in range(self.Y)
            for c in range(2)
        ]

    def at(self, a, b, y, c):
        return ((a % self.A) * self.R + b % self.R) * self.fsdp + (y % self.Y) * 2 + c % 2

    def move(self, array, a=0, b=0, y=0, c=0):
        route = [
            (self.at(*p), self.at(p[0] + a, p[1] + b, p[2] + y, p[3] + c)) for p in self.places
        ]
        return lax.ppermute(array, BOTH, route)

    def swap(self, array):
        return self.move(array, c=1)

    def exchange_a(self, array):
        groups = [
            [self.at(a, b, y, c) for a in range(self.A)]
            for b in range(self.R)
            for y in range(self.Y)
            for c in range(2)
        ]
        return lax.all_to_all(array, BOTH, 0, 0, axis_index_groups=groups, tiled=True)

    def ring_a(self, array):
        held = [array]
        for _ in range(self.A - 1):
            held.append(self.move(held[-1], a=1))
        return held

    def by_core(self, first, second):
        return (
            jnp.where(self.c == 0, first, second),
            jnp.where(self.c == 0, second, first),
        )

    def spread(self, piece, b_first):
        got = {(0, 0): piece}
        if b_first:
            for i in range(1, self.R):
                got[i, 0] = self.move(piece, b=i)
            for i in range(self.R):
                for j in range(1, self.Y):
                    got[i, j] = self.move(got[i, 0], y=j)
        else:
            for j in range(1, self.Y):
                got[0, j] = self.move(piece, y=j)
            for j in range(self.Y):
                for i in range(1, self.R):
                    got[i, j] = self.move(got[0, j], b=i)
        return [got[i, j] for i in range(self.R) for j in range(self.Y)]

    def collect(self, pieces, b_first, wide=False):
        held = {
            (i, j): pieces[i * self.Y + j] for i in range(self.R) for j in range(self.Y)
        }
        sent = (lambda v: v) if wide else (lambda v: v.astype(bf16))
        if b_first:
            rows = {}
            for j in reversed(range(self.Y)):
                total = held[0, j].astype(f32)
                for i in range(1, self.R):
                    total = total + self.move(sent(held[i, j]), b=-i).astype(f32)
                rows[j] = total
            total = rows[0]
            for j in range(1, self.Y):
                total = total + self.move(sent(rows[j]), y=-j).astype(f32)
            return total
        columns = {}
        for i in reversed(range(self.R)):
            total = held[i, 0].astype(f32)
            for j in range(1, self.Y):
                total = total + self.move(sent(held[i, j]), y=-j).astype(f32)
            columns[i] = total
        total = columns[0]
        for i in range(1, self.R):
            total = total + self.move(sent(columns[i]), b=-i).astype(f32)
        return total

    def sum_over_a(self, partial, rows):
        total = partial[:rows].astype(f32)
        for d in range(1, self.A):
            block = partial[d * rows : (d + 1) * rows].astype(bf16)
            total = total + self.move(block, a=-d).astype(f32)
        return total


def on_device(
    tokens,
    block_pos,
    w_query,
    key_weight,
    value_weight,
    w_out,
    w_gate,
    w_up,
    w_down,
    attn_gain,
    mlp_gain,
    qk_gain,
    grad_out,
):
    g = Grid()
    A, R, Y = g.A, g.R, g.Y
    a, b, y, c = g.a, g.b, g.y, g.c
    pieces = R * Y
    rows_own = w_query.shape[0]
    width = tokens.shape[2]
    piece_width = width // pieces
    token_rows = tokens.shape[1]
    group_rows = A * token_rows
    score_scale = HEAD_SIZE ** (-0.5)
    q_cols = GROUP * HEAD_SIZE
    ff_cols = FF // (2 * A)

    def permuted(rows):
        split = rows.reshape(rows.shape[0], A, R, Y, 2 * rows_own)
        split = jnp.transpose(split, (2, 3, 0, 1, 4)).reshape(R, Y, rows.shape[0], piece_width)
        split = jnp.stack([split[(b - i) % R] for i in range(R)])
        split = jnp.stack([split[:, (y - j) % Y] for j in range(Y)], axis=1)
        return jnp.concatenate([split[i, j] for i in range(R) for j in range(Y)], axis=1)

    def restored(rows):
        split = rows.reshape(rows.shape[0], R, Y, piece_width)
        split = jnp.transpose(split, (1, 2, 0, 3))
        split = jnp.stack([split[(b - i) % R] for i in range(R)])
        split = jnp.stack([split[:, (y - j) % Y] for j in range(Y)], axis=1)
        split = split.reshape(R, Y, rows.shape[0], A, 2 * rows_own)
        return jnp.transpose(split, (2, 3, 0, 1, 4)).reshape(rows.shape[0], width)

    def cut(array, i):
        return array[:, i * piece_width : (i + 1) * piece_width]

    def own_and_other(local):
        turned = jnp.transpose(local, (2, 1, 0, 3))
        keep = lax.dynamic_index_in_dim(turned, c, 0, keepdims=False)
        send = lax.dynamic_index_in_dim(turned, 1 - c, 0, keepdims=False)
        low, high = g.by_core(keep, g.swap(send))
        return jnp.concatenate([low, high], axis=1)

    def columns_to_parts(local):
        mine = own_and_other(local)
        return g.exchange_a(mine).reshape(A * 2 * rows_own, mine.shape[-1])

    qkv_local = jnp.concatenate(
        [
            w_query.reshape(rows_own, A, 2, q_cols),
            key_weight.reshape(rows_own, A, 2, HEAD_SIZE),
            value_weight.reshape(rows_own, A, 2, HEAD_SIZE),
        ],
        axis=-1,
    )
    x_own = permuted(tokens[0])
    x_parts = g.ring_a(x_own)
    qkv_own = g.spread(columns_to_parts(qkv_local), True)
    qkv_other = [g.swap(piece) for piece in qkv_own]

    packed = jnp.concatenate([attn_gain, mlp_gain, qk_gain.reshape(-1)])
    low, high = g.by_core(packed, g.swap(packed))
    packed = jnp.stack([low, high])
    packed = jnp.stack(g.spread(packed, True))
    packed = g.exchange_a(jnp.broadcast_to(packed[None], (A,) + packed.shape))
    packed = jnp.transpose(packed, (1, 0, 2, 3)).astype(f32)
    first_gain = packed[..., :rows_own].reshape(width)
    second_gain = packed[..., rows_own : 2 * rows_own].reshape(width)
    small = packed[..., 2 * rows_own :].reshape(R, Y, A, 2, 2, -1)
    small = jnp.stack([small[(b - i) % R] for i in range(R)])
    small = jnp.stack([small[:, (y - j) % Y] for j in range(Y)], axis=1)
    small = jnp.transpose(small, (4, 2, 0, 1, 3, 5)).reshape(2, HEAD_SIZE)
    query_gain, key_gain = small[0], small[1]

    out_local = own_and_other(w_out.reshape(rows_own, A, 2, q_cols))
    out_local = jnp.transpose(out_local, (1, 0, 2)).reshape(2 * rows_own, A * q_cols)
    out_all = g.exchange_a(jnp.broadcast_to(out_local[None], (A,) + out_local.shape))
    out_own = g.spread(out_all.reshape(A * 2 * rows_own, A * q_cols), False)
    out_other = [g.swap(piece) for piece in out_own]
    gu_local = jnp.concatenate(
        [w_gate.reshape(rows_own, A, 2, ff_cols), w_up.reshape(rows_own, A, 2, ff_cols)], axis=-1
    )
    gu_own = g.spread(columns_to_parts(gu_local), True)
    gu_other = [g.swap(piece) for piece in gu_own]
    down_own = g.spread(columns_to_parts(w_down.reshape(rows_own, A, 2, ff_cols)), False)
    down_other = [g.swap(piece) for piece in down_own]

    order = block_pos[0]
    row_offsets = jnp.arange(token_rows, dtype=jnp.int32)

    def positions(shift):
        blocks = [order[((a - d) % A) * R + (b - shift) % R] for d in range(A)]
        return jnp.concatenate([block * token_rows + row_offsets for block in blocks])

    local_pos = positions(0)
    key_pos = jnp.concatenate([positions(i) for i in range(R)])
    exponent = jnp.arange(HEAD_SIZE // 2, dtype=f32) * (-2.0 / HEAD_SIZE)
    angles = local_pos.astype(f32)[:, None] * (rope_base**exponent)[None, :]
    cosine, sine = jnp.cos(angles), jnp.sin(angles)
    cosine3, sine3 = cosine[:, None, :], sine[:, None, :]

    x_group = jnp.concatenate(x_parts, axis=0)
    inputs = x_group.astype(f32)
    x_root = inv_rms(inputs)
    normed = (inputs * x_root * first_gain).astype(bf16)

    def project(left, weights):
        total = dot(cut(left, 0), weights[0])
        for i in range(1, pieces):
            total = total + dot(cut(left, i), weights[i])
        return total

    def heads_of(weights):
        made = project(normed, weights)
        q_pre = made[:, :q_cols].reshape(group_rows, GROUP, HEAD_SIZE)
        k_pre = made[:, q_cols : q_cols + HEAD_SIZE]
        value = made[:, q_cols + HEAD_SIZE :].astype(bf16)
        q_root, k_root = inv_rms(q_pre), inv_rms(k_pre)
        query = rotate(q_pre * q_root * query_gain, cosine3, sine3).astype(bf16)
        key = rotate(k_pre * k_root * key_gain, cosine, sine).astype(bf16)
        return q_pre, q_root, query, k_pre, k_root, key, value

    made = [heads_of(qkv_own), heads_of(qkv_other)]
    key_values = jnp.concatenate([made[0][5], made[0][6], made[1][5], made[1][6]], axis=1)
    key_values = jnp.concatenate(
        [key_values] + [g.move(key_values, b=i) for i in range(1, R)], axis=0
    )

    visible = local_pos[:, None] >= key_pos[None, :]

    def attend(h):
        query = made[h][2]
        key = key_values[:, 2 * h * HEAD_SIZE : (2 * h + 1) * HEAD_SIZE]
        value = key_values[:, (2 * h + 1) * HEAD_SIZE : (2 * h + 2) * HEAD_SIZE]
        scores = jnp.einsum("qgd,td->gqt", query, key, preferred_element_type=f32) * score_scale
        scores = jnp.where(visible, scores, -1e30)
        top = jnp.max(scores, axis=-1, keepdims=True)
        weights = jnp.exp(scores - top)
        totals = jnp.sum(weights, axis=-1, keepdims=True)
        log_total = top + jnp.log(totals)
        mixed = jnp.einsum("gqt,td->gqd", weights.astype(bf16), value, preferred_element_type=f32)
        return mixed / totals, log_total

    mixed = [attend(0), attend(1)]
    attended = jnp.concatenate(
        [jnp.transpose(m[0], (1, 0, 2)).reshape(group_rows, q_cols) for m in mixed], axis=1
    ).astype(bf16)
    attended = jnp.stack(
        [jnp.roll(got, d * token_rows, axis=0) for d, got in enumerate(g.ring_a(attended))]
    )
    attended = jnp.stack([attended[(a - part) % A] for part in range(A)])
    att_own = jnp.concatenate([attended[part, :, :q_cols] for part in range(A)], axis=1)
    att_other = jnp.concatenate([attended[part, :, q_cols:] for part in range(A)], axis=1)

    branch = jnp.concatenate(
        [dot_t(att_own, out_own[i]) + dot_t(att_other, out_other[i]) for i in range(pieces)], axis=1
    )
    middle = inputs + branch
    root2 = inv_rms(middle)
    normed2 = (middle * root2 * second_gain).astype(bf16)
    dout_own = permuted(grad_out[0])
    dout = jnp.concatenate(g.ring_a(dout_own), axis=0)

    def feed(weights):
        both = project(normed2, weights)
        return both[:, :ff_cols], both[:, ff_cols:]

    gates = [feed(gu_own), feed(gu_other)]
    inner = [(jax.nn.silu(gate) * up).astype(bf16) for gate, up in gates]
    d_inner = [project(dout, down_own), project(dout, down_other)]

    def gate_back(gate, up, d_in):
        s = jax.nn.sigmoid(gate)
        d_gate = d_in * up * s * (1.0 + gate * (1.0 - s))
        return jnp.concatenate([d_gate, d_in * gate * s], axis=1).astype(bf16)

    d_gu = [gate_back(*gates[h], d_inner[h]) for h in range(2)]
    d_normed2 = jnp.concatenate(
        [dot_t(d_gu[0], gu_own[i]) + dot_t(d_gu[1], gu_other[i]) for i in range(pieces)], axis=1
    )
    mlp_gain_grad = jnp.sum(d_normed2 * middle * root2, axis=0)
    e2 = g.sum_over_a(d_normed2, token_rows)
    grad_middle = dout_own.astype(f32) + norm_back(
        middle[:token_rows], root2[:token_rows], second_gain, e2
    )
    out_part = jnp.concatenate(
        [dot_t(inner[0], down_own[i]) + dot_t(inner[1], down_other[i]) for i in range(pieces)],
        axis=1,
    )
    result = restored((middle[:token_rows] + g.sum_over_a(out_part, token_rows)).astype(bf16))

    def weight_gradient(left, own, other, b_first):
        lefts = [cut(left, i) for i in range(pieces)]
        sent = [g.swap(dot_tn(part, other).astype(bf16)) for part in lefts]
        kept = [
            (dot_tn(part, own) + got.astype(f32)).astype(bf16) for part, got in zip(lefts, sent)
        ]
        total = g.collect(kept, b_first).astype(bf16)
        total = g.exchange_a(total.reshape(A, 2 * rows_own, -1)).reshape(A, 2, rows_own, -1)
        keep = lax.dynamic_index_in_dim(total, c, 1, keepdims=False)
        send = lax.dynamic_index_in_dim(total, 1 - c, 1, keepdims=False)
        low, high = g.by_core(keep, g.swap(send))
        whole = jnp.stack([low, high], axis=1)
        return jnp.transpose(whole, (2, 0, 1, 3)).astype(f32)

    gu_grad = weight_gradient(normed2, d_gu[0], d_gu[1], True)
    down_grad = weight_gradient(dout, inner[0], inner[1], False)

    d_branch = grad_middle.astype(bf16)

    def to_parts(array, cols):
        send = [
            lax.dynamic_slice_in_dim(array, ((a + d) % A) * cols, cols, axis=1) for d in range(A)
        ]
        return [send[0]] + [g.move(send[d], a=d) for d in range(1, A)]

    def out_back(i):
        return dot(cut(d_branch, i), out_own[i]), dot(cut(d_branch, i), out_other[i])

    d_att_own, d_att_other = out_back(0)
    for i in range(1, pieces):
        more_own, more_other = out_back(i)
        d_att_own, d_att_other = d_att_own + more_own, d_att_other + more_other
    d_att = jnp.concatenate(
        [
            d_att_own.reshape(token_rows, A, q_cols),
            d_att_other.reshape(token_rows, A, q_cols),
        ],
        axis=-1,
    ).astype(bf16)
    d_att = jnp.concatenate(to_parts(d_att.reshape(token_rows, A * 2 * q_cols), 2 * q_cols), axis=0)

    def attend_back(h):
        query = made[h][2]
        key = key_values[:, 2 * h * HEAD_SIZE : (2 * h + 1) * HEAD_SIZE]
        value = key_values[:, (2 * h + 1) * HEAD_SIZE : (2 * h + 2) * HEAD_SIZE]
        d_mixed = d_att[:, h * q_cols : (h + 1) * q_cols].reshape(group_rows, GROUP, HEAD_SIZE)
        o, log_total = mixed[h]
        delta = jnp.sum(jnp.transpose(d_mixed, (1, 0, 2)).astype(f32) * o, axis=-1, keepdims=True)
        scores = jnp.einsum("qgd,td->gqt", query, key, preferred_element_type=f32) * score_scale
        scores = jnp.where(visible, scores, -1e30)
        weights = jnp.exp(scores - log_total)
        d_weights = jnp.einsum("qgd,td->gqt", d_mixed, value, preferred_element_type=f32)
        d_scores = (weights * (d_weights - delta)).astype(bf16)
        d_query = jnp.einsum("gqt,td->qgd", d_scores, key, preferred_element_type=f32)
        d_key = jnp.einsum("gqt,qgd->td", d_scores, query, preferred_element_type=f32)
        d_value = jnp.einsum(
            "gqt,qgd->td", weights.astype(bf16), d_mixed, preferred_element_type=f32
        )
        return d_query * score_scale, d_key, d_value

    backs = [attend_back(0), attend_back(1)]
    d_kv = jnp.concatenate([backs[0][1], backs[0][2], backs[1][1], backs[1][2]], axis=1)
    d_kv_total = d_kv[:group_rows]
    for i in range(1, R):
        block = d_kv[i * group_rows : (i + 1) * group_rows].astype(bf16)
        d_kv_total = d_kv_total + g.move(block, b=-i).astype(f32)

    def projections_back(h):
        q_pre, q_root, _, k_pre, k_root, _, _ = made[h]
        e_q = unrotate(backs[h][0], cosine3, sine3)
        d_key = d_kv_total[:, 2 * h * HEAD_SIZE : (2 * h + 1) * HEAD_SIZE] * score_scale
        d_value = d_kv_total[:, (2 * h + 1) * HEAD_SIZE : (2 * h + 2) * HEAD_SIZE]
        e_k = unrotate(d_key, cosine, sine)
        d_q_pre = norm_back(q_pre, q_root, query_gain, e_q).reshape(group_rows, q_cols)
        d_k_pre = norm_back(k_pre, k_root, key_gain, e_k)
        gains = jnp.stack(
            [jnp.sum(e_q * q_pre * q_root, axis=(0, 1)), jnp.sum(e_k * k_pre * k_root, axis=0)]
        )
        return jnp.concatenate([d_q_pre, d_k_pre, d_value], axis=1).astype(bf16), gains

    d_qkv_own, gains_own = projections_back(0)
    d_qkv_other, gains_other = projections_back(1)
    d_normed = jnp.concatenate(
        [
            dot_t(d_qkv_own, qkv_own[i]) + dot_t(d_qkv_other, qkv_other[i])
            for i in range(pieces)
        ],
        axis=1,
    )
    attn_gain_grad = jnp.sum(d_normed * inputs * x_root, axis=0)
    e1 = g.sum_over_a(d_normed, token_rows)
    grad_input = grad_middle + norm_back(
        inputs[:token_rows], x_root[:token_rows], first_gain, e1
    )
    qkv_grad = weight_gradient(normed, d_qkv_own, d_qkv_other, True)

    att_low, att_high = g.by_core(att_own, att_other)
    att_heads = jnp.stack(
        [att_low.reshape(group_rows, A, q_cols), att_high.reshape(group_rows, A, q_cols)], axis=2
    ).reshape(group_rows, A * 2 * q_cols)
    by_part = jnp.transpose(
        d_branch.reshape(token_rows, pieces, A, 2 * rows_own), (0, 2, 1, 3)
    ).reshape(token_rows, width)
    rows_of_part = jnp.concatenate(to_parts(by_part, pieces * 2 * rows_own), axis=0)
    out_grad = dot_tn(rows_of_part, att_heads).reshape(pieces, 2, rows_own, -1)
    keep = lax.dynamic_index_in_dim(out_grad, c, 1, keepdims=False)
    send = lax.dynamic_index_in_dim(out_grad, 1 - c, 1, keepdims=False).astype(bf16)
    out_grad = keep + g.swap(send).astype(f32)
    grad_wo = g.collect([out_grad[i] for i in range(pieces)], False)

    small = (gains_own + gains_other).reshape(2, A, R, Y, 2, -1)
    small = jnp.transpose(small, (2, 3, 1, 4, 0, 5))
    small = jnp.stack([small[(b - i) % R] for i in range(R)])
    small = jnp.stack([small[:, (y - j) % Y] for j in range(Y)], axis=1)
    small = small.reshape(pieces, A, 2, -1)
    sums = jnp.concatenate(
        [
            attn_gain_grad.reshape(pieces, A, 2, rows_own),
            mlp_gain_grad.reshape(pieces, A, 2, rows_own),
            small,
        ],
        axis=-1,
    )
    keep = lax.dynamic_index_in_dim(sums, c, 2, keepdims=False)
    send = lax.dynamic_index_in_dim(sums, 1 - c, 2, keepdims=False)
    sums = keep + g.swap(send)
    sums = g.collect([sums[i] for i in range(pieces)], True, wide=True)
    sums = jnp.sum(g.exchange_a(sums), axis=0)

    gate_up = gu_grad.reshape(rows_own, 2 * A, 2, ff_cols)
    return (
        result[None],
        restored(grad_input)[None],
        qkv_grad[..., :q_cols].reshape(rows_own, -1),
        qkv_grad[..., q_cols : q_cols + HEAD_SIZE].reshape(rows_own, -1),
        qkv_grad[..., q_cols + HEAD_SIZE :].reshape(rows_own, -1),
        grad_wo,
        gate_up[:, :, 0].reshape(rows_own, -1),
        gate_up[:, :, 1].reshape(rows_own, -1),
        down_grad.reshape(rows_own, -1),
        sums[:rows_own],
        sums[rows_own : 2 * rows_own],
        sums[2 * rows_own :].reshape(2, -1),
    )


def solution(mesh):
    placed = (
        P("fsdp", "seq", None),
        P("fsdp", None),
        P(("seq", "fsdp"), None),
        P(("seq", "fsdp"), None),
        P(("seq", "fsdp"), None),
        P(("seq", "fsdp"), None),
        P(("seq", "fsdp"), None),
        P(("seq", "fsdp"), None),
        P(("seq", "fsdp"), None),
        P(("seq", "fsdp")),
        P(("seq", "fsdp")),
        P(None, ("seq", "fsdp")),
        P("fsdp", "seq", None),
    )
    return jax.shard_map(
        on_device,
        mesh=mesh,
        in_specs=placed,
        out_specs=(
            P("fsdp", "seq", None),
            P("fsdp", "seq", None),
            P(("seq", "fsdp"), None),
            P(("seq", "fsdp"), None),
            P(("seq", "fsdp"), None),
            P(("seq", "fsdp"), None),
            P(("seq", "fsdp"), None),
            P(("seq", "fsdp"), None),
            P(("seq", "fsdp"), None),
            P(("seq", "fsdp")),
            P(("seq", "fsdp")),
            P(None, ("seq", "fsdp")),
        ),
        check_vma=False,
    )
```

time: 2920 us -> 933 us (0.32)
  waiting for transfers between devices: 2190 us -> 388 us
  blocking collectives: 129 us -> 0 us
  other arithmetic: 176 us -> 95.3 us
  starting transfers between devices: 61.1 us -> 127 us
  matrix products: 244 us -> 184 us
  local copies, waits for them, and re-layouts: 66 us -> 120 us
    reduce_scatter x2 -> x0, waiting for transfers between devices: 1440 us -> none  [the longest x1 1270 us: on_device(): lax.psum_scatter(jnp.concatenate([matmul_tn(left_norm, gate_and_up), matm...]
    all_gather x7 -> x0, waiting for transfers between devices: 466 us -> none  [the longest x1 143 us: on_device(): lax.all_gather(w_down, ('seq', 'fsdp'), axis=0, tiled=True)]
    concatenate x4 -> x16, other arithmetic: 135 us -> 21.3 us  [the longest x1 6.14 us: on_device(): dout = jnp.concatenate(g.ring_a(dout_own), axis=0)]
    unnamed x2 -> x0, blocking collectives: 89.4 us -> none
    all_to_all x0 -> x9, waiting for transfers between devices: none -> 82.9 us  [exchange_a(): lax.all_to_all(array, BOTH, 0, 0, axis_index_groups=groups, tiled=True)]
    dot_general x46 -> x101, matrix products: 244 us -> 184 us  [the longest x32 59.8 us: dot(): return jnp.dot(left, right, preferred_element_type=f32)]
    all_to_all x0 -> x9, starting transfers between devices: none -> 49 us  [exchange_a(): lax.all_to_all(array, BOTH, 0, 0, axis_index_groups=groups, tiled=True)]
    all_gather x1 -> x0, blocking collectives: 40.1 us -> none  [on_device(): lax.all_gather(qk_gain, ('seq', 'fsdp'), axis=1, tiled=True)]
  transfers between devices with their start and end apart: 33 -> 103, of which waited for: 31 -> 30; matrix products, arithmetic and copies ran while one was open for 11% -> 37% of each run, Pallas kernels for 0% -> 0%
where the time goes in v1:
time: 933 us; the launch traced here: 923 us
  waiting for transfers between devices  388 us (42%)
  matrix products  184 us (20%)
  starting transfers between devices  127 us (14%)
  local copies, waits for them, and re-layouts  120 us (13%)
  other arithmetic  95.3 us (10%)
  between operations  9.92 us (1%)
    ppermute x94, waiting for transfers between devices, move(): return lax.ppermute(array, BOTH, route)  305 us
    all_to_all x9, waiting for transfers between devices, exchange_a(): lax.all_to_all(array, BOTH, 0, 0, axis_index_groups=groups, tiled=True)  82.9 us
    ppermute x94, starting transfers between devices, move(): return lax.ppermute(array, BOTH, route)  77.8 us
    dot_general x32, matrix products, dot(): return jnp.dot(left, right, preferred_element_type=f32)  59.8 us
    dot_general x25, matrix products, dot_tn(): lax.dot_general(left, right, (((0,), (0,)), ((), ())), preferred_element_...  56.7 us
    all_to_all x9, starting transfers between devices, exchange_a(): lax.all_to_all(array, BOTH, 0, 0, axis_index_groups=groups, tiled=True)  49 us
    dot_general x32, matrix products, dot_t(): lax.dot_general(left, right, (((1,), (1,)), ((), ())), preferred_element_...  47.1 us
  transfers between devices with their start and end apart: 103, of which 30 were waited for; matrix products, arithmetic and copies ran while one was open for 37% of the time, Pallas kernels for 0%

profile of v1, /device:TPU:0, one launch (start us, length us, event | category | flops | bytes accessed | tf_op | source)
XLA Modules:
  0.0 923.1 jit_solution(108992364706004004)
XLA Ops:
  69.5 4.7 all-to-all-start.1
  76.3 5.2 collective-permute-done.46
  81.4 11.1 %collective-permute-done.1 = bf16[128,2048]{0,1:T(8,128)(2,1)} collective-permute-done((bf16[128,2048]{0,1:T(8,128)(2,1)}, bf16[128,2048]{0,1:T(8,128)(2,1)}, u32[]{:S(2)}, u32[]{:S(2)}) %collective-permute-start.1) | collective-permute-done | bytes 524320 | tf_op jit(solution)/shard_map/ppermute | solution.py:84
  95.4 28.8 %all-to-all-done.1 = bf16[4,128,512]{2,1,0:T(8,128)(2,1)} async-done(((bf16[4,128,512]{2,1,0:T(8,128)(2,1)}), bf16[4,128,512]{2,1,0:T(8,128)(2,1)}, u32[]{:S(2)}, u32[]{:S(2)}) %all-to-all-start.1) | async-done | bytes 524320 | tf_op jit(solution)/shard_map/all_to_all | solution.py:96
  135.8 6.9 collective-permute-done.9
  149.7 10.6 %all-to-all-done.4 = bf16[4,128,768]{2,1,0:T(8,128)(2,1)} async-done(((bf16[4,128,768]{2,1,0:T(8,128)(2,1)}), bf16[4,128,768]{2,1,0:T(8,128)(2,1)}, u32[]{:S(2)}, u32[]{:S(2)}) %all-to-all-start.4) | async-done | bytes 786464 | tf_op jit(solution)/shard_map/all_to_all | solution.py:96
  165.8 6.1 pad_maximum_fusion.5
  178.7 12.5 %all-to-all-done.2 = bf16[4,128,1024]{2,1,0:T(8,128)(2,1)} async-done(((bf16[4,128,1024]{2,1,0:T(8,128)(2,1)}), bf16[4,128,1024]{2,1,0:T(8,128)(2,1)}, u32[]{:S(2)}, u32[]{:S(2)}) %all-to-all-start.2) | async-done | bytes 1048608 | tf_op jit(solution)/shard_map/all_to_all | solution.py:96
  191.1 4.5 all-to-all-start.3
  228.7 26.8 %collective-permute-done.15 = bf16[512,512]{0,1:T(8,128)(2,1)S(1)} collective-permute-done((bf16[512,512]{0,1:T(8,128)(2,1)S(1)}, bf16[512,512]{0,1:T(8,128)(2,1)S(1)}, u32[]{:S(2)}, u32[]{:S(2)}) %collective-permute-start.15) | collective-permute-done | bytes 524320 | tf_op jit(solution)/shard_map/ppermute | solution.py:84
  274.4 7.3 collective-permute-done.16
  286.4 10.8 %collective-permute-done.17 = bf16[512,512]{0,1:T(8,128)(2,1)} collective-permute-done((bf16[512,512]{0,1:T(8,128)(2,1)S(1)}, bf16[512,512]{0,1:T(8,128)(2,1)}, u32[]{:S(2)}, u32[]{:S(2)}) %collective-permute-start.17) | collective-permute-done | bytes 524320 | tf_op jit(solution)/shard_map/ppermute | solution.py:84
  300.7 11.3 %collective-permute-done.18 = bf16[512,512]{0,1:T(8,128)(2,1)} collective-permute-done((bf16[512,512]{0,1:T(8,128)(2,1)}, bf16[512,512]{0,1:T(8,128)(2,1)}, u32[]{:S(2)}, u32[]{:S(2)}) %collective-permute-start.18) | collective-permute-done | bytes 524320 | tf_op jit(solution)/shard_map/ppermute | solution.py:84
  332.8 13.6 %collective-permute-done.29 = bf16[512,1536]{1,0:T(8,128)(2,1)S(1)} collective-permute-done((bf16[512,1536]{1,0:T(8,128)(2,1)}, bf16[512,1536]{1,0:T(8,128)(2,1)S(1)}, u32[]{:S(2)}, u32[]{:S(2)}) %collective-permute-start.29) | collective-permute-done | bytes 1572896 | tf_op jit(solution)/shard_map/ppermute | solution.py:84
  347.9 11.0 %collective-permute-done.28 = bf16[512,1536]{1,0:T(8,128)(2,1)S(1)} collective-permute-done((bf16[512,1536]{1,0:T(8,128)(2,1)}, bf16[512,1536]{1,0:T(8,128)(2,1)S(1)}, u32[]{:S(2)}, u32[]{:S(2)}) %collective-permute-start.28) | collective-permute-done | bytes 1572896 | tf_op jit(solution)/shard_map/ppermute | solution.py:84
  369.8 19.4 %collective-permute-done.30 = bf16[512,1536]{1,0:T(8,128)(2,1)S(1)} collective-permute-done((bf16[512,1536]{1,0:T(8,128)(2,1)S(1)}, bf16[512,1536]{1,0:T(8,128)(2,1)S(1)}, u32[]{:S(2)}, u32[]{:S(2)}) %collective-permute-start.30) | collective-permute-done | bytes 1572896 | tf_op jit(solution)/shard_map/ppermute | solution.py:84
  457.7 17.3 %collective-permute-done.50 = bf16[128,2048]{0,1:T(8,128)(2,1)} collective-permute-done((bf16[128,2048]{0,1:T(8,128)(2,1)}, bf16[128,2048]{0,1:T(8,128)(2,1)}, u32[]{:S(2)}, u32[]{:S(2)}) %collective-permute-start.50) | collective-permute-done | bytes 524320 | tf_op jit(solution)/shard_map/ppermute | solution.py:84
  477.7 8.5 collective-permute-done.45
  486.3 32.7 %collective-permute-done.44 = bf16[128,2048]{0,1:T(8,128)(2,1)} collective-permute-done((bf16[128,2048]{0,1:T(8,128)(2,1)}, bf16[128,2048]{0,1:T(8,128)(2,1)}, u32[]{:S(2)}, u32[]{:S(2)}) %collective-permute-start.44) | collective-permute-done | bytes 524320 | tf_op jit(solution)/shard_map/ppermute | solution.py:84
  545.1 8.7 collective-permute-start.54
  619.6 9.8 %collective-permute-done.55 = bf16[512,512]{0,1:T(8,128)(2,1)S(1)} collective-permute-done((bf16[512,512]{0,1:T(8,128)(2,1)S(1)}, bf16[512,512]{0,1:T(8,128)(2,1)S(1)}, u32[]{:S(2)}, u32[]{:S(2)}) %collective-permute-start.55) | collective-permute-done | bytes 524320 | tf_op jit(solution)/shard_map/ppermute | solution.py:84
  657.0 5.3 all-to-all-start.8
  685.1 37.4 %collective-permute-done.64 = bf16[512,512]{1,0:T(8,128)(2,1)S(1)} collective-permute-done((bf16[512,512]{1,0:T(8,128)(2,1)S(1)}, bf16[512,512]{1,0:T(8,128)(2,1)S(1)}, u32[]{:S(2)}, u32[]{:S(2)}) %collective-permute-start.64) | collective-permute-done | bytes 524320 | tf_op jit(solution)/shard_map/ppermute | solution.py:84
  725.7 12.9 %collective-permute-done.88 = bf16[512,768]{1,0:T(8,128)(2,1)S(1)} collective-permute-done((bf16[512,768]{1,0:T(8,128)(2,1)S(1)}, bf16[512,768]{1,0:T(8,128)(2,1)S(1)}, u32[]{:S(2)}, u32[]{:S(2)}) %collective-permute-start.88) | collective-permute-done | bytes 786464 | tf_op jit(solution)/shard_map/ppermute | solution.py:84
  745.2 4.6 add_convert_fusion.1
  755.8 35.9 %collective-permute-done.61 = bf16[512,512]{1,0:T(8,128)(2,1)S(1)} collective-permute-done((bf16[512,512]{1,0:T(8,128)(2,1)S(1)}, bf16[512,512]{1,0:T(8,128)(2,1)S(1)}, u32[]{:S(2)}, u32[]{:S(2)}) %collective-permute-start.61) | collective-permute-done | bytes 524320 | tf_op jit(solution)/shard_map/ppermute | solution.py:84
  799.4 19.3 %collective-permute-done.57 = bf16[128,2048]{0,1:T(8,128)(2,1)S(1)} collective-permute-done((bf16[128,2048]{0,1:T(8,128)(2,1)S(1)}, bf16[128,2048]{0,1:T(8,128)(2,1)S(1)}, u32[]{:S(2)}, u32[]{:S(2)}) %collective-permute-start.57) | collective-permute-done | bytes 524320 | tf_op jit(solution)/shard_map/ppermute | solution.py:84
  821.6 14.7 %all-to-all-start.5 = ((bf16[4,128,512]{2,1,0:T(8,128)(2,1)}), bf16[4,128,512]{2,1,0:T(8,128)(2,1)}, u32[]{:S(2)}, u32[]{:S(2)}) async-start(bf16[4,128,512]{2,1,0:T(8,128)(2,1)} %bitcast.570), calls=%async_computation.5 | async-start | bytes 1048576 | tf_op jit(solution)/shard_map/all_to_all | solution.py:96
  838.7 4.7 add_convert_fusion
  843.5 7.0 all-to-all-done.5
  854.4 4.7 subtract_add_fusion
  873.3 17.4 %all-to-all-done.6 = bf16[4,128,1536]{2,1,0:T(8,128)(2,1)S(1)} async-done(((bf16[4,128,1536]{2,1,0:T(8,128)(2,1)}), bf16[4,128,1536]{2,1,0:T(8,128)(2,1)S(1)}, u32[]{:S(2)}, u32[]{:S(2)}) %all-to-all-start.6) | async-done | bytes 1572896 | tf_op jit(solution)/shard_map/all_to_all | solution.py:96
  (933 shorter events, 481.7 us)
Async XLA Ops:
  3.8 60.1 %collective-permute-start.19 = (bf16[4,64,256]{2,1,0:T(8,128)(2,1)}, bf16[4,64,256]{2,1,0:T(8,128)(2,1)}, u32[]{:S(2)}, u32[]{:S(2)}) collective-permute-start(bf16[4,64,256]{2,1,0:T(8,128)(2,1)} %bitcast.532), channel_id=1, source_target_pairs={{0,1},{1,0},{2,3},{3,2},{4,5},{5,4},{6,7},{7,6},{8,9},{9,8},{10,11... | collective-permute-start | bytes 393224 | tf_op jit(solution)/shard_map/ppermute | solution.py:84
  8.0 59.5 %collective-permute-start.7 = (bf16[4,64,512]{2,1,0:T(8,128)(2,1)}, bf16[4,64,512]{2,1,0:T(8,128)(2,1)}, u32[]{:S(2)}, u32[]{:S(2)}) collective-permute-start(bf16[4,64,512]{2,1,0:T(8,128)(2,1)} %bitcast.531), channel_id=1, source_target_pairs={{0,1},{1,0},{2,3},{3,2},{4,5},{5,4},{6,7},{7,6},{8,9},{9,8},{10,11... | collective-permute-start | bytes 786440 | tf_op jit(solution)/shard_map/ppermute | solution.py:84
  13.0 54.0 %collective-permute-start = (bf16[128,2048]{0,1:T(8,128)(2,1)}, bf16[128,2048]{0,1:T(8,128)(2,1)}, u32[]{:S(2)}, u32[]{:S(2)}) collective-permute-start(bf16[128,2048]{0,1:T(8,128)(2,1)} %pad_maximum_fusion.17), channel_id=1, source_target_pairs={{0,8},{1,9},{2,10},{3,11},{4,12},{5,13},{6,14},{7,15},{8,16},{9,17... | collective-permute-start | bytes 1572872 | tf_op jit(solution)/shard_map/ppermute | solution.py:84
  69.5 54.8 %all-to-all-start.1 = ((bf16[4,128,512]{2,1,0:T(8,128)(2,1)}), bf16[4,128,512]{2,1,0:T(8,128)(2,1)}, u32[]{:S(2)}, u32[]{:S(2)}) async-start(bf16[4,128,512]{2,1,0:T(8,128)(2,1)} %pad_maximum_fusion.18), calls=%async_computation.1 | async-start | bytes 1048576 | tf_op jit(solution)/shard_map/all_to_all | solution.py:96
  81.4 48.5 %collective-permute-start.47 = (bf16[128,2048]{0,1:T(8,128)(2,1)}, bf16[128,2048]{0,1:T(8,128)(2,1)}, u32[]{:S(2)}, u32[]{:S(2)}) collective-permute-start(bf16[128,2048]{0,1:T(8,128)(2,1)} %collective-permute-done.46), channel_id=1, source_target_pairs={{0,8},{1,9},{2,10},{3,11},{4,12},{5,13},{6,14},{7,15},{8,16},{9,17... | collective-permute-start | bytes 1572872 | tf_op jit(solution)/shard_map/ppermute | solution.py:84
  129.9 44.3 %collective-permute-start.11 = (bf16[512,512]{1,0:T(8,128)(2,1)}, bf16[512,512]{1,0:T(8,128)(2,1)S(1)}, u32[]{:S(2)}, u32[]{:S(2)}) collective-permute-start(bf16[512,512]{1,0:T(8,128)(2,1)} %bitcast.24), channel_id=1, source_target_pairs={{0,1},{1,0},{2,3},{3,2},{4,5},{5,4},{6,7},{7,6},{8,9},{9,8},{10,11... | collective-permute-start | bytes 1572872 | tf_op jit(solution)/shard_map/ppermute | solution.py:84
  143.2 60.2 %collective-permute-start.13 = (bf16[512,512]{1,0:T(8,128)(2,1)}, bf16[512,512]{1,0:T(8,128)(2,1)}, u32[]{:S(2)}, u32[]{:S(2)}) collective-permute-start(bf16[512,512]{1,0:T(8,128)(2,1)} %collective-permute-done.9), channel_id=1, source_target_pairs={{0,1},{1,0},{2,3},{3,2},{4,5},{5,4},{6,7},{7,6},{8,9},{9,8},{10,11... | collective-permute-start | bytes 1572872 | tf_op jit(solution)/shard_map/ppermute | solution.py:84
  143.2 52.4 %collective-permute-start.12 = (bf16[512,512]{1,0:T(8,128)(2,1)}, bf16[512,512]{1,0:T(8,128)(2,1)}, u32[]{:S(2)}, u32[]{:S(2)}) collective-permute-start(bf16[512,512]{1,0:T(8,128)(2,1)} %collective-permute-done.8), channel_id=1, source_target_pairs={{0,1},{1,0},{2,3},{3,2},{4,5},{5,4},{6,7},{7,6},{8,9},{9,8},{10,11... | collective-permute-start | bytes 1572872 | tf_op jit(solution)/shard_map/ppermute | solution.py:84
  177.0 88.3 %collective-permute-start.36 = (bf16[512,768]{1,0:T(8,128)(2,1)}, bf16[512,768]{1,0:T(8,128)(2,1)}, u32[]{:S(2)}, u32[]{:S(2)}) collective-permute-start(bf16[512,768]{1,0:T(8,128)(2,1)} %bitcast.69), channel_id=1, source_target_pairs={{0,1},{1,0},{2,3},{3,2},{4,5},{5,4},{6,7},{7,6},{8,9},{9,8},{10,11... | collective-permute-start | bytes 2359304 | tf_op jit(solution)/shard_map/ppermute | solution.py:84
  191.1 109.6 %all-to-all-start.3 = ((bf16[4,128,1536]{2,1,0:T(8,128)(2,1)}), bf16[4,128,1536]{2,1,0:T(8,128)(2,1)}, u32[]{:S(2)}, u32[]{:S(2)}) async-start(bf16[4,128,1536]{2,1,0:T(8,128)(2,1)} %pad_maximum_fusion.8), calls=%async_computation.3 | async-start | bytes 3145728 | tf_op jit(solution)/shard_map/all_to_all | solution.py:96
  195.7 77.6 %collective-permute-start.21 = (bf16[512,1024]{1,0:T(8,128)(2,1)}, bf16[512,1024]{1,0:T(8,128)(2,1)}, u32[]{:S(2)}, u32[]{:S(2)}) collective-permute-start(bf16[512,1024]{1,0:T(8,128)(2,1)} %bitcast.55), channel_id=1, source_target_pairs={{0,2},{1,3},{2,0},{3,1},{4,6},{5,7},{6,4},{7,5},{8,10},{9,11},{10,... | collective-permute-start | bytes 3145736 | tf_op jit(solution)/shard_map/ppermute | solution.py:84
  203.4 80.7 %collective-permute-start.23 = (bf16[512,1024]{1,0:T(8,128)(2,1)}, bf16[512,1024]{1,0:T(8,128)(2,1)}, u32[]{:S(2)}, u32[]{:S(2)}) collective-permute-start(bf16[512,1024]{1,0:T(8,128)(2,1)} %bitcast.55), channel_id=1, source_target_pairs={{0,4},{1,5},{2,6},{3,7},{4,0},{5,1},{6,2},{7,3},{8,12},{9,13},{10,... | collective-permute-start | bytes 3145736 | tf_op jit(solution)/shard_map/ppermute | solution.py:84
  209.3 60.9 %collective-permute-start.41 = (bf16[512,768]{1,0:T(8,128)(2,1)}, bf16[512,768]{1,0:T(8,128)(2,1)}, u32[]{:S(2)}, u32[]{:S(2)}) collective-permute-start(bf16[512,768]{1,0:T(8,128)(2,1)} %collective-permute-done.37), channel_id=1, source_target_pairs={{0,4},{1,5},{2,6},{3,7},{4,0},{5,1},{6,2},{7,3},{8,12},{9,13},{10,... | collective-permute-start | bytes 2359304 | tf_op jit(solution)/shard_map/ppermute | solution.py:84
  273.3 57.5 %collective-permute-start.20 = (bf16[512,1024]{1,0:T(8,128)(2,1)}, bf16[512,1024]{1,0:T(8,128)(2,1)}, u32[]{:S(2)}, u32[]{:S(2)}) collective-permute-start(bf16[512,1024]{1,0:T(8,128)(2,1)} %bitcast.55), channel_id=1, source_target_pairs={{0,1},{1,0},{2,3},{3,2},{4,5},{5,4},{6,7},{7,6},{8,9},{9,8},{10,11... | collective-permute-start | bytes 3145736 | tf_op jit(solution)/shard_map/ppermute | solution.py:84
  273.6 47.7 %collective-permute-start.25 = (bf16[512,1024]{1,0:T(8,128)(2,1)}, bf16[512,1024]{1,0:T(8,128)(2,1)}, u32[]{:S(2)}, u32[]{:S(2)}) collective-permute-start(bf16[512,1024]{1,0:T(8,128)(2,1)} %collective-permute-done.21), channel_id=1, source_target_pairs={{0,4},{1,5},{2,6},{3,7},{4,0},{5,1},{6,2},{7,3},{8,12},{9,13},{10,... | collective-permute-start | bytes 3145736 | tf_op jit(solution)/shard_map/ppermute | solution.py:84
  330.8 77.7 %collective-permute-start.42 = (bf16[512,768]{1,0:T(8,128)(2,1)}, bf16[512,768]{1,0:T(8,128)(2,1)S(1)}, u32[]{:S(2)}, u32[]{:S(2)}) collective-permute-start(bf16[512,768]{1,0:T(8,128)(2,1)} %collective-permute-done.41), channel_id=1, source_target_pairs={{0,1},{1,0},{2,3},{3,2},{4,5},{5,4},{6,7},{7,6},{8,9},{9,8},{10,11... | collective-permute-start | bytes 2359304 | tf_op jit(solution)/shard_map/ppermute | solution.py:84
  358.9 44.7 %collective-permute-start.34 = (bf16[512,1536]{1,0:T(8,128)(2,1)S(1)}, bf16[512,1536]{1,0:T(8,128)(2,1)S(1)}, u32[]{:S(2)}, u32[]{:S(2)}) collective-permute-start(bf16[512,1536]{1,0:T(8,128)(2,1)S(1)} %collective-permute-done.29), channel_id=1, source_target_pairs={{0,1},{1,0},{2,3},{3,2},{4,5},{5,4},{6,7},{7,6},{8,9},{9,8},{10,11... | collective-permute-start | bytes 4718600 | tf_op jit(solution)/shard_map/ppermute | solution.py:84
  447.0 71.9 %collective-permute-start.44 = (bf16[128,2048]{0,1:T(8,128)(2,1)}, bf16[128,2048]{0,1:T(8,128)(2,1)}, u32[]{:S(2)}, u32[]{:S(2)}) collective-permute-start(bf16[128,2048]{0,1:T(8,128)(2,1)} %get-tuple-element.76), channel_id=1, source_target_pairs={{0,16},{1,17},{2,18},{3,19},{4,20},{5,21},{6,22},{7,23},{8,24},{9,... | collective-permute-start | bytes 1572872 | tf_op jit(solution)/shard_map/ppermute | solution.py:84
  454.7 64.2 %collective-permute-start.43 = (bf16[128,2048]{0,1:T(8,128)(2,1)S(1)}, bf16[128,2048]{0,1:T(8,128)(2,1)S(1)}, u32[]{:S(2)}, u32[]{:S(2)}) collective-permute-start(bf16[128,2048]{0,1:T(8,128)(2,1)S(1)} %copy-done.123), channel_id=1, source_target_pairs={{0,24},{1,25},{2,26},{3,27},{4,28},{5,29},{6,30},{7,31},{8,0},{9,1... | collective-permute-start | bytes 1572872 | tf_op jit(solution)/shard_map/ppermute | solution.py:84
  475.1 194.0 %collective-permute-start.78 = (bf16[512,1536]{1,0:T(8,128)(2,1)}, bf16[512,1536]{1,0:T(8,128)(2,1)}, u32[]{:S(2)}, u32[]{:S(2)}) collective-permute-start(bf16[512,1536]{1,0:T(8,128)(2,1)} %convolution_convert_fusion), channel_id=1, source_target_pairs={{0,1},{1,0},{2,3},{3,2},{4,5},{5,4},{6,7},{7,6},{8,9},{9,8},{10,11... | collective-permute-start | bytes 4718600 | tf_op jit(solution)/shard_map/ppermute | solution.py:84
  475.1 133.8 %collective-permute-start.86 = (bf16[512,768]{1,0:T(8,128)(2,1)}, bf16[512,768]{1,0:T(8,128)(2,1)}, u32[]{:S(2)}, u32[]{:S(2)}) collective-permute-start(bf16[512,768]{1,0:T(8,128)(2,1)} %convolution_convert_fusion.4), channel_id=1, source_target_pairs={{0,1},{1,0},{2,3},{3,2},{4,5},{5,4},{6,7},{7,6},{8,9},{9,8},{10,11... | collective-permute-start | bytes 2359304 | tf_op jit(solution)/shard_map/ppermute | solution.py:84
  602.8 140.5 %collective-permute-start.77 = (bf16[512,1536]{1,0:T(8,128)(2,1)}, bf16[512,1536]{1,0:T(8,128)(2,1)}, u32[]{:S(2)}, u32[]{:S(2)}) collective-permute-start(bf16[512,1536]{1,0:T(8,128)(2,1)} %convolution_convert_fusion.1), channel_id=1, source_target_pairs={{0,1},{1,0},{2,3},{3,2},{4,5},{5,4},{6,7},{7,6},{8,9},{9,8},{10,11... | collective-permute-start | bytes 4718600 | tf_op jit(solution)/shard_map/ppermute | solution.py:84
  613.4 59.9 %collective-permute-start.75 = (bf16[512,1536]{1,0:T(8,128)(2,1)}, bf16[512,1536]{1,0:T(8,128)(2,1)}, u32[]{:S(2)}, u32[]{:S(2)}) collective-permute-start(bf16[512,1536]{1,0:T(8,128)(2,1)} %convolution_convert_fusion.2), channel_id=1, source_target_pairs={{0,1},{1,0},{2,3},{3,2},{4,5},{5,4},{6,7},{7,6},{8,9},{9,8},{10,11... | collective-permute-start | bytes 4718600 | tf_op jit(solution)/shard_map/ppermute | solution.py:84
  673.8 70.1 %collective-permute-start.79 = (bf16[512,1536]{1,0:T(8,128)(2,1)}, bf16[512,1536]{1,0:T(8,128)(2,1)}, u32[]{:S(2)}, u32[]{:S(2)}) collective-permute-start(bf16[512,1536]{1,0:T(8,128)(2,1)} %add_convert_fusion.2), channel_id=1, source_target_pairs={{0,4},{1,5},{2,6},{3,7},{4,0},{5,1},{6,2},{7,3},{8,12},{9,13},{10,... | collective-permute-start | bytes 4718600 | tf_op jit(solution)/shard_map/ppermute | solution.py:84
  676.6 45.9 %collective-permute-start.64 = (bf16[512,512]{1,0:T(8,128)(2,1)S(1)}, bf16[512,512]{1,0:T(8,128)(2,1)S(1)}, u32[]{:S(2)}, u32[]{:S(2)}) collective-permute-start(bf16[512,512]{1,0:T(8,128)(2,1)S(1)} %add_convert_fusion.14), channel_id=1, source_target_pairs={{0,4},{1,5},{2,6},{3,7},{4,0},{5,1},{6,2},{7,3},{8,12},{9,13},{10,... | collective-permute-start | bytes 1572872 | tf_op jit(solution)/shard_map/ppermute | solution.py:84
  678.8 46.3 %collective-permute-start.84 = (bf16[512,768]{1,0:T(8,128)(2,1)S(1)}, bf16[512,768]{1,0:T(8,128)(2,1)S(1)}, u32[]{:S(2)}, u32[]{:S(2)}) collective-permute-start(bf16[512,768]{1,0:T(8,128)(2,1)S(1)} %copy-done.185), channel_id=1, source_target_pairs={{0,2},{1,3},{2,0},{3,1},{4,6},{5,7},{6,4},{7,5},{8,10},{9,11},{10,... | collective-permute-start | bytes 2359304 | tf_op jit(solution)/shard_map/ppermute | solution.py:84
  680.0 58.5 %collective-permute-start.88 = (bf16[512,768]{1,0:T(8,128)(2,1)S(1)}, bf16[512,768]{1,0:T(8,128)(2,1)S(1)}, u32[]{:S(2)}, u32[]{:S(2)}) collective-permute-start(bf16[512,768]{1,0:T(8,128)(2,1)S(1)} %add_convert_fusion.7), channel_id=1, source_target_pairs={{0,4},{1,5},{2,6},{3,7},{4,0},{5,1},{6,2},{7,3},{8,12},{9,13},{10,... | collective-permute-start | bytes 2359304 | tf_op jit(solution)/shard_map/ppermute | solution.py:84
  739.8 81.8 %all-to-all-start.7 = ((bf16[4,128,768]{2,1,0:T(8,128)(2,1)}), bf16[4,128,768]{2,1,0:T(8,128)(2,1)S(1)}, u32[]{:S(2)}, u32[]{:S(2)}) async-start(bf16[4,128,768]{2,1,0:T(8,128)(2,1)} %bitcast.545), calls=%async_computation.7 | async-start | bytes 1572864 | tf_op jit(solution)/shard_map/all_to_all | solution.py:96
  743.3 95.3 %collective-permute-start.74 = (bf16[512,1536]{1,0:T(8,128)(2,1)}, bf16[512,1536]{1,0:T(8,128)(2,1)}, u32[]{:S(2)}, u32[]{:S(2)}) collective-permute-start(bf16[512,1536]{1,0:T(8,128)(2,1)} %convolution_convert_fusion.3), channel_id=1, source_target_pairs={{0,1},{1,0},{2,3},{3,2},{4,5},{5,4},{6,7},{7,6},{8,9},{9,8},{10,11... | collective-permute-start | bytes 4718600 | tf_op jit(solution)/shard_map/ppermute | solution.py:84
  743.9 94.8 %collective-permute-start.76 = (bf16[512,1536]{1,0:T(8,128)(2,1)}, bf16[512,1536]{1,0:T(8,128)(2,1)}, u32[]{:S(2)}, u32[]{:S(2)}) collective-permute-start(bf16[512,1536]{1,0:T(8,128)(2,1)} %add_convert_fusion.4), channel_id=1, source_target_pairs={{0,4},{1,5},{2,6},{3,7},{4,0},{5,1},{6,2},{7,3},{8,12},{9,13},{10,... | collective-permute-start | bytes 4718600 | tf_op jit(solution)/shard_map/ppermute | solution.py:84
  752.3 86.4 %collective-permute-start.80 = (bf16[512,1536]{1,0:T(8,128)(2,1)}, bf16[512,1536]{1,0:T(8,128)(2,1)}, u32[]{:S(2)}, u32[]{:S(2)}) collective-permute-start(bf16[512,1536]{1,0:T(8,128)(2,1)} %add_convert_fusion.1), channel_id=1, source_target_pairs={{0,2},{1,3},{2,0},{3,1},{4,6},{5,7},{6,4},{7,5},{8,10},{9,11},{10,... | collective-permute-start | bytes 4718600 | tf_op jit(solution)/shard_map/ppermute | solution.py:84
  820.7 47.2 %collective-permute-start.71 = (bf16[64,2048]{1,0:T(8,128)(2,1)}, bf16[64,2048]{1,0:T(8,128)(2,1)}, u32[]{:S(2)}, u32[]{:S(2)}) collective-permute-start(bf16[64,2048]{1,0:T(8,128)(2,1)} %get-tuple-element.87), channel_id=1, source_target_pairs={{0,2},{1,3},{2,0},{3,1},{4,6},{5,7},{6,4},{7,5},{8,10},{9,11},{10,... | collective-permute-start | bytes 786440 | tf_op jit(solution)/shard_map/ppermute | solution.py:84
  (274 other events, 4322.7 us)

commit v2 on v1

v2 whole, which is shorter than its diff:
```python
import jax
import jax.numpy as jnp
import numpy as np
from jax import lax
from jax.experimental import pallas as pl
from jax.experimental.pallas import tpu as pltpu
from jax.sharding import PartitionSpec as P

QUERY_HEADS = 16
KEY_VALUE_HEADS = 8
HEAD_SIZE = 128
FF = 6144

rope_base = 1000000.0
norm_eps = 1e-06
BOTH = ("seq", "fsdp")
bf16 = jnp.bfloat16
f32 = jnp.float32

PARTS = KEY_VALUE_HEADS // 2
GROUP = QUERY_HEADS // KEY_VALUE_HEADS


LANES = 128
EXTRA = 16
VMEM_BYTES = 48 * 1024 * 1024
ALL_VMEM_BYTES = 60 * 1024 * 1024


def dot(left, right):
    return jnp.dot(left, right, preferred_element_type=f32)


def dot_t(left, right):
    return lax.dot_general(left, right, (((1,), (1,)), ((), ())), preferred_element_type=f32)


def dot_tn(left, right):
    return lax.dot_general(left, right, (((0,), (0,)), ((), ())), preferred_element_type=f32)


def inv_rms(tensor):
    return lax.rsqrt(jnp.mean(tensor * tensor, axis=-1, keepdims=True) + norm_eps)


def norm_back(tensor, root, gain, incoming):
    scaled = gain * incoming
    return root * scaled - tensor * (root * root * root) * jnp.mean(
        scaled * tensor, axis=-1, keepdims=True
    )


def halves(tensor):
    half_width = tensor.shape[-1] // 2
    return tensor[..., :half_width], tensor[..., half_width:]


def rotate(tensor, cosine, sine):
    front, back = halves(tensor)
    return jnp.concatenate([front * cosine - back * sine, back * cosine + front * sine], axis=-1)


def unrotate(tensor, cosine, sine):
    front, back = halves(tensor)
    return jnp.concatenate([front * cosine + back * sine, back * cosine - front * sine], axis=-1)


class Grid:
    def __init__(self):
        self.fsdp = lax.axis_size("fsdp")
        self.A = PARTS
        self.R = lax.axis_size("seq") // self.A
        self.Y = self.fsdp // 2
        s, f = lax.axis_index("seq"), lax.axis_index("fsdp")
        self.a, self.b = s // self.R, s % self.R
        self.y, self.c = f // 2, f % 2
        self.places = [
            (a, b, y, c)
            for a in range(self.A)
            for b in range(self.R)
            for y in range(self.Y)
            for c in range(2)
        ]

    def at(self, a, b, y, c):
        return (a * self.R + b % self.R) * self.fsdp + (y % self.Y) * 2 + c % 2

    def groups(self, along):
        found = {}
        for place in self.places:
            fixed = tuple(v for v, name in zip(place, "abyc") if name not in along)
            found.setdefault(fixed, []).append(self.at(*place))
        return list(found.values())

    def move(self, array, a=0, b=0, y=0, c=0):
        route = [
            (self.at(*p), self.at(p[0] ^ a, p[1] + b, p[2] + y, p[3] + c)) for p in self.places
        ]
        return lax.ppermute(array, BOTH, route)

    def swap(self, array):
        return self.move(array, c=1)

    def exchange_a(self, array):
        return lax.all_to_all(array, BOTH, 0, 0, axis_index_groups=self.groups("a"), tiled=True)

    def gather_by(self, array):
        return lax.all_gather(array, BOTH, axis_index_groups=self.groups("by"), axis=0, tiled=True)

    def scatter(self, along, array):
        return lax.psum_scatter(
            array, BOTH, axis_index_groups=self.groups(along), scatter_dimension=0, tiled=True
        )

    def deal_a(self, blocks):
        return [blocks[0]] + [self.move(blocks[d], a=d) for d in range(1, self.A)]

    def gather_a(self, array):
        return self.deal_a([array] * self.A)

    def ahead(self, array):
        return [
            lax.dynamic_index_in_dim(array, self.a ^ d, 0, keepdims=False) for d in range(self.A)
        ]

    def in_place(self, blocks):
        held = jnp.stack(blocks)
        return jnp.stack(
            [
                lax.dynamic_index_in_dim(held, self.a ^ part, 0, keepdims=False)
                for part in range(self.A)
            ]
        )

    def by_core(self, first, second):
        return (
            jnp.where(self.c == 0, first, second),
            jnp.where(self.c == 0, second, first),
        )

    def pairs(self):
        return [(i, j) for i in range(self.R) for j in range(self.Y)]

    def spread(self, piece):
        return [piece] + [self.move(piece, b=i, y=j) for i, j in self.pairs()[1:]]

    def mine_first(self, pieces):
        return [
            lax.dynamic_index_in_dim(
                pieces, (self.b - i) % self.R * self.Y + (self.y - j) % self.Y, 0, False
            )
            for i, j in self.pairs()
        ]

    def collect(self, pieces, *late):
        held = self.mine_first(pieces)
        got = [self.move(part, b=-i, y=-j) for part, (i, j) in zip(held[1:], self.pairs()[1:])]
        got = after(got, *late) if late else got
        return added(held[0], got)

    def to_rows_owner(self, partial):
        got = self.exchange_a(partial.reshape(self.A, -1, partial.shape[1]))
        return added(got[0], list(got[1:]))


def added(first, rest):
    total = first.astype(f32)
    for part in rest:
        total = total + part.astype(f32)
    return total


def whole_call(body, scalars, ins, outs):
    return pl.pallas_call(
        body,
        grid_spec=pltpu.PrefetchScalarGridSpec(
            num_scalar_prefetch=1,
            grid=(1,),
            in_specs=[pl.BlockSpec(v.shape, lambda i, s, n=v.ndim: (0,) * n) for v in ins],
            out_specs=[pl.BlockSpec(v.shape, lambda i, s, n=len(v.shape): (0,) * n) for v in outs],
        ),
        out_shape=outs,
        compiler_params=pltpu.CompilerParams(vmem_limit_bytes=VMEM_BYTES),
    )(scalars, *ins)


def like(shape, kind=bf16):
    return jax.ShapeDtypeStruct(shape, kind)


def at_multiple(number, size):
    return pl.ds(pl.multiple_of(number * size, size), size)


def reorder(arrays, source):
    count = len(arrays)

    def body(_, *refs):
        for i, at in enumerate(source):
            for src, dst in zip(refs[:count], refs[count:]):
                dst[:, i * LANES : (i + 1) * LANES] = src[:, at * LANES : (at + 1) * LANES]

    return whole_call(
        body, jnp.zeros((1,), jnp.int32), arrays, [like(v.shape, v.dtype) for v in arrays]
    )


def cut_columns(groups, spot, parts):
    flat = [a for group in groups for a in group]
    rows = flat[0].shape[0]
    widths = [a.shape[1] // (2 * parts) for a in flat]
    group_widths = [sum(a.shape[1] // (2 * parts) for a in group) for group in groups]

    def body(spot_ref, *refs):
        ins, outs = refs[: len(flat)], refs[len(flat) :]
        for half in range(2):
            core = spot_ref[0] if half == 0 else 1 - spot_ref[0]
            at = 0
            for k, group in enumerate(groups):
                start = 0
                for _ in group:
                    n = widths[at]
                    outs[2 * k + half][0, :, start : start + n] = ins[at][:, at_multiple(core, n)]
                    start += n
                    at += 1

    out_specs, out_shape = [], []
    for n in group_widths:
        for _ in range(2):
            out_specs.append(pl.BlockSpec((1, rows, n), lambda i, spot: (i, 0, 0)))
            out_shape.append(like((parts, rows, n)))
    made = pl.pallas_call(
        body,
        grid_spec=pltpu.PrefetchScalarGridSpec(
            num_scalar_prefetch=1,
            grid=(parts,),
            in_specs=[pl.BlockSpec((rows, 2 * n), lambda i, spot: (0, i)) for n in widths],
            out_specs=out_specs,
        ),
        out_shape=out_shape,
        compiler_params=pltpu.CompilerParams(vmem_limit_bytes=ALL_VMEM_BYTES),
    )(spot, *flat)
    return [(made[2 * k], made[2 * k + 1]) for k in range(len(groups))]


def merge_with_extra(keep, got, extras, spot):
    parts, rows, n = keep.shape
    more = extras[0].shape[0]

    def body(spot_ref, keep_ref, got_ref, own_ref, other_ref, out):
        here, there = spot_ref[0], 1 - spot_ref[0]
        for part in range(parts):
            out[part, at_multiple(here, rows), :] = keep_ref[part]
            out[part, at_multiple(there, rows), :] = got_ref[part]
            for core, ref in ((here, own_ref), (there, other_ref)):
                where = pl.ds(pl.multiple_of(2 * rows + core * more, more), more)
                out[part, where, :] = ref[...]

    return whole_call(
        body, spot, [keep, got, *extras], [like((parts, 2 * (rows + more), n))]
    )[0]


def merge_rows(keep, got, spot, widths):
    parts, rows, _ = keep.shape

    def body(spot_ref, keep_ref, got_ref, *outs):
        for part in range(parts):
            for core, ref in ((spot_ref[0], keep_ref), (1 - spot_ref[0], got_ref)):
                start = 0
                for n, out in zip(widths, outs):
                    out[part, at_multiple(core, rows), :] = ref[part, :, start : start + n]
                    start += n

    return whole_call(body, spot, [keep, got], [like((parts, 2 * rows, n)) for n in widths])


def stack_parts(blocks, spot):
    parts = len(blocks)
    rows, n = blocks[0].shape

    def body(spot_ref, *refs):
        for d in range(parts):
            refs[parts][at_multiple(spot_ref[1] ^ d, rows), :] = refs[d][...]

    return whole_call(body, spot, blocks, [like((parts * rows, n))])[0]


def reorder_rows(array, source):
    rows = array.shape[0] // len(source)

    def body(_, src, dst):
        for i, at in enumerate(source):
            dst[i * rows : (i + 1) * rows, :] = src[at * rows : (at + 1) * rows, :]

    return whole_call(body, jnp.zeros((1,), jnp.int32), [array], [like(array.shape)])[0]


def stack_with_extra(blocks, where, parts, rows, more):
    n = blocks[0].shape[1]

    def body(where_ref, *refs):
        for k in range(len(blocks)):
            for part in range(parts):
                start = part * (rows + more)
                place = part * len(blocks) + where_ref[k]
                refs[-2][at_multiple(place, rows), :] = refs[k][start : start + rows, :]
                refs[-1][at_multiple(place, more), :] = refs[k][start + rows : start + rows + more, :]

    total = len(blocks) * parts
    return whole_call(body, where, blocks, [like((total * rows, n)), like((total * more, n))])


def gather_heads(blocks, spot, half):
    parts = len(blocks)
    tokens = blocks[0].shape[0]

    def body(spot_ref, *refs):
        for d in range(parts):
            for k, core in enumerate((spot_ref[0], 1 - spot_ref[0])):
                where = at_multiple(2 * (spot_ref[1] ^ d) + core, half)
                refs[-1][:, where] = refs[d][:, k * half : (k + 1) * half]

    return whole_call(body, spot, blocks, [like((tokens, 2 * parts * half))])[0]


def column_blocks(arrays, parts):
    rows = arrays[0].shape[0]
    widths = [array.shape[1] // parts for array in arrays]

    def body(_, *refs):
        for part in range(parts):
            start = 0
            for n, src in zip(widths, refs):
                refs[-1][part, :, start : start + n] = src[:, part * n : (part + 1) * n]
                start += n

    return whole_call(
        body, jnp.zeros((1,), jnp.int32), arrays, [like((parts, rows, sum(widths)))]
    )[0]


def join_columns(keep, got, spot, widths):
    parts, rows, total = keep.shape

    def body(spot_ref, keep_ref, got_ref, *outs):
        mine = pl.program_id(1) == spot_ref[0]
        start = 0
        for n, out in zip(widths, outs):
            part = slice(start, start + n)
            out[...] = jnp.where(mine, keep_ref[0, :, part], got_ref[0, :, part]).astype(f32)
            start += n

    block = pl.BlockSpec((1, rows, total), lambda i, h, spot: (i, 0, 0))
    return pl.pallas_call(
        body,
        grid_spec=pltpu.PrefetchScalarGridSpec(
            num_scalar_prefetch=1,
            grid=(parts, 2),
            in_specs=[block, block],
            out_specs=[pl.BlockSpec((rows, n), lambda i, h, spot: (0, 2 * i + h)) for n in widths],
        ),
        out_shape=[like((rows, 2 * parts * n), f32) for n in widths],
        compiler_params=pltpu.CompilerParams(vmem_limit_bytes=VMEM_BYTES),
    )(spot, keep, got)


def token_products(groups, orders):
    counts = [len(lefts) for lefts, _ in groups]
    tokens, width = groups[0][0][0].shape
    widths = [rights[0].shape[1] for _, rights in groups]
    blocks = len(orders[0])
    unit = width // blocks
    steps = min(4, blocks)
    per_step = blocks // steps

    def body(order_ref, *refs):
        for k in range(per_step):
            at, start = 0, 0
            for m, (count, n) in enumerate(zip(counts, widths)):
                place = order_ref[m * blocks + pl.program_id(0) * per_step + k]
                where = at_multiple(place, unit)
                total = dot_tn(refs[at][:, where], refs[at + count][...])
                for i in range(1, count):
                    total = total + dot_tn(refs[at + i][:, where], refs[at + count + i][...])
                refs[-1][k * unit : (k + 1) * unit, start : start + n] = total.astype(bf16)
                at += 2 * count
                start += n

    flat = [v for lefts, rights in groups for v in (*lefts, *rights)]
    return pl.pallas_call(
        body,
        grid_spec=pltpu.PrefetchScalarGridSpec(
            num_scalar_prefetch=1,
            grid=(steps,),
            in_specs=[pl.BlockSpec(v.shape, lambda i, s: (0, 0)) for v in flat],
            out_specs=pl.BlockSpec((per_step * unit, sum(widths)), lambda i, s: (i, 0)),
        ),
        out_shape=like((width, sum(widths))),
        compiler_params=pltpu.CompilerParams(vmem_limit_bytes=VMEM_BYTES),
    )(jnp.asarray(np.concatenate(orders), jnp.int32), *flat)


def product_t(left, right, rows, add=None):
    tokens, n = left.shape
    width = right.shape[0]

    def body(left_ref, right_ref, *refs):
        made = dot_t(left_ref[...], right_ref[...])
        if add is not None:
            made = made + refs[0][...].astype(f32)
        refs[-1][...] = made.astype(refs[-1].dtype)

    ins = [left, right] + ([] if add is None else [add])
    block = pl.BlockSpec((tokens, rows), lambda i: (0, i))
    return pl.pallas_call(
        body,
        grid=(width // rows,),
        in_specs=[
            pl.BlockSpec((tokens, n), lambda i: (0, 0)),
            pl.BlockSpec((rows, n), lambda i: (i, 0)),
        ]
        + ([] if add is None else [block]),
        out_specs=block,
        out_shape=like((tokens, width)),
        compiler_params=pltpu.CompilerParams(vmem_limit_bytes=VMEM_BYTES),
    )(*ins)


def after(values, *others):
    return list(lax.optimization_barrier(tuple(values) + others))[: len(values)]


def on_device(
    tokens,
    block_pos,
    w_query,
    key_weight,
    value_weight,
    w_out,
    w_gate,
    w_up,
    w_down,
    attn_gain,
    mlp_gain,
    qk_gain,
    grad_out,
):
    g = Grid()
    A, R, Y = g.A, g.R, g.Y
    a, b, y, c = g.a, g.b, g.y, g.c
    pieces = R * Y
    rows_own = w_query.shape[0]
    width = tokens.shape[2]
    piece_width = width // pieces
    token_rows = tokens.shape[1]
    group_rows = A * token_rows
    score_scale = HEAD_SIZE ** (-0.5)
    q_cols = GROUP * HEAD_SIZE
    qkv_cols = q_cols + 2 * HEAD_SIZE
    ff_cols = FF // (2 * A)
    spot = jnp.stack([c, a]).astype(jnp.int32)

    unit = 2 * rows_own

    def permute(arrays, back):
        cuts = (R * Y, A, unit) if back else (A, R * Y, unit)
        columns = np.arange(width).reshape(cuts).transpose(1, 0, 2).reshape(-1)
        if unit % LANES == 0:
            return reorder(arrays, (columns[::LANES] // LANES).tolist())
        return [jnp.take(array, columns, axis=1) for array in arrays]

    places = jnp.stack(
        [(b - i) % R * Y + (y - j) % Y for i, j in g.pairs()]
    ).astype(jnp.int32)

    x_own, dout_own = tokens[0], grad_out[0]
    x_parts = g.gather_a(x_own)
    out_w = lax.all_gather(w_out, BOTH, axis=0, tiled=True)
    cuts = cut_columns(
        [[w_query, key_weight, value_weight], [w_gate, w_up, w_down]], spot, A
    )
    packed = jnp.concatenate([attn_gain, mlp_gain, qk_gain.reshape(-1)])
    packed = jnp.stack(
        [jnp.pad(v, (0, qkv_cols - v.shape[0])) for v in (packed, block_pos[0].astype(bf16))]
    )
    packed = jnp.pad(packed, ((0, EXTRA - 2), (0, 0)))
    sent = jnp.concatenate([cuts[0][1].reshape(A * rows_own, qkv_cols), packed])
    got = g.swap(sent)
    other_packed = got[A * rows_own :]
    qkv_local = merge_with_extra(
        cuts[0][0],
        got[: A * rows_own].reshape(A, rows_own, qkv_cols),
        [packed, other_packed],
        spot,
    )
    qkv_piece = g.exchange_a(qkv_local).reshape(-1, qkv_cols)
    qkv_w, extras = stack_with_extra(g.spread(qkv_piece), places, A, unit, 2 * EXTRA)
    packed = extras.reshape(2 * A * pieces, EXTRA, qkv_cols)[:, 0].astype(f32)
    first_gain = packed[..., :rows_own].reshape(width)
    second_gain = packed[..., rows_own : 2 * rows_own].reshape(width)
    small = packed[..., 2 * rows_own : 2 * rows_own + 2 * (HEAD_SIZE // (2 * pieces * A))]
    small = jnp.transpose(small.reshape(2 * A * pieces, 2, -1), (1, 0, 2)).reshape(2, HEAD_SIZE)
    query_gain, key_gain = small[0], small[1]

    gu_local, down_local = merge_rows(cuts[1][0], g.swap(cuts[1][1]), spot, [2 * ff_cols, ff_cols])
    (gu_local,) = after([gu_local], qkv_w, *x_parts)
    gu_piece = g.exchange_a(gu_local).reshape(A * unit, 2 * ff_cols)
    (down_local,) = after([down_local], gu_piece)
    down_piece = g.exchange_a(down_local).reshape(A * unit, ff_cols)

    blocks_seen = block_pos.shape[1]
    orders = [block_pos[0], other_packed[1, :blocks_seen].astype(jnp.int32)]
    row_offsets = jnp.arange(token_rows, dtype=jnp.int32)

    def positions(order, shift):
        blocks = [order[part * R + (b - shift) % R] for part in range(A)]
        return jnp.concatenate([block * token_rows + row_offsets for block in blocks])

    local_pos = [positions(order, 0) for order in orders]
    key_pos = [jnp.concatenate([positions(order, i) for i in range(R)]) for order in orders]
    exponent = jnp.arange(HEAD_SIZE // 2, dtype=f32) * (-2.0 / HEAD_SIZE)
    angles = jnp.concatenate(local_pos).astype(f32)[:, None] * (rope_base**exponent)[None, :]
    cosine, sine = jnp.cos(angles), jnp.sin(angles)
    cosine3, sine3 = cosine[:, None, :], sine[:, None, :]

    x_group = stack_parts(x_parts, spot)
    inputs = x_group.astype(f32)
    x_root = inv_rms(inputs)
    normed_own = (inputs * x_root * first_gain).astype(bf16)
    normed = [normed_own, g.swap(normed_own)]
    made = jnp.concatenate([dot(part, qkv_w) for part in normed], axis=0)
    gu_by = g.gather_by(after([gu_piece], out_w, made)[0])
    down_w = g.gather_by(down_piece)
    q_pre = made[:, :q_cols].reshape(2 * group_rows, GROUP, HEAD_SIZE)
    k_pre = made[:, q_cols : q_cols + HEAD_SIZE]
    value = made[:, q_cols + HEAD_SIZE :].astype(bf16)
    q_root, k_root = inv_rms(q_pre), inv_rms(k_pre)
    query = rotate(q_pre * q_root * query_gain, cosine3, sine3).astype(bf16)
    key = rotate(k_pre * k_root * key_gain, cosine, sine).astype(bf16)
    key_values = jnp.concatenate([key, value], axis=1)
    key_values = [key_values] + [g.move(key_values, b=i) for i in range(1, R)]

    def of_sequence(array, n):
        return array[n * group_rows : (n + 1) * group_rows]

    keys = [
        jnp.concatenate([of_sequence(kv, n)[:, :HEAD_SIZE] for kv in key_values]) for n in range(2)
    ]
    values = [
        jnp.concatenate([of_sequence(kv, n)[:, HEAD_SIZE:] for kv in key_values]) for n in range(2)
    ]

    visible = [local_pos[n][:, None] >= key_pos[n][None, :] for n in range(2)]

    def attend(n):
        scores = jnp.einsum(
            "qgd,td->gqt", of_sequence(query, n), keys[n], preferred_element_type=f32
        )
        scores = jnp.where(visible[n], scores * score_scale, -1e30)
        top = jnp.max(scores, axis=-1, keepdims=True)
        weights = jnp.exp(scores - top)
        totals = jnp.sum(weights, axis=-1, keepdims=True)
        log_total = top + jnp.log(totals)
        mixed = jnp.einsum(
            "gqt,td->gqd", weights.astype(bf16), values[n], preferred_element_type=f32
        )
        return mixed / totals, log_total

    def flat(heads):
        return jnp.transpose(heads, (1, 0, 2)).reshape(group_rows, q_cols).astype(bf16)

    mixed_other = attend(1)
    got = g.swap(flat(mixed_other[0]))
    mixed = [attend(0), mixed_other]
    attended = jnp.concatenate([flat(mixed[0][0]), got], axis=1)
    (attended,) = after([attended], down_piece)
    att_parts = g.gather_a(attended)
    att_heads = gather_heads(att_parts, spot, q_cols)

    (dout_by,) = permute(after([dout_own], att_parts[-1]), False)
    dout_parts = g.gather_a(dout_by)
    middle = inputs + dot_t(att_heads, out_w)
    root2 = inv_rms(middle)
    normed2_own = (middle * root2 * second_gain).astype(bf16)
    normed2 = [normed2_own, g.swap(normed2_own)]
    gu_w = reorder_rows(gu_by, np.arange(R * Y * A).reshape(R * Y, A).T.reshape(-1).tolist())
    both = [dot(part, gu_w) for part in normed2]
    dout_group = stack_parts(after(dout_parts, both[0]), spot)
    dout = [dout_group, g.swap(dout_group)]
    d_inner = [dot(part, down_w) for part in dout]

    def feed(n):
        gate, up = both[n][:, :ff_cols], both[n][:, ff_cols:]
        s = jax.nn.sigmoid(gate)
        act = gate * s
        d_gate = d_inner[n] * up * s * (1.0 + gate * (1.0 - s))
        return (
            (act * up).astype(bf16),
            jnp.concatenate([d_gate, d_inner[n] * act], axis=1).astype(bf16),
        )

    fed = [feed(0), feed(1)]
    inner, d_gu = [f[0] for f in fed], [f[1] for f in fed]

    def of_both(parts, weight):
        got = g.swap(product_t(parts[1], weight, 512))
        return product_t(parts[0], weight, 512, got)

    def own_rows(array):
        return lax.dynamic_slice_in_dim(array, a * token_rows, token_rows, axis=0)

    d_normed2 = of_both(d_gu, gu_w)
    mlp_gain_grad = jnp.sum(d_normed2 * middle * root2, axis=0)
    e2 = g.to_rows_owner(d_normed2)
    middle_own = own_rows(middle)
    grad_middle = dout_own.astype(f32) + norm_back(middle_own, own_rows(root2), second_gain, e2)

    by_order = np.arange(R * A * Y).reshape(A, R * Y).T.reshape(-1)

    def over_tokens(*groups):
        if unit % LANES == 0:
            orders = [by_order if natural else np.arange(R * A * Y) for _, _, natural in groups]
            return token_products([group[:2] for group in groups], orders)
        made = []
        for lefts, rights, natural in groups:
            total = dot_tn(lefts[0], rights[0]) + dot_tn(lefts[1], rights[1])
            total = total.reshape(R * A * Y, unit, -1)
            made.append(jnp.take(total, by_order, axis=0) if natural else total)
        return jnp.concatenate(made, axis=-1).reshape(width, -1).astype(bf16)

    def to_owner(dealt, widths):
        keep = lax.dynamic_index_in_dim(dealt, c, 1, keepdims=False)
        send = lax.dynamic_index_in_dim(dealt, 1 - c, 1, keepdims=False)
        return join_columns(keep, g.swap(send), spot, widths)

    def part_rows(total):
        return total.reshape(A, unit, -1)

    def core_rows(dealt):
        return dealt.reshape(A, 2, rows_own, -1)

    mlp_grad = over_tokens((after(normed2, d_normed2), d_gu, True), (dout, inner, False))
    mlp_total = g.scatter("by", mlp_grad)
    out_part = of_both(after(inner, mlp_grad), down_w)

    d_branch = grad_middle.astype(bf16)
    d_att = dot(d_branch, out_w).astype(bf16)
    if pieces * unit % LANES == 0:
        dealt = column_blocks([d_att, d_branch], A)
    else:
        dealt = jnp.concatenate([d_att.reshape(token_rows, A, -1), d_branch.reshape(token_rows, A, -1)], -1)
        dealt = jnp.swapaxes(dealt, 0, 1)
    dealt = g.exchange_a(dealt).reshape(group_rows, -1)
    d_att, rows_of_part = dealt[:, : 2 * q_cols], dealt[:, 2 * q_cols :]
    (out_part,) = after([out_part], d_att)
    out_mine = g.scatter("a", out_part)
    mlp_dealt = g.exchange_a(after([part_rows(mlp_total)], d_att)[0])
    mine_half, other_half = g.by_core(d_att[:, :q_cols], d_att[:, q_cols:])
    d_att = [mine_half, g.swap(other_half)]

    def attend_back(n):
        d_mixed = d_att[n].reshape(group_rows, GROUP, HEAD_SIZE)
        o, log_total = mixed[n]
        delta = jnp.sum(jnp.transpose(d_mixed, (1, 0, 2)).astype(f32) * o, axis=-1, keepdims=True)
        q = of_sequence(query, n)
        scores = jnp.einsum("qgd,td->gqt", q, keys[n], preferred_element_type=f32)
        scores = jnp.where(visible[n], scores * score_scale, -1e30)
        weights = jnp.exp(scores - log_total)
        d_weights = jnp.einsum("qgd,td->gqt", d_mixed, values[n], preferred_element_type=f32)
        d_scores = (weights * (d_weights - delta)).astype(bf16)
        d_query = jnp.einsum("gqt,td->qgd", d_scores, keys[n], preferred_element_type=f32)
        d_key = jnp.einsum("gqt,qgd->td", d_scores, q, preferred_element_type=f32)
        d_value = jnp.einsum(
            "gqt,qgd->td", weights.astype(bf16), d_mixed, preferred_element_type=f32
        )
        return d_query * score_scale, jnp.concatenate([d_key * score_scale, d_value], axis=1)

    backs = [attend_back(0), attend_back(1)]
    d_query = jnp.concatenate([back[0] for back in backs], axis=0)
    d_kv = jnp.concatenate([of_sequence(back[1], 0) for back in backs], axis=0)
    for i in range(1, R):
        block = jnp.concatenate([of_sequence(back[1], i) for back in backs], axis=0)
        d_kv = d_kv + g.move(block.astype(bf16), b=-i).astype(f32)
    e_q = unrotate(d_query, cosine3, sine3)
    e_k = unrotate(d_kv[:, :HEAD_SIZE], cosine, sine)
    d_q_pre = norm_back(q_pre, q_root, query_gain, e_q).reshape(2 * group_rows, q_cols)
    d_k_pre = norm_back(k_pre, k_root, key_gain, e_k)
    qk_gain_grad = jnp.stack(
        [jnp.sum(e_q * q_pre * q_root, axis=(0, 1)), jnp.sum(e_k * k_pre * k_root, axis=0)]
    )
    d_qkv = jnp.concatenate([d_q_pre, d_k_pre, d_kv[:, HEAD_SIZE:]], axis=1).astype(bf16)
    d_qkv = [of_sequence(d_qkv, 0), of_sequence(d_qkv, 1)]
    qkv_grad = over_tokens((normed, d_qkv, True))
    d_qkv = after(d_qkv, qkv_grad, mlp_dealt)
    d_normed = of_both(d_qkv, qkv_w)
    (out_sum,) = permute([out_mine.astype(f32)], True)
    result = (middle_own + out_sum).astype(bf16)
    qkv_total = g.scatter("by", qkv_grad)
    attn_gain_grad = jnp.sum(d_normed * inputs * x_root, axis=0)
    e1 = g.to_rows_owner(d_normed)
    grad_input = grad_middle + norm_back(
        x_own.astype(f32), inv_rms(x_own.astype(f32)), first_gain, e1
    )

    (qkv_total,) = after([qkv_total], e1)
    dealt = core_rows(g.exchange_a(part_rows(qkv_total)))
    grad_wq, grad_wk, grad_wv = to_owner(dealt, [q_cols, HEAD_SIZE, HEAD_SIZE])

    def by_first(array):
        return jnp.swapaxes(array, 0, 1).reshape(pieces, A, 2, -1)

    small = qk_gain_grad.reshape(2, A, pieces, 2, -1)
    small = jnp.transpose(small, (2, 1, 3, 0, 4)).reshape(pieces, A, 2, -1)
    sums = jnp.concatenate(
        [
            by_first(attn_gain_grad.reshape(A, pieces, 2, rows_own)),
            by_first(mlp_gain_grad.reshape(A, pieces, 2, rows_own)),
            small,
        ],
        axis=-1,
    )
    keep = lax.dynamic_index_in_dim(sums, c, 2, keepdims=False)
    send = lax.dynamic_index_in_dim(sums, 1 - c, 2, keepdims=False)
    sums = g.collect(keep + g.swap(send))
    sums = sum(g.deal_a(g.ahead(sums)))
    sums = [
        sums[:rows_own],
        sums[rows_own : 2 * rows_own],
        sums[2 * rows_own :].reshape(2, -1),
    ]

    (rows_of_part,) = after([rows_of_part], d_kv)
    grad_wo = g.scatter("byc", dot_tn(rows_of_part, att_heads).astype(bf16)).astype(f32)
    grad_wg, grad_wu, grad_wd = to_owner(core_rows(mlp_dealt), [ff_cols] * 3)
    return (
        result[None],
        grad_input[None],
        grad_wq,
        grad_wk,
        grad_wv,
        grad_wo,
        grad_wg,
        grad_wu,
        grad_wd,
        *sums,
    )


def solution(mesh):
    placed = (
        P("fsdp", "seq", None),
        P("fsdp", None),
        P(("seq", "fsdp"), None),
        P(("seq", "fsdp"), None),
        P(("seq", "fsdp"), None),
        P(("seq", "fsdp"), None),
        P(("seq", "fsdp"), None),
        P(("seq", "fsdp"), None),
        P(("seq", "fsdp"), None),
        P(("seq", "fsdp")),
        P(("seq", "fsdp")),
        P(None, ("seq", "fsdp")),
        P("fsdp", "seq", None),
    )
    return jax.shard_map(
        on_device,
        mesh=mesh,
        in_specs=placed,
        out_specs=(
            P("fsdp", "seq", None),
            P("fsdp", "seq", None),
            P(("seq", "fsdp"), None),
            P(("seq", "fsdp"), None),
            P(("seq", "fsdp"), None),
            P(("seq", "fsdp"), None),
            P(("seq", "fsdp"), None),
            P(("seq", "fsdp"), None),
            P(("seq", "fsdp"), None),
            P(("seq", "fsdp")),
            P(("seq", "fsdp")),
            P(None, ("seq", "fsdp")),
        ),
        check_vma=False,
    )
```

time: 933 us -> 718 us (0.77)
  matrix products: 184 us -> 72.3 us
  Pallas kernels: 0 us -> 84.9 us
  waiting for transfers between devices: 388 us -> 308 us
  local copies, waits for them, and re-layouts: 120 us -> 57 us
  other arithmetic: 95.3 us -> 61 us
  starting transfers between devices: 127 us -> 96.8 us
  between operations: 9.92 us -> 26.8 us
    ppermute x94 -> x33, waiting for transfers between devices: 305 us -> 111 us  [move(): return lax.ppermute(array, BOTH, route)]
    all_to_all x9 -> x8, waiting for transfers between devices: 82.9 us -> 196 us  [exchange_a(): lax.all_to_all(array, BOTH, 0, 0, axis_index_groups=self.groups('a'), til...]
    pallas_call x0 -> x21, Pallas kernels: none -> 84.9 us  [the longest x6 27.4 us: product_t(): pl.pallas_call(body, grid=(width // rows,), in_specs=[pl.BlockSpec((token...]
    dot_general x25 -> x1, matrix products: 56.7 us -> 2.72 us  [dot_tn(): lax.dot_general(left, right, (((0,), (0,)), ((), ())), preferred_element_...]
    ppermute x94 -> x33, starting transfers between devices: 77.8 us -> 34.3 us  [move(): return lax.ppermute(array, BOTH, route)]
    dot_general x32 -> x1, matrix products: 47.1 us -> 7.86 us  [dot_t(): lax.dot_general(left, right, (((1,), (1,)), ((), ())), preferred_element_...]
    reshape x26 -> x5, local copies, waits for them, and re-layouts: 36.8 us -> 1.77 us  [the longest x1 1.49 us: on_device(): q_pre = made[:, :q_cols].reshape(2 * group_rows, GROUP, HEAD_SIZE)]
    dot_general x32 -> x7, matrix products: 59.8 us -> 38 us  [dot(): return jnp.dot(left, right, preferred_element_type=f32)]
  transfers between devices with their start and end apart: 103 -> 48, of which waited for: 30 -> 19; matrix products, arithmetic and copies ran while one was open for 37% -> 22% of each run, Pallas kernels for 0% -> 7%
where the time goes in v2:
time: 718 us; the launch traced here: 707 us
  waiting for transfers between devices  308 us (43%)
  starting transfers between devices  96.8 us (13%)
  Pallas kernels  84.9 us (12%)
  matrix products  72.3 us (10%)
  other arithmetic  61 us (8%)
  local copies, waits for them, and re-layouts  57 us (8%)
  between operations  26.8 us (4%)
    all_to_all x8, waiting for transfers between devices, exchange_a(): lax.all_to_all(array, BOTH, 0, 0, axis_index_groups=self.groups('a'), til...  196 us
    ppermute x33, waiting for transfers between devices, move(): return lax.ppermute(array, BOTH, route)  111 us
    all_to_all x8, starting transfers between devices, exchange_a(): lax.all_to_all(array, BOTH, 0, 0, axis_index_groups=self.groups('a'), til...  61.8 us
    dot_general x7, matrix products, dot(): return jnp.dot(left, right, preferred_element_type=f32)  38 us
    ppermute x33, starting transfers between devices, move(): return lax.ppermute(array, BOTH, route)  34.3 us
    pallas_call x6, Pallas kernels, product_t(): pl.pallas_call(body, grid=(width // rows,), in_specs=[pl.BlockSpec((token...  27.4 us
    unnamed x232, local copies, waits for them, and re-layouts  27.2 us
    pallas_call x2, Pallas kernels, token_products(): pl.pallas_call(body, grid_spec=pltpu.PrefetchScalarGridSpec(num_scalar_pr...  22.4 us
  transfers between devices with their start and end apart: 48, of which 19 were waited for; matrix products, arithmetic and copies ran while one was open for 22% of the time, Pallas kernels for 7%

profile of v2, /device:TPU:0, one launch (start us, length us, event | category | flops | bytes accessed | tf_op | source)
XLA Modules:
  0.0 707.2 jit_solution(11322936025827585825)
XLA Ops:
  10.7 5.0 shard_map.239
  21.0 6.2 all-to-all-start
  27.2 20.4 %all-to-all-done = bf16[4,160,512]{2,1,0:T(8,128)(2,1)S(1)} async-done(((bf16[4,160,512]{2,1,0:T(8,128)(2,1)}), bf16[4,160,512]{2,1,0:T(8,128)(2,1)S(1)}, u32[]{:S(2)}, u32[]{:S(2)}) %all-to-all-start) | async-done | bytes 655392 | tf_op jit(solution)/shard_map/all_to_all | solution.py:105
  59.0 9.0 %collective-permute-done.4.refs_1_ = bf16[640,512]{1,0:T(8,128)(2,1)S(1)} collective-permute-done((bf16[640,512]{1,0:T(8,128)(2,1)S(1)}, bf16[640,512]{1,0:T(8,128)(2,1)S(1)}, u32[]{:S(2)}, u32[]{:S(2)}) %collective-permute-start.4) | collective-permute-done | bytes 655392 | tf_op jit(solution)/shard_map/ppermute | solution.py:99
  73.3 16.4 %collective-permute-done.6.refs_3_ = bf16[640,512]{1,0:T(8,128)(2,1)S(1)} collective-permute-done((bf16[640,512]{1,0:T(8,128)(2,1)S(1)}, bf16[640,512]{1,0:T(8,128)(2,1)S(1)}, u32[]{:S(2)}, u32[]{:S(2)}) %collective-permute-start.6) | collective-permute-done | bytes 655392 | tf_op jit(solution)/shard_map/ppermute | solution.py:99
  92.6 21.2 %collective-permute-done.1.refs_2_ = bf16[128,2048]{1,0:T(8,128)(2,1)S(1)} collective-permute-done((bf16[128,2048]{1,0:T(8,128)(2,1)S(1)}, bf16[128,2048]{1,0:T(8,128)(2,1)S(1)}, u32[]{:S(2)}, u32[]{:S(2)}) %collective-permute-start.1) | collective-permute-done | bytes 524320 | tf_op jit(solution)/shard_map/ppermute | solution.py:99
  115.4 21.2 %all-to-all-start.1 = ((bf16[4,128,1536]{2,1,0:T(8,128)(2,1)}), bf16[4,128,1536]{2,1,0:T(8,128)(2,1)}, u32[]{:S(2)}, u32[]{:S(2)}) async-start(bf16[4,128,1536]{2,1,0:T(8,128)(2,1)} %copy-done.18), calls=%async_computation.1 | async-start | bytes 3145728 | tf_op jit(solution)/shard_map/all_to_all | solution.py:105
  147.8 25.2 %all-to-all-done.1 = bf16[4,128,1536]{2,1,0:T(8,128)(2,1)} async-done(((bf16[4,128,1536]{2,1,0:T(8,128)(2,1)}), bf16[4,128,1536]{2,1,0:T(8,128)(2,1)}, u32[]{:S(2)}, u32[]{:S(2)}) %all-to-all-start.1) | async-done | bytes 1572896 | tf_op jit(solution)/shard_map/all_to_all | solution.py:105
  209.9 11.1 %collective-permute-done.8 = bf16[1024,256]{1,0:T(8,128)(2,1)} collective-permute-done((bf16[1024,256]{1,0:T(8,128)(2,1)}, bf16[1024,256]{1,0:T(8,128)(2,1)}, u32[]{:S(2)}, u32[]{:S(2)}) %collective-permute-start.8) | collective-permute-done | bytes 524320 | tf_op jit(solution)/shard_map/ppermute | solution.py:99
  243.9 11.3 %collective-permute-done.13.refs_3_ = bf16[512,512]{1,0:T(8,128)(2,1)} collective-permute-done((bf16[512,512]{1,0:T(8,128)(2,1)S(1)}, bf16[512,512]{1,0:T(8,128)(2,1)}, u32[]{:S(2)}, u32[]{:S(2)}) %collective-permute-start.13) | collective-permute-done | bytes 524320 | tf_op jit(solution)/shard_map/ppermute | solution.py:99
  256.2 6.7 collective-permute-start.15
  265.3 6.0 collective-permute-done.11.refs_1_
  271.3 12.8 %collective-permute-done.12.refs_2_ = bf16[512,512]{1,0:T(8,128)(2,1)} collective-permute-done((bf16[512,512]{1,0:T(8,128)(2,1)S(1)}, bf16[512,512]{1,0:T(8,128)(2,1)}, u32[]{:S(2)}, u32[]{:S(2)}) %collective-permute-start.12) | collective-permute-done | bytes 524320 | tf_op jit(solution)/shard_map/ppermute | solution.py:99
  286.3 7.9 %multiply_reduce_fusion.1 = (f32[512]{0:T(512)S(1)}, f32[512,2048]{1,0:T(8,128)S(1)}) fusion(bf16[512,2048]{1,0:T(8,128)(2,1)S(1)} %shard_map.243, bf16[2048,2048]{1,0:T(8,128)(2,1)} %all-gather.4.cloned.1.call-done, bf16[512,2048]{1,0:T(8,128)(2,1)S(1)} %shard_map.238), kind=kOutput, calls=%fused_computation.21 | convolution fusion | flops 4299161088 | bytes 16779264 | tf_op jit(solution)/shard_map/dot_general | solution.py:35
  296.8 5.9 shard_map.244.right_ref
  302.7 8.7 %fusion.125 = f32[512,1536]{1,0:T(8,128)} fusion(bf16[512,2048]{1,0:T(8,128)(2,1)} %multiply_convert_fusion.refs_0_, bf16[2048,1536]{1,0:T(8,128)(2,1)} %shard_map.244.right_ref), kind=kOutput, calls=%fused_computation.308 | convolution fusion | flops 3221225472 | bytes 11534336 | tf_op jit(solution)/shard_map/dot_general | solution.py:31
  311.4 6.3 collective-permute-done.16.refs_2_
  321.3 6.7 fusion.126
  328.0 5.6 multiply_convert_fusion.2
  333.7 6.2 shard_map.247
  345.4 6.3 shard_map.248
  353.0 16.4 %shard_map.249 = bf16[2048,2304]{1,0:T(8,128)(2,1)} custom-call(s32[32]{0:T(128)S(1)} %copy-done.27, bf16[512,2048]{1,0:T(8,128)(2,1)} %multiply_convert_fusion.refs_0_, bf16[512,2048]{1,0:T(8,128)(2,1)} %collective-permute-done.14.refs_1_, bf16[512,1536]{1,0:T(8,128)(2,1)S(1)} %pad_maximum_fusion.1.left_ref.refs_2_, ...), custom_call_target="tpu_custom_call" | custom-call | tf_op jit(solution)/shard_map/pallas_call | solution.py:391
  369.4 12.7 %all-to-all-start.3 = ((bf16[4,128,2048]{2,1,0:T(8,128)(2,1)}), bf16[4,128,2048]{2,1,0:T(8,128)(2,1)}, u32[]{:S(2)}, u32[]{:S(2)}) async-start(bf16[4,128,2048]{2,1,0:T(8,128)(2,1)} %bitcast.293), calls=%async_computation.3 | async-start | bytes 4194304 | tf_op jit(solution)/shard_map/all_to_all | solution.py:105
  383.4 47.8 %all-to-all-done.3 = bf16[4,128,2048]{2,1,0:T(8,128)(2,1)} async-done(((bf16[4,128,2048]{2,1,0:T(8,128)(2,1)}), bf16[4,128,2048]{2,1,0:T(8,128)(2,1)}, u32[]{:S(2)}, u32[]{:S(2)}) %all-to-all-start.3) | async-done | bytes 2097184 | tf_op jit(solution)/shard_map/all_to_all | solution.py:105
  449.7 23.4 %all-to-all-done.4 = bf16[4,128,1024]{2,1,0:T(8,128)(2,1)} async-done(((bf16[4,128,1024]{2,1,0:T(8,128)(2,1)}), bf16[4,128,1024]{2,1,0:T(8,128)(2,1)}, u32[]{:S(2)}, u32[]{:S(2)}) %all-to-all-start.4) | async-done | bytes 1048608 | tf_op jit(solution)/shard_map/all_to_all | solution.py:105
  498.6 11.4 %collective-permute-done.22 = bf16[1024,256]{1,0:T(8,128)(2,1)S(1)} collective-permute-done((bf16[1024,256]{1,0:T(8,128)(2,1)S(1)}, bf16[1024,256]{1,0:T(8,128)(2,1)S(1)}, u32[]{:S(2)}, u32[]{:S(2)}) %collective-permute-start.22) | collective-permute-done | bytes 524320 | tf_op jit(solution)/shard_map/ppermute | solution.py:99
  552.0 6.0 shard_map.254
  559.3 46.3 %all-to-all-done.5 = bf16[4,128,2304]{2,1,0:T(8,128)(2,1)} async-done(((bf16[4,128,2304]{2,1,0:T(8,128)(2,1)}), bf16[4,128,2304]{2,1,0:T(8,128)(2,1)}, u32[]{:S(2)}, u32[]{:S(2)}) %all-to-all-start.5) | async-done | bytes 2359328 | tf_op jit(solution)/shard_map/all_to_all | solution.py:105
  621.5 4.8 all-to-all-start.6
  644.2 6.3 shard_map.258
  655.0 20.2 %all-to-all-done.6 = bf16[4,128,2048]{2,1,0:T(8,128)(2,1)} async-done(((bf16[4,128,2048]{2,1,0:T(8,128)(2,1)}), bf16[4,128,2048]{2,1,0:T(8,128)(2,1)}, u32[]{:S(2)}, u32[]{:S(2)}) %all-to-all-start.6) | async-done | bytes 2097184 | tf_op jit(solution)/shard_map/all_to_all | solution.py:105
  682.1 12.9 %all-to-all-done.7 = bf16[4,128,512]{2,1,0:T(8,128)(2,1)S(1)} async-done(((bf16[4,128,512]{2,1,0:T(8,128)(2,1)}), bf16[4,128,512]{2,1,0:T(8,128)(2,1)S(1)}, u32[]{:S(2)}, u32[]{:S(2)}) %all-to-all-start.7) | async-done | bytes 524320 | tf_op jit(solution)/shard_map/all_to_all | solution.py:105
  (506 shorter events, 245.7 us)
Async XLA Ops:
  7.2 165.8 %all-gather.4.cloned.1.call-start = ((), (), s32[]{:S(2)}) async-start(), calls=%async_computation.12 | async-start | bytes 8650752 | tf_op jit(solution)/shard_map/all_gather | solution.py:479
  21.0 26.6 %all-to-all-start = ((bf16[4,160,512]{2,1,0:T(8,128)(2,1)}), bf16[4,160,512]{2,1,0:T(8,128)(2,1)S(1)}, u32[]{:S(2)}, u32[]{:S(2)}) async-start(bf16[4,160,512]{2,1,0:T(8,128)(2,1)} %shard_map.240), calls=%async_computation | async-start | bytes 1310720 | tf_op jit(solution)/shard_map/all_to_all | solution.py:105
  27.2 29.9 %collective-permute-start.10 = (bf16[4,64,2304]{2,1,0:T(8,128)(2,1)}, bf16[4,64,2304]{2,1,0:T(8,128)(2,1)}, u32[]{:S(2)}, u32[]{:S(2)}) collective-permute-start(bf16[4,64,2304]{2,1,0:T(8,128)(2,1)} %get-tuple-element.50), channel_id=1, source_target_pairs={{0,1},{1,0},{2,3},{3,2},{4,5},{5,4},{6,7},{7,6},{8,9},{9,8},{10,11... | collective-permute-start | bytes 3538952 | tf_op jit(solution)/shard_map/ppermute | solution.py:99
  47.6 20.4 %collective-permute-start.4 = (bf16[640,512]{1,0:T(8,128)(2,1)S(1)}, bf16[640,512]{1,0:T(8,128)(2,1)S(1)}, u32[]{:S(2)}, u32[]{:S(2)}) collective-permute-start(bf16[640,512]{1,0:T(8,128)(2,1)S(1)} %bitcast.299), channel_id=1, source_target_pairs={{0,2},{1,3},{2,0},{3,1},{4,6},{5,7},{6,4},{7,5},{8,10},{9,11},{10,... | collective-permute-start | bytes 1966088 | tf_op jit(solution)/shard_map/ppermute | solution.py:99
  49.1 43.5 %collective-permute-start = (bf16[128,2048]{1,0:T(8,128)(2,1)S(1)}, bf16[128,2048]{1,0:T(8,128)(2,1)}, u32[]{:S(2)}, u32[]{:S(2)}) collective-permute-start(bf16[128,2048]{1,0:T(8,128)(2,1)S(1)} %bitcast.295), channel_id=1, source_target_pairs={{0,8},{1,9},{2,10},{3,11},{4,12},{5,13},{6,14},{7,15},{8,0},{9,1},... | collective-permute-start | bytes 1572872 | tf_op jit(solution)/shard_map/ppermute | solution.py:99
  55.0 18.3 %collective-permute-start.5 = (bf16[640,512]{1,0:T(8,128)(2,1)S(1)}, bf16[640,512]{1,0:T(8,128)(2,1)S(1)}, u32[]{:S(2)}, u32[]{:S(2)}) collective-permute-start(bf16[640,512]{1,0:T(8,128)(2,1)S(1)} %bitcast.300), channel_id=1, source_target_pairs={{0,4},{1,5},{2,6},{3,7},{4,0},{5,1},{6,2},{7,3},{8,12},{9,13},{10,... | collective-permute-start | bytes 1966088 | tf_op jit(solution)/shard_map/ppermute | solution.py:99
  56.1 33.6 %collective-permute-start.6 = (bf16[640,512]{1,0:T(8,128)(2,1)S(1)}, bf16[640,512]{1,0:T(8,128)(2,1)S(1)}, u32[]{:S(2)}, u32[]{:S(2)}) collective-permute-start(bf16[640,512]{1,0:T(8,128)(2,1)S(1)} %bitcast.301), channel_id=1, source_target_pairs={{0,6},{1,7},{2,4},{3,5},{4,2},{5,3},{6,0},{7,1},{8,14},{9,15},{10,... | collective-permute-start | bytes 1966088 | tf_op jit(solution)/shard_map/ppermute | solution.py:99
  57.1 56.7 %collective-permute-start.1 = (bf16[128,2048]{1,0:T(8,128)(2,1)S(1)}, bf16[128,2048]{1,0:T(8,128)(2,1)S(1)}, u32[]{:S(2)}, u32[]{:S(2)}) collective-permute-start(bf16[128,2048]{1,0:T(8,128)(2,1)S(1)} %bitcast.296), channel_id=1, source_target_pairs={{0,16},{1,17},{2,18},{3,19},{4,20},{5,21},{6,22},{7,23},{8,24},{9,... | collective-permute-start | bytes 1572872 | tf_op jit(solution)/shard_map/ppermute | solution.py:99
  68.0 46.6 %collective-permute-start.2 = (bf16[128,2048]{1,0:T(8,128)(2,1)S(1)}, bf16[128,2048]{1,0:T(8,128)(2,1)S(1)}, u32[]{:S(2)}, u32[]{:S(2)}) collective-permute-start(bf16[128,2048]{1,0:T(8,128)(2,1)S(1)} %bitcast.297), channel_id=1, source_target_pairs={{0,24},{1,25},{2,26},{3,27},{4,28},{5,29},{6,30},{7,31},{8,16},{9,... | collective-permute-start | bytes 1572872 | tf_op jit(solution)/shard_map/ppermute | solution.py:99
  115.4 57.6 %all-to-all-start.1 = ((bf16[4,128,1536]{2,1,0:T(8,128)(2,1)}), bf16[4,128,1536]{2,1,0:T(8,128)(2,1)}, u32[]{:S(2)}, u32[]{:S(2)}) async-start(bf16[4,128,1536]{2,1,0:T(8,128)(2,1)} %copy-done.18), calls=%async_computation.1 | async-start | bytes 3145728 | tf_op jit(solution)/shard_map/all_to_all | solution.py:105
  136.6 160.2 %all-gather.6.cloned.1.call-start = ((), (), s32[]{:S(2)}) async-start(), calls=%async_computation.13 | async-start | bytes 7864320 | tf_op jit(solution)/shard_map/all_gather | solution.py:108
  200.2 20.9 %collective-permute-start.8 = (bf16[1024,256]{1,0:T(8,128)(2,1)}, bf16[1024,256]{1,0:T(8,128)(2,1)}, u32[]{:S(2)}, u32[]{:S(2)}) collective-permute-start(bf16[1024,256]{1,0:T(8,128)(2,1)} %pad_maximum_fusion.8), channel_id=1, source_target_pairs={{0,4},{1,5},{2,6},{3,7},{4,0},{5,1},{6,2},{7,3},{8,12},{9,13},{10,... | collective-permute-start | bytes 1572872 | tf_op jit(solution)/shard_map/ppermute | solution.py:99
  205.4 33.1 %all-to-all-start.2 = ((bf16[4,128,768]{2,1,0:T(8,128)(2,1)}), bf16[4,128,768]{2,1,0:T(8,128)(2,1)}, u32[]{:S(2)}, u32[]{:S(2)}) async-start(bf16[4,128,768]{2,1,0:T(8,128)(2,1)} %get-tuple-element.54), calls=%async_computation.2 | async-start | bytes 1572864 | tf_op jit(solution)/shard_map/all_to_all | solution.py:105
  209.7 118.3 %all-gather.8.cloned.1.call-start = ((), (), s32[]{:S(2)}) async-start(), calls=%async_computation.14 | async-start | bytes 3932160 | tf_op jit(solution)/shard_map/all_gather | solution.py:108
  240.8 30.5 %collective-permute-start.11 = (bf16[512,512]{1,0:T(8,128)(2,1)S(1)}, bf16[512,512]{1,0:T(8,128)(2,1)}, u32[]{:S(2)}, u32[]{:S(2)}) collective-permute-start(bf16[512,512]{1,0:T(8,128)(2,1)S(1)} %pad_maximum_fusion.9.refs_0_), channel_id=1, source_target_pairs={{0,8},{1,9},{2,10},{3,11},{4,12},{5,13},{6,14},{7,15},{8,0},{9,1},... | collective-permute-start | bytes 1572872 | tf_op jit(solution)/shard_map/ppermute | solution.py:99
  240.8 43.3 %collective-permute-start.12 = (bf16[512,512]{1,0:T(8,128)(2,1)S(1)}, bf16[512,512]{1,0:T(8,128)(2,1)}, u32[]{:S(2)}, u32[]{:S(2)}) collective-permute-start(bf16[512,512]{1,0:T(8,128)(2,1)S(1)} %pad_maximum_fusion.9.refs_0_), channel_id=1, source_target_pairs={{0,16},{1,17},{2,18},{3,19},{4,20},{5,21},{6,22},{7,23},{8,24},{9,... | collective-permute-start | bytes 1572872 | tf_op jit(solution)/shard_map/ppermute | solution.py:99
  243.9 275.4 %reduce-scatter.7.cloned.1.call-start = ((), (), s32[]{:S(2)}) async-start(), calls=%async_computation.16 | async-start | bytes 11796480 | tf_op jit(solution)/shard_map/reduce_scatter | solution.py:111
  256.2 55.3 %collective-permute-start.15 = (bf16[128,2048]{1,0:T(8,128)(2,1)}, bf16[128,2048]{1,0:T(8,128)(2,1)}, u32[]{:S(2)}, u32[]{:S(2)}) collective-permute-start(bf16[128,2048]{1,0:T(8,128)(2,1)} %shard_map.245.refs_0_), channel_id=1, source_target_pairs={{0,8},{1,9},{2,10},{3,11},{4,12},{5,13},{6,14},{7,15},{8,0},{9,1},... | collective-permute-start | bytes 1572872 | tf_op jit(solution)/shard_map/ppermute | solution.py:99
  262.9 54.8 %collective-permute-start.16 = (bf16[128,2048]{1,0:T(8,128)(2,1)}, bf16[128,2048]{1,0:T(8,128)(2,1)}, u32[]{:S(2)}, u32[]{:S(2)}) collective-permute-start(bf16[128,2048]{1,0:T(8,128)(2,1)} %shard_map.245.refs_0_), channel_id=1, source_target_pairs={{0,16},{1,17},{2,18},{3,19},{4,20},{5,21},{6,22},{7,23},{8,24},{9,... | collective-permute-start | bytes 1572872 | tf_op jit(solution)/shard_map/ppermute | solution.py:99
  262.9 54.8 %collective-permute-start.17 = (bf16[128,2048]{1,0:T(8,128)(2,1)}, bf16[128,2048]{1,0:T(8,128)(2,1)}, u32[]{:S(2)}, u32[]{:S(2)}) collective-permute-start(bf16[128,2048]{1,0:T(8,128)(2,1)} %shard_map.245.refs_0_), channel_id=1, source_target_pairs={{0,24},{1,25},{2,26},{3,27},{4,28},{5,29},{6,30},{7,31},{8,16},{9,... | collective-permute-start | bytes 1572872 | tf_op jit(solution)/shard_map/ppermute | solution.py:99
  296.8 24.5 %collective-permute-start.14 = (bf16[512,2048]{1,0:T(8,128)(2,1)}, bf16[512,2048]{1,0:T(8,128)(2,1)}, u32[]{:S(2)}, u32[]{:S(2)}) collective-permute-start(bf16[512,2048]{1,0:T(8,128)(2,1)} %multiply_convert_fusion.refs_0_), channel_id=1, source_target_pairs={{0,1},{1,0},{2,3},{3,2},{4,5},{5,4},{6,7},{7,6},{8,9},{9,8},{10,11... | collective-permute-start | bytes 6291464 | tf_op jit(solution)/shard_map/ppermute | solution.py:99
  369.4 61.7 %all-to-all-start.3 = ((bf16[4,128,2048]{2,1,0:T(8,128)(2,1)}), bf16[4,128,2048]{2,1,0:T(8,128)(2,1)}, u32[]{:S(2)}, u32[]{:S(2)}) async-start(bf16[4,128,2048]{2,1,0:T(8,128)(2,1)} %bitcast.293), calls=%async_computation.3 | async-start | bytes 4194304 | tf_op jit(solution)/shard_map/all_to_all | solution.py:105
  442.8 30.4 %all-to-all-start.4 = ((bf16[4,128,1024]{2,1,0:T(8,128)(2,1)}), bf16[4,128,1024]{2,1,0:T(8,128)(2,1)}, u32[]{:S(2)}, u32[]{:S(2)}) async-start(bf16[4,128,1024]{2,1,0:T(8,128)(2,1)} %shard_map.252), calls=%async_computation.4 | async-start | bytes 2097152 | tf_op jit(solution)/shard_map/all_to_all | solution.py:105
  447.1 187.9 %reduce-scatter.11.cloned.1.call-start = ((), (), s32[]{:S(2)}) async-start(), calls=%async_computation.18 | async-start | bytes 2359296 | tf_op jit(solution)/shard_map/reduce_scatter | solution.py:111
  519.3 86.3 %all-to-all-start.5 = ((bf16[4,128,2304]{2,1,0:T(8,128)(2,1)}), bf16[4,128,2304]{2,1,0:T(8,128)(2,1)}, u32[]{:S(2)}, u32[]{:S(2)}) async-start(bf16[4,128,2304]{2,1,0:T(8,128)(2,1)} %bitcast.309), calls=%async_computation.7 | async-start | bytes 4718592 | tf_op jit(solution)/shard_map/all_to_all | solution.py:105
  524.0 112.8 %reduce-scatter.5.cloned.1.call-start = ((), (), s32[]{:S(2)}) async-start(), calls=%async_computation.15 | async-start | bytes 2621440 | tf_op jit(solution)/shard_map/reduce_scatter | solution.py:111
  532.2 145.1 %reduce-scatter.9.cloned.1.call-start = ((), (), s32[]{:S(2)}) async-start(), calls=%async_computation.17 | async-start | bytes 2621440 | tf_op jit(solution)/shard_map/reduce_scatter | solution.py:111
  621.5 53.7 %all-to-all-start.6 = ((bf16[4,128,2048]{2,1,0:T(8,128)(2,1)}), bf16[4,128,2048]{2,1,0:T(8,128)(2,1)}, u32[]{:S(2)}, u32[]{:S(2)}) async-start(bf16[4,128,2048]{2,1,0:T(8,128)(2,1)} %bitcast.294), calls=%async_computation.8 | async-start | bytes 4194304 | tf_op jit(solution)/shard_map/all_to_all | solution.py:105
  650.6 30.2 %collective-permute-start.32 = (f32[136]{0:T(256)S(1)}, f32[136]{0:T(256)S(1)}, u32[]{:S(2)}, u32[]{:S(2)}) collective-permute-start(f32[136]{0:T(256)S(1)} %bitcast.333), channel_id=1, source_target_pairs={{0,24},{1,25},{2,26},{3,27},{4,28},{5,29},{6,30},{7,31},{8,16},{9,... | collective-permute-start | bytes 1640 | tf_op jit(solution)/shard_map/ppermute | solution.py:99
  654.3 26.5 %collective-permute-start.31 = (f32[136]{0:T(256)S(1)}, f32[136]{0:T(256)S(1)}, u32[]{:S(2)}, u32[]{:S(2)}) collective-permute-start(f32[136]{0:T(256)S(1)} %bitcast.332), channel_id=1, source_target_pairs={{0,16},{1,17},{2,18},{3,19},{4,20},{5,21},{6,22},{7,23},{8,24},{9,... | collective-permute-start | bytes 1640 | tf_op jit(solution)/shard_map/ppermute | solution.py:99
  654.3 26.5 %collective-permute-start.30 = (f32[136]{0:T(256)S(1)}, f32[136]{0:T(256)S(1)}, u32[]{:S(2)}, u32[]{:S(2)}) collective-permute-start(f32[136]{0:T(256)S(1)} %bitcast.331), channel_id=1, source_target_pairs={{0,8},{1,9},{2,10},{3,11},{4,12},{5,13},{6,14},{7,15},{8,0},{9,1},... | collective-permute-start | bytes 1640 | tf_op jit(solution)/shard_map/ppermute | solution.py:99
  677.3 17.7 %all-to-all-start.7 = ((bf16[4,128,512]{2,1,0:T(8,128)(2,1)}), bf16[4,128,512]{2,1,0:T(8,128)(2,1)S(1)}, u32[]{:S(2)}, u32[]{:S(2)}) async-start(bf16[4,128,512]{2,1,0:T(8,128)(2,1)} %bitcast.317), calls=%async_computation.10 | async-start | bytes 1048576 | tf_op jit(solution)/shard_map/all_to_all | solution.py:105
  (129 other events, 1139.3 us)
Sparse Core Ops, SparseCore 0:
  10.9 120.8 all-gather.3
  173.2 75.5 all-gather.5
  250.6 43.7 all-gather.7
  369.6 103.9 reduce-scatter.6
  514.0 42.2 reduce-scatter.10
  558.5 54.3 reduce-scatter.4
  615.9 34.2 reduce-scatter.8

commit v3 on v2

--- a/solution.py
+++ b/solution.py
@@ -115,8 +115,18 @@
     def deal_a(self, blocks):
         return [blocks[0]] + [self.move(blocks[d], a=d) for d in range(1, self.A)]
 
-    def gather_a(self, array):
-        return self.deal_a([array] * self.A)
+    def gather_a(self, array, own_first=True, then=()):
+        held = {0: array}
+        bit = self.A // 2
+        while bit:
+            own = self.move(array, a=bit)
+            rest = [d for d in held if d]
+            sent = [held[d] for d in rest]
+            sent = after(sent, *((own,) if own_first else then)) if rest else sent
+            held[bit] = own
+            held.update({d | bit: self.move(v, a=bit) for d, v in zip(rest, sent)})
+            bit //= 2
+        return [held[d] for d in range(self.A)]
 
     def ahead(self, array):
         return [
@@ -286,16 +296,6 @@
     return whole_call(body, spot, blocks, [like((parts * rows, n))])[0]
 
 
-def reorder_rows(array, source):
-    rows = array.shape[0] // len(source)
-
-    def body(_, src, dst):
-        for i, at in enumerate(source):
-            dst[i * rows : (i + 1) * rows, :] = src[at * rows : (at + 1) * rows, :]
-
-    return whole_call(body, jnp.zeros((1,), jnp.int32), [array], [like(array.shape)])[0]
-
-
 def stack_with_extra(blocks, where, parts, rows, more):
     n = blocks[0].shape[1]
 
@@ -374,18 +374,26 @@
     steps = min(4, blocks)
     per_step = blocks // steps
 
+    in_turn = [bool(np.array_equal(order, np.arange(blocks))) for order in orders]
+
     def body(order_ref, *refs):
-        for k in range(per_step):
-            at, start = 0, 0
-            for m, (count, n) in enumerate(zip(counts, widths)):
-                place = order_ref[m * blocks + pl.program_id(0) * per_step + k]
-                where = at_multiple(place, unit)
+        at, start = 0, 0
+        for m, (count, n) in enumerate(zip(counts, widths)):
+            first = pl.program_id(0) * per_step
+            if in_turn[m]:
+                places = [at_multiple(pl.program_id(0), per_step * unit)]
+            else:
+                places = [
+                    at_multiple(order_ref[m * blocks + first + k], unit) for k in range(per_step)
+                ]
+            size = per_step * unit // len(places)
+            for k, where in enumerate(places):
                 total = dot_tn(refs[at][:, where], refs[at + count][...])
                 for i in range(1, count):
                     total = total + dot_tn(refs[at + i][:, where], refs[at + count + i][...])
-                refs[-1][k * unit : (k + 1) * unit, start : start + n] = total.astype(bf16)
-                at += 2 * count
-                start += n
+                refs[-1][k * size : (k + 1) * size, start : start + n] = total.astype(bf16)
+            at += 2 * count
+            start += n
 
     flat = [v for lefts, rights in groups for v in (*lefts, *rights)]
     return pl.pallas_call(
@@ -401,30 +409,68 @@
     )(jnp.asarray(np.concatenate(orders), jnp.int32), *flat)
 
 
-def product_t(left, right, rows, add=None):
-    tokens, n = left.shape
-    width = right.shape[0]
-
-    def body(left_ref, right_ref, *refs):
-        made = dot_t(left_ref[...], right_ref[...])
+def product_t(lefts, right, rows, add=None):
+    count = len(lefts)
+    tokens = lefts[0].shape[0]
+    width, n = right.shape
+
+    def body(*refs):
+        right_ref = refs[count]
+        total, start = None, 0
+        for left in refs[:count]:
+            stop = start + left.shape[1]
+            part = dot_t(left[...], right_ref[:, start:stop])
+            total = part if total is None else total + part
+            start = stop
         if add is not None:
-            made = made + refs[0][...].astype(f32)
-        refs[-1][...] = made.astype(refs[-1].dtype)
-
-    ins = [left, right] + ([] if add is None else [add])
+            total = total + refs[count + 1][...].astype(f32)
+        refs[-1][...] = total.astype(bf16)
+
     block = pl.BlockSpec((tokens, rows), lambda i: (0, i))
     return pl.pallas_call(
         body,
         grid=(width // rows,),
-        in_specs=[
-            pl.BlockSpec((tokens, n), lambda i: (0, 0)),
-            pl.BlockSpec((rows, n), lambda i: (i, 0)),
-        ]
+        in_specs=[pl.BlockSpec(left.shape, lambda i: (0, 0)) for left in lefts]
+        + [pl.BlockSpec((rows, n), lambda i: (i, 0))]
         + ([] if add is None else [block]),
         out_specs=block,
         out_shape=like((tokens, width)),
         compiler_params=pltpu.CompilerParams(vmem_limit_bytes=VMEM_BYTES),
-    )(*ins)
+    )(*lefts, right, *([] if add is None else [add]))
+
+
+def feed_forward(normed, gate_up, dout, down):
+    tokens, width = normed.shape
+    units = down.shape[1]
+    cols = 256
+    steps = units // cols
+
+    def body(normed_ref, gate_ref, up_ref, dout_ref, down_ref, inner_ref, d_gate_ref, d_up_ref):
+        gate = dot(normed_ref[...], gate_ref[...])
+        up = dot(normed_ref[...], up_ref[...])
+        d_inner = dot(dout_ref[...], down_ref[...])
+        s = jax.nn.sigmoid(gate)
+        act = gate * s
+        inner_ref[...] = (act * up).astype(bf16)
+        d_gate_ref[...] = (d_inner * up * s * (1.0 + gate * (1.0 - s))).astype(bf16)
+        d_up_ref[...] = (d_inner * act).astype(bf16)
+
+    rows = pl.BlockSpec((tokens, width), lambda i: (0, 0))
+    block = pl.BlockSpec((tokens, cols), lambda i: (0, i))
+    return pl.pallas_call(
+        body,
+        grid=(steps,),
+        in_specs=[
+            rows,
+            pl.BlockSpec((width, cols), lambda i: (0, i)),
+            pl.BlockSpec((width, cols), lambda i: (0, steps + i)),
+            rows,
+            pl.BlockSpec((width, cols), lambda i: (0, i)),
+        ],
+        out_specs=[block] * 3,
+        out_shape=[like((tokens, units))] * 3,
+        compiler_params=pltpu.CompilerParams(vmem_limit_bytes=ALL_VMEM_BYTES),
+    )(normed, gate_up, gate_up, dout, down)
 
 
 def after(values, *others):
@@ -475,21 +521,19 @@
     ).astype(jnp.int32)
 
     x_own, dout_own = tokens[0], grad_out[0]
-    x_parts = g.gather_a(x_own)
+    x_parts = g.gather_a(x_own, own_first=False)
     out_w = lax.all_gather(w_out, BOTH, axis=0, tiled=True)
-    cuts = cut_columns(
-        [[w_query, key_weight, value_weight], [w_gate, w_up, w_down]], spot, A
-    )
+    (cut,) = cut_columns([[w_query, key_weight, value_weight]], spot, A)
     packed = jnp.concatenate([attn_gain, mlp_gain, qk_gain.reshape(-1)])
     packed = jnp.stack(
         [jnp.pad(v, (0, qkv_cols - v.shape[0])) for v in (packed, block_pos[0].astype(bf16))]
     )
     packed = jnp.pad(packed, ((0, EXTRA - 2), (0, 0)))
-    sent = jnp.concatenate([cuts[0][1].reshape(A * rows_own, qkv_cols), packed])
+    sent = jnp.concatenate([cut[1].reshape(A * rows_own, qkv_cols), packed])
     got = g.swap(sent)
     other_packed = got[A * rows_own :]
     qkv_local = merge_with_extra(
-        cuts[0][0],
+        cut[0],
         got[: A * rows_own].reshape(A, rows_own, qkv_cols),
         [packed, other_packed],
         spot,
@@ -503,8 +547,9 @@
     small = jnp.transpose(small.reshape(2 * A * pieces, 2, -1), (1, 0, 2)).reshape(2, HEAD_SIZE)
     query_gain, key_gain = small[0], small[1]
 
-    gu_local, down_local = merge_rows(cuts[1][0], g.swap(cuts[1][1]), spot, [2 * ff_cols, ff_cols])
-    (gu_local,) = after([gu_local], qkv_w, *x_parts)
+    (cut,) = cut_columns([[w_gate, w_up, w_down]], after([spot], qkv_local)[0], A)
+    gu_local, down_local = merge_rows(cut[0], g.swap(cut[1]), spot, [2 * ff_cols, ff_cols])
+    (gu_local,) = after([gu_local], qkv_piece)
     gu_piece = g.exchange_a(gu_local).reshape(A * unit, 2 * ff_cols)
     (down_local,) = after([down_local], gu_piece)
     down_piece = g.exchange_a(down_local).reshape(A * unit, ff_cols)
@@ -531,7 +576,7 @@
     normed = [normed_own, g.swap(normed_own)]
     made = jnp.concatenate([dot(part, qkv_w) for part in normed], axis=0)
     gu_by = g.gather_by(after([gu_piece], out_w, made)[0])
-    down_w = g.gather_by(down_piece)
+    down_w = g.gather_by(after([down_piece], gu_by)[0])
     q_pre = made[:, :q_cols].reshape(2 * group_rows, GROUP, HEAD_SIZE)
     k_pre = made[:, q_cols : q_cols + HEAD_SIZE]
     value = made[:, q_cols + HEAD_SIZE :].astype(bf16)
@@ -576,32 +621,20 @@
     attended = jnp.concatenate([flat(mixed[0][0]), got], axis=1)
     (attended,) = after([attended], down_piece)
     att_parts = g.gather_a(attended)
-    att_heads = gather_heads(att_parts, spot, q_cols)
+    att_heads = gather_heads(after(att_parts, gu_by), spot, q_cols)
 
     (dout_by,) = permute(after([dout_own], att_parts[-1]), False)
-    dout_parts = g.gather_a(dout_by)
     middle = inputs + dot_t(att_heads, out_w)
+    dout_parts = g.gather_a(dout_by, False, (middle,))
     root2 = inv_rms(middle)
     normed2_own = (middle * root2 * second_gain).astype(bf16)
+    (normed2_own,) = permute([normed2_own], False)
     normed2 = [normed2_own, g.swap(normed2_own)]
-    gu_w = reorder_rows(gu_by, np.arange(R * Y * A).reshape(R * Y, A).T.reshape(-1).tolist())
-    both = [dot(part, gu_w) for part in normed2]
-    dout_group = stack_parts(after(dout_parts, both[0]), spot)
+    dout_group = stack_parts(dout_parts, spot)
     dout = [dout_group, g.swap(dout_group)]
-    d_inner = [dot(part, down_w) for part in dout]
-
-    def feed(n):
-        gate, up = both[n][:, :ff_cols], both[n][:, ff_cols:]
-        s = jax.nn.sigmoid(gate)
-        act = gate * s
-        d_gate = d_inner[n] * up * s * (1.0 + gate * (1.0 - s))
-        return (
-            (act * up).astype(bf16),
-            jnp.concatenate([d_gate, d_inner[n] * act], axis=1).astype(bf16),
-        )
-
-    fed = [feed(0), feed(1)]
-    inner, d_gu = [f[0] for f in fed], [f[1] for f in fed]
+    fed = [feed_forward(normed2[n], gu_by, dout[n], down_w) for n in range(2)]
+    inner = [f[0] for f in fed]
+    d_gu = [f[1:] for f in fed]
 
     def of_both(parts, weight):
         got = g.swap(product_t(parts[1], weight, 512))
@@ -610,11 +643,11 @@
     def own_rows(array):
         return lax.dynamic_slice_in_dim(array, a * token_rows, token_rows, axis=0)
 
-    d_normed2 = of_both(d_gu, gu_w)
-    mlp_gain_grad = jnp.sum(d_normed2 * middle * root2, axis=0)
-    e2 = g.to_rows_owner(d_normed2)
-    middle_own = own_rows(middle)
-    grad_middle = dout_own.astype(f32) + norm_back(middle_own, own_rows(root2), second_gain, e2)
+    d_normed2 = of_both(d_gu, gu_by)
+    (e2,) = permute([g.to_rows_owner(d_normed2)], True)
+    middle_own, root2_own = own_rows(middle), own_rows(root2)
+    mlp_gain_grad = jnp.sum(e2 * middle_own * root2_own, axis=0)
+    grad_middle = dout_own.astype(f32) + norm_back(middle_own, root2_own, second_gain, e2)
 
     by_order = np.arange(R * A * Y).reshape(A, R * Y).T.reshape(-1)
 
@@ -640,9 +673,14 @@
     def core_rows(dealt):
         return dealt.reshape(A, 2, rows_own, -1)
 
-    mlp_grad = over_tokens((after(normed2, d_normed2), d_gu, True), (dout, inner, False))
+    later = after(normed2, d_normed2)
+    mlp_grad = over_tokens(
+        (later, [d[0] for d in d_gu], False),
+        (later, [d[1] for d in d_gu], False),
+        (dout, inner, False),
+    )
     mlp_total = g.scatter("by", mlp_grad)
-    out_part = of_both(after(inner, mlp_grad), down_w)
+    out_part = of_both([[v] for v in after(inner, d_normed2)], down_w)
 
     d_branch = grad_middle.astype(bf16)
     d_att = dot(d_branch, out_w).astype(bf16)
@@ -653,8 +691,7 @@
         dealt = jnp.swapaxes(dealt, 0, 1)
     dealt = g.exchange_a(dealt).reshape(group_rows, -1)
     d_att, rows_of_part = dealt[:, : 2 * q_cols], dealt[:, 2 * q_cols :]
-    (out_part,) = after([out_part], d_att)
-    out_mine = g.scatter("a", out_part)
+    out_mine = g.scatter("a", after([out_part], mlp_total, d_att)[0])
     mlp_dealt = g.exchange_a(after([part_rows(mlp_total)], d_att)[0])
     mine_half, other_half = g.by_core(d_att[:, :q_cols], d_att[:, q_cols:])
     d_att = [mine_half, g.swap(other_half)]
@@ -682,6 +719,7 @@
     for i in range(1, R):
         block = jnp.concatenate([of_sequence(back[1], i) for back in backs], axis=0)
         d_kv = d_kv + g.move(block.astype(bf16), b=-i).astype(f32)
+    (d_kv,) = after([d_kv], mlp_dealt)
     e_q = unrotate(d_query, cosine3, sine3)
     e_k = unrotate(d_kv[:, :HEAD_SIZE], cosine, sine)
     d_q_pre = norm_back(q_pre, q_root, query_gain, e_q).reshape(2 * group_rows, q_cols)
@@ -692,9 +730,9 @@
     d_qkv = jnp.concatenate([d_q_pre, d_k_pre, d_kv[:, HEAD_SIZE:]], axis=1).astype(bf16)
     d_qkv = [of_sequence(d_qkv, 0), of_sequence(d_qkv, 1)]
     qkv_grad = over_tokens((normed, d_qkv, True))
-    d_qkv = after(d_qkv, qkv_grad, mlp_dealt)
-    d_normed = of_both(d_qkv, qkv_w)
-    (out_sum,) = permute([out_mine.astype(f32)], True)
+    d_qkv = after(d_qkv, qkv_grad)
+    d_normed = of_both([[v] for v in d_qkv], qkv_w)
+    (out_sum,) = permute([after([out_mine], d_normed)[0].astype(f32)], True)
     result = (middle_own + out_sum).astype(bf16)
     qkv_total = g.scatter("by", qkv_grad)
     attn_gain_grad = jnp.sum(d_normed * inputs * x_root, axis=0)

time: 718 us -> 653 us (0.909)
  starting transfers between devices: 96.8 us -> 67.8 us
  matrix products: 72.3 us -> 45.4 us
  Pallas kernels: 84.9 us -> 101 us
  waiting for transfers between devices: 308 us -> 293 us
    all_to_all x8, starting transfers between devices: 61.8 us -> 35.2 us  [exchange_a(): lax.all_to_all(array, BOTH, 0, 0, axis_index_groups=self.groups('a'), til...]
    dot_general x7 -> x3, matrix products: 38 us -> 12 us  [dot(): return jnp.dot(left, right, preferred_element_type=f32)]
    all_to_all x8, waiting for transfers between devices: 196 us -> 171 us  [exchange_a(): lax.all_to_all(array, BOTH, 0, 0, axis_index_groups=self.groups('a'), til...]
    pallas_call x6 -> x8, Pallas kernels: 27.4 us -> 48.9 us  [the longest x6 28.3 us: product_t(): pl.pallas_call(body, grid=(width // rows,), in_specs=[pl.BlockSpec(left.s...]
    pallas_call x10 -> x11, Pallas kernels: 20.5 us -> 10.4 us  [whole_call(): pl.pallas_call(body, grid_spec=pltpu.PrefetchScalarGridSpec(num_scalar_pr...]
    unnamed x232 -> x248, local copies, waits for them, and re-layouts: 27.2 us -> 23.8 us
  transfers between devices with their start and end apart: 48 -> 48, of which waited for: 19 -> 19; matrix products, arithmetic and copies ran while one was open for 22% -> 21% of each run, Pallas kernels for 7% -> 9%
where the time goes in v3:
time: 653 us; the launch traced here: 645 us
  waiting for transfers between devices  293 us (45%)
  Pallas kernels  101 us (15%)
  starting transfers between devices  67.8 us (10%)
  local copies, waits for them, and re-layouts  56.2 us (9%)
  other arithmetic  54.9 us (8%)
  matrix products  45.4 us (7%)
  between operations  27.2 us (4%)
    all_to_all x8, waiting for transfers between devices, exchange_a(): lax.all_to_all(array, BOTH, 0, 0, axis_index_groups=self.groups('a'), til...  171 us
    ppermute x33, waiting for transfers between devices, move(): return lax.ppermute(array, BOTH, route)  115 us
    all_to_all x8, starting transfers between devices, exchange_a(): lax.all_to_all(array, BOTH, 0, 0, axis_index_groups=self.groups('a'), til...  35.2 us
    ppermute x33, starting transfers between devices, move(): return lax.ppermute(array, BOTH, route)  31.8 us
    pallas_call x6, Pallas kernels, product_t(): pl.pallas_call(body, grid=(width // rows,), in_specs=[pl.BlockSpec(left.s...  28.3 us
    unnamed x248, local copies, waits for them, and re-layouts  23.8 us
    pallas_call x2, Pallas kernels, token_products(): pl.pallas_call(body, grid_spec=pltpu.PrefetchScalarGridSpec(num_scalar_pr...  23.7 us
    pallas_call x2, Pallas kernels, feed_forward(): pl.pallas_call(body, grid=(steps,), in_specs=[rows, pl.BlockSpec((width,...  20.6 us
  transfers between devices with their start and end apart: 48, of which 19 were waited for; matrix products, arithmetic and copies ran while one was open for 21% of the time, Pallas kernels for 9%

profile of v3, /device:TPU:0, one launch (start us, length us, event | category | flops | bytes accessed | tf_op | source)
XLA Modules:
  0.0 645.1 jit_solution(11499816877589188485)
XLA Ops:
  31.8 4.7 shard_map.242
  44.0 24.3 %all-to-all-done = bf16[4,160,512]{2,1,0:T(8,128)(2,1)S(1)} async-done(((bf16[4,160,512]{2,1,0:T(8,128)(2,1)}), bf16[4,160,512]{2,1,0:T(8,128)(2,1)S(1)}, u32[]{:S(2)}, u32[]{:S(2)}) %all-to-all-start) | async-done | bytes 655392 | tf_op jit(solution)/shard_map/all_to_all | solution.py:105
  68.3 4.4 all-to-all-start.1
  85.7 46.7 %collective-permute-done.2.refs_3_ = bf16[128,2048]{1,0:T(8,128)(2,1)S(1)} collective-permute-done((bf16[128,2048]{1,0:T(8,128)(2,1)S(1)}, bf16[128,2048]{1,0:T(8,128)(2,1)S(1)}, u32[]{:S(2)}, u32[]{:S(2)}) %collective-permute-start.2) | collective-permute-done | bytes 524320 | tf_op jit(solution)/shard_map/ppermute | solution.py:99
  147.3 4.2 all-to-all-start.2
  173.6 5.9 collective-permute-done.8
  198.5 21.3 %collective-permute-done.11.refs_1_ = bf16[512,512]{1,0:T(8,128)(2,1)S(1)} collective-permute-done((bf16[512,512]{1,0:T(8,128)(2,1)S(1)}, bf16[512,512]{1,0:T(8,128)(2,1)S(1)}, u32[]{:S(2)}, u32[]{:S(2)}) %collective-permute-start.11) | collective-permute-done | bytes 524320 | tf_op jit(solution)/shard_map/ppermute | solution.py:99
  225.7 9.1 %collective-permute-done.13.refs_3_ = bf16[512,512]{1,0:T(8,128)(2,1)} collective-permute-done((bf16[512,512]{1,0:T(8,128)(2,1)}, bf16[512,512]{1,0:T(8,128)(2,1)}, u32[]{:S(2)}, u32[]{:S(2)}) %collective-permute-start.13) | collective-permute-done | bytes 524320 | tf_op jit(solution)/shard_map/ppermute | solution.py:99
  242.2 7.9 %multiply_reduce_fusion = (f32[512]{0:T(512)S(1)}, f32[512,2048]{1,0:T(8,128)S(1)}) fusion(bf16[512,2048]{1,0:T(8,128)(2,1)S(1)} %shard_map.244, bf16[2048,2048]{1,0:T(8,128)(2,1)} %all-gather.4.cloned.1.call-done, bf16[512,2048]{1,0:T(8,128)(2,1)S(1)} %shard_map.238), kind=kOutput, calls=%fused_computation.20 | convolution fusion | flops 4299161088 | bytes 16779264 | tf_op jit(solution)/shard_map/dot_general | solution.py:35
  250.1 9.3 %collective-permute-done.15.refs_2_ = bf16[128,2048]{1,0:T(8,128)(2,1)S(1)} collective-permute-done((bf16[128,2048]{1,0:T(8,128)(2,1)S(1)}, bf16[128,2048]{1,0:T(8,128)(2,1)S(1)}, u32[]{:S(2)}, u32[]{:S(2)}) %collective-permute-start.15) | collective-permute-done | bytes 524320 | tf_op jit(solution)/shard_map/ppermute | solution.py:99
  261.6 10.6 %collective-permute-done.16.refs_3_ = bf16[128,2048]{1,0:T(8,128)(2,1)S(1)} collective-permute-done((bf16[128,2048]{1,0:T(8,128)(2,1)S(1)}, bf16[128,2048]{1,0:T(8,128)(2,1)S(1)}, u32[]{:S(2)}, u32[]{:S(2)}) %collective-permute-start.16) | collective-permute-done | bytes 524320 | tf_op jit(solution)/shard_map/ppermute | solution.py:99
  277.2 10.4 %shard_map.249 = (bf16[512,768]{1,0:T(8,128)(2,1)}, bf16[512,768]{1,0:T(8,128)(2,1)}, bf16[512,768]{1,0:T(8,128)(2,1)}) custom-call(bf16[512,2048]{1,0:T(8,128)(2,1)} %copy-done.37, bf16[2048,1536]{1,0:T(8,128)(2,1)} %all-gather.6.cloned.1.call-done.gate_ref.up_ref.refs_2_, bf16[2048,1536]{1,0:T(8,128)(2,1)} %all-gather.6.cloned.1.call-done.gate_ref.up_ref.refs_2_, ...), custom_call_target="tpu_custom_call" | custom-call | tf_op jit(solution)/shard_map/pallas_call | solution.py:460
  289.8 6.0 shard_map.250
  296.1 10.3 %shard_map.248 = (bf16[512,768]{1,0:T(8,128)(2,1)}, bf16[512,768]{1,0:T(8,128)(2,1)}, bf16[512,768]{1,0:T(8,128)(2,1)}) custom-call(bf16[512,2048]{1,0:T(8,128)(2,1)} %copy-done.1, bf16[2048,1536]{1,0:T(8,128)(2,1)} %all-gather.6.cloned.1.call-done.gate_ref.up_ref.refs_2_, bf16[2048,1536]{1,0:T(8,128)(2,1)} %all-gather.6.cloned.1.call-done.gate_ref.up_ref.refs_2_, ...), custom_call_target="tpu_custom_call" | custom-call | tf_op jit(solution)/shard_map/pallas_call | solution.py:460
  308.7 6.5 %shard_map.251 = bf16[512,2048]{1,0:T(8,128)(2,1)S(1)} custom-call(bf16[512,768]{1,0:T(8,128)(2,1)S(1)} %copy-done.15, bf16[512,768]{1,0:T(8,128)(2,1)S(1)} %copy-done.17, bf16[2048,1536]{1,0:T(8,128)(2,1)} %all-gather.6.cloned.1.call-done.gate_ref.up_ref.refs_2_, bf16[512,2048]{1,0:T(8,128)(2,1)} %collective-permute-done.19.refs_3_), custom_call_target="tpu_custom_call" | custom-call | tf_op jit(solution)/shard_map/pallas_call | solution.py:430
  316.5 17.6 %shard_map.254 = bf16[2048,2304]{1,0:T(8,128)(2,1)} custom-call(s32[48]{0:T(128)S(1)} %copy-done.33, bf16[512,2048]{1,0:T(8,128)(2,1)} %copy-done.1, bf16[512,2048]{1,0:T(8,128)(2,1)} %copy-done.37, bf16[512,768]{1,0:T(8,128)(2,1)S(1)} %copy-done.16, bf16[512,768]{1,0:T(8,128)(2,1)S(1)} %copy-done.12, bf16[512,2048]{1,0:T(8,128)(2,1)} %copy-done.1, ...), custom_call_target="tpu_custom_call" | custom-call | tf_op jit(solution)/shard_map/pallas_call | solution.py:399
  334.1 6.3 all-to-all-start.3
  346.8 42.5 %all-to-all-done.3 = bf16[4,128,2048]{2,1,0:T(8,128)(2,1)} async-done(((bf16[4,128,2048]{2,1,0:T(8,128)(2,1)}), bf16[4,128,2048]{2,1,0:T(8,128)(2,1)}, u32[]{:S(2)}, u32[]{:S(2)}) %all-to-all-start.3) | async-done | bytes 2097184 | tf_op jit(solution)/shard_map/all_to_all | solution.py:105
  394.5 4.8 convolution_convert_fusion.1.refs_0_
  400.4 4.2 all-to-all-start.4
  408.5 5.5 shard_map.253
  414.0 16.2 %all-to-all-done.4 = bf16[4,128,1024]{2,1,0:T(8,128)(2,1)} async-done(((bf16[4,128,1024]{2,1,0:T(8,128)(2,1)}), bf16[4,128,1024]{2,1,0:T(8,128)(2,1)}, u32[]{:S(2)}, u32[]{:S(2)}) %all-to-all-start.4) | async-done | bytes 1048608 | tf_op jit(solution)/shard_map/all_to_all | solution.py:105
  443.0 4.6 all-to-all-start.5
  472.1 64.1 %all-to-all-done.5 = bf16[4,128,2304]{2,1,0:T(8,128)(2,1)} async-done(((bf16[4,128,2304]{2,1,0:T(8,128)(2,1)}), bf16[4,128,2304]{2,1,0:T(8,128)(2,1)}, u32[]{:S(2)}, u32[]{:S(2)}) %all-to-all-start.5) | async-done | bytes 2359328 | tf_op jit(solution)/shard_map/all_to_all | solution.py:105
  539.9 6.0 shard_map.257
  554.9 4.7 shard_map.259
  559.7 4.4 all-to-all-start.6
  564.5 4.2 convolution_convert_fusion
  575.4 6.3 shard_map.262
  594.3 18.7 %all-to-all-done.6 = bf16[4,128,2048]{2,1,0:T(8,128)(2,1)} async-done(((bf16[4,128,2048]{2,1,0:T(8,128)(2,1)}), bf16[4,128,2048]{2,1,0:T(8,128)(2,1)}, u32[]{:S(2)}, u32[]{:S(2)}) %all-to-all-start.6) | async-done | bytes 2097184 | tf_op jit(solution)/shard_map/all_to_all | solution.py:105
  619.9 5.4 reduce-scatter.11.cloned.1.call-done
  627.2 5.7 all-to-all-done.7
  (520 shorter events, 214.9 us)
Async XLA Ops:
  7.2 131.6 %all-gather.4.cloned.1.call-start = ((), (), s32[]{:S(2)}) async-start(), calls=%async_computation.12 | async-start | bytes 8650752 | tf_op jit(solution)/shard_map/all_gather | solution.py:525
  7.9 68.2 %collective-permute-start.1 = (bf16[128,2048]{1,0:T(8,128)(2,1)}, bf16[128,2048]{1,0:T(8,128)(2,1)S(1)}, u32[]{:S(2)}, u32[]{:S(2)}) collective-permute-start(bf16[128,2048]{1,0:T(8,128)(2,1)} %bitcast.281), channel_id=1, source_target_pairs={{0,16},{1,17},{2,18},{3,19},{4,20},{5,21},{6,22},{7,23},{8,24},{9,... | collective-permute-start | bytes 1572872 | tf_op jit(solution)/shard_map/ppermute | solution.py:99
  12.0 73.7 %collective-permute-start = (bf16[128,2048]{1,0:T(8,128)(2,1)}, bf16[128,2048]{1,0:T(8,128)(2,1)}, u32[]{:S(2)}, u32[]{:S(2)}) collective-permute-start(bf16[128,2048]{1,0:T(8,128)(2,1)} %bitcast.282), channel_id=1, source_target_pairs={{0,8},{1,9},{2,10},{3,11},{4,12},{5,13},{6,14},{7,15},{8,0},{9,1},... | collective-permute-start | bytes 1572872 | tf_op jit(solution)/shard_map/ppermute | solution.py:99
  37.0 31.3 %all-to-all-start = ((bf16[4,160,512]{2,1,0:T(8,128)(2,1)}), bf16[4,160,512]{2,1,0:T(8,128)(2,1)S(1)}, u32[]{:S(2)}, u32[]{:S(2)}) async-start(bf16[4,160,512]{2,1,0:T(8,128)(2,1)} %shard_map.240), calls=%async_computation | async-start | bytes 1310720 | tf_op jit(solution)/shard_map/all_to_all | solution.py:105
  68.3 70.5 %all-to-all-start.1 = ((bf16[4,128,1536]{2,1,0:T(8,128)(2,1)}), bf16[4,128,1536]{2,1,0:T(8,128)(2,1)}, u32[]{:S(2)}, u32[]{:S(2)}) async-start(bf16[4,128,1536]{2,1,0:T(8,128)(2,1)} %get-tuple-element.66), calls=%async_computation.1 | async-start | bytes 3145728 | tf_op jit(solution)/shard_map/all_to_all | solution.py:105
  72.7 150.1 %all-gather.6.cloned.1.call-start = ((), (), s32[]{:S(2)}) async-start(), calls=%async_computation.13 | async-start | bytes 7864320 | tf_op jit(solution)/shard_map/all_gather | solution.py:108
  76.1 56.3 %collective-permute-start.2 = (bf16[128,2048]{1,0:T(8,128)(2,1)S(1)}, bf16[128,2048]{1,0:T(8,128)(2,1)S(1)}, u32[]{:S(2)}, u32[]{:S(2)}) collective-permute-start(bf16[128,2048]{1,0:T(8,128)(2,1)S(1)} %collective-permute-done.1.refs_2_), channel_id=1, source_target_pairs={{0,8},{1,9},{2,10},{3,11},{4,12},{5,13},{6,14},{7,15},{8,0},{9,1},... | collective-permute-start | bytes 1572872 | tf_op jit(solution)/shard_map/ppermute | solution.py:99
  78.9 56.8 %collective-permute-start.4 = (bf16[640,512]{1,0:T(8,128)(2,1)S(1)}, bf16[640,512]{1,0:T(8,128)(2,1)S(1)}, u32[]{:S(2)}, u32[]{:S(2)}) collective-permute-start(bf16[640,512]{1,0:T(8,128)(2,1)S(1)} %bitcast.284), channel_id=1, source_target_pairs={{0,2},{1,3},{2,0},{3,1},{4,6},{5,7},{6,4},{7,5},{8,10},{9,11},{10,... | collective-permute-start | bytes 1966088 | tf_op jit(solution)/shard_map/ppermute | solution.py:99
  80.5 55.2 %collective-permute-start.5 = (bf16[640,512]{1,0:T(8,128)(2,1)S(1)}, bf16[640,512]{1,0:T(8,128)(2,1)S(1)}, u32[]{:S(2)}, u32[]{:S(2)}) collective-permute-start(bf16[640,512]{1,0:T(8,128)(2,1)S(1)} %bitcast.285), channel_id=1, source_target_pairs={{0,4},{1,5},{2,6},{3,7},{4,0},{5,1},{6,2},{7,3},{8,12},{9,13},{10,... | collective-permute-start | bytes 1966088 | tf_op jit(solution)/shard_map/ppermute | solution.py:99
  82.0 53.7 %collective-permute-start.6 = (bf16[640,512]{1,0:T(8,128)(2,1)S(1)}, bf16[640,512]{1,0:T(8,128)(2,1)S(1)}, u32[]{:S(2)}, u32[]{:S(2)}) collective-permute-start(bf16[640,512]{1,0:T(8,128)(2,1)S(1)} %bitcast.286), channel_id=1, source_target_pairs={{0,6},{1,7},{2,4},{3,5},{4,2},{5,3},{6,0},{7,1},{8,14},{9,15},{10,... | collective-permute-start | bytes 1966088 | tf_op jit(solution)/shard_map/ppermute | solution.py:99
  147.3 47.1 %all-to-all-start.2 = ((bf16[4,128,768]{2,1,0:T(8,128)(2,1)}), bf16[4,128,768]{2,1,0:T(8,128)(2,1)}, u32[]{:S(2)}, u32[]{:S(2)}) async-start(bf16[4,128,768]{2,1,0:T(8,128)(2,1)} %get-tuple-element.67), calls=%async_computation.2 | async-start | bytes 1572864 | tf_op jit(solution)/shard_map/all_to_all | solution.py:105
  151.6 125.6 %all-gather.8.cloned.1.call-start = ((), (), s32[]{:S(2)}) async-start(), calls=%async_computation.14 | async-start | bytes 3932160 | tf_op jit(solution)/shard_map/all_gather | solution.py:108
  161.4 18.1 %collective-permute-start.8 = (bf16[1024,256]{1,0:T(8,128)(2,1)}, bf16[1024,256]{1,0:T(8,128)(2,1)}, u32[]{:S(2)}, u32[]{:S(2)}) collective-permute-start(bf16[1024,256]{1,0:T(8,128)(2,1)} %pad_maximum_fusion.6), channel_id=1, source_target_pairs={{0,4},{1,5},{2,6},{3,7},{4,0},{5,1},{6,2},{7,3},{8,12},{9,13},{10,... | collective-permute-start | bytes 1572872 | tf_op jit(solution)/shard_map/ppermute | solution.py:99
  194.5 25.4 %collective-permute-start.11 = (bf16[512,512]{1,0:T(8,128)(2,1)S(1)}, bf16[512,512]{1,0:T(8,128)(2,1)S(1)}, u32[]{:S(2)}, u32[]{:S(2)}) collective-permute-start(bf16[512,512]{1,0:T(8,128)(2,1)S(1)} %pad_maximum_fusion.7.refs_0_), channel_id=1, source_target_pairs={{0,8},{1,9},{2,10},{3,11},{4,12},{5,13},{6,14},{7,15},{8,0},{9,1},... | collective-permute-start | bytes 1572872 | tf_op jit(solution)/shard_map/ppermute | solution.py:99
  196.1 26.3 %collective-permute-start.12 = (bf16[512,512]{1,0:T(8,128)(2,1)S(1)}, bf16[512,512]{1,0:T(8,128)(2,1)}, u32[]{:S(2)}, u32[]{:S(2)}) collective-permute-start(bf16[512,512]{1,0:T(8,128)(2,1)S(1)} %pad_maximum_fusion.7.refs_0_), channel_id=1, source_target_pairs={{0,16},{1,17},{2,18},{3,19},{4,20},{5,21},{6,22},{7,23},{8,24},{9,... | collective-permute-start | bytes 1572872 | tf_op jit(solution)/shard_map/ppermute | solution.py:99
  222.8 220.2 %reduce-scatter.5.cloned.1.call-start = ((), (), s32[]{:S(2)}) async-start(), calls=%async_computation.15 | async-start | bytes 11796480 | tf_op jit(solution)/shard_map/reduce_scatter | solution.py:111
  234.9 24.4 %collective-permute-start.15 = (bf16[128,2048]{1,0:T(8,128)(2,1)S(1)}, bf16[128,2048]{1,0:T(8,128)(2,1)S(1)}, u32[]{:S(2)}, u32[]{:S(2)}) collective-permute-start(bf16[128,2048]{1,0:T(8,128)(2,1)S(1)} %shard_map.246.refs_0_), channel_id=1, source_target_pairs={{0,16},{1,17},{2,18},{3,19},{4,20},{5,21},{6,22},{7,23},{8,24},{9,... | collective-permute-start | bytes 1572872 | tf_op jit(solution)/shard_map/ppermute | solution.py:99
  237.3 24.3 %collective-permute-start.14 = (bf16[128,2048]{1,0:T(8,128)(2,1)S(1)}, bf16[128,2048]{1,0:T(8,128)(2,1)S(1)}, u32[]{:S(2)}, u32[]{:S(2)}) collective-permute-start(bf16[128,2048]{1,0:T(8,128)(2,1)S(1)} %shard_map.246.refs_0_), channel_id=1, source_target_pairs={{0,8},{1,9},{2,10},{3,11},{4,12},{5,13},{6,14},{7,15},{8,0},{9,1},... | collective-permute-start | bytes 1572872 | tf_op jit(solution)/shard_map/ppermute | solution.py:99
  334.1 55.2 %all-to-all-start.3 = ((bf16[4,128,2048]{2,1,0:T(8,128)(2,1)}), bf16[4,128,2048]{2,1,0:T(8,128)(2,1)}, u32[]{:S(2)}, u32[]{:S(2)}) async-start(bf16[4,128,2048]{2,1,0:T(8,128)(2,1)} %bitcast.280), calls=%async_computation.4 | async-start | bytes 4194304 | tf_op jit(solution)/shard_map/all_to_all | solution.py:105
  346.7 61.8 %collective-permute-start.20 = (bf16[512,2048]{1,0:T(8,128)(2,1)}, bf16[512,2048]{1,0:T(8,128)(2,1)S(1)}, u32[]{:S(2)}, u32[]{:S(2)}) collective-permute-start(bf16[512,2048]{1,0:T(8,128)(2,1)} %shard_map.252), channel_id=1, source_target_pairs={{0,1},{1,0},{2,3},{3,2},{4,5},{5,4},{6,7},{7,6},{8,9},{9,8},{10,11... | collective-permute-start | bytes 6291464 | tf_op jit(solution)/shard_map/ppermute | solution.py:99
  400.4 29.8 %all-to-all-start.4 = ((bf16[4,128,1024]{2,1,0:T(8,128)(2,1)}), bf16[4,128,1024]{2,1,0:T(8,128)(2,1)}, u32[]{:S(2)}, u32[]{:S(2)}) async-start(bf16[4,128,1024]{2,1,0:T(8,128)(2,1)} %shard_map.256), calls=%async_computation.5 | async-start | bytes 2097152 | tf_op jit(solution)/shard_map/all_to_all | solution.py:105
  431.4 17.0 %collective-permute-start.21 = (bf16[512,256]{1,0:T(8,128)(2,1)S(1)}, bf16[512,256]{1,0:T(8,128)(2,1)S(1)}, u32[]{:S(2)}, u32[]{:S(2)}) collective-permute-start(bf16[512,256]{1,0:T(8,128)(2,1)S(1)} %get-tuple-element.132), channel_id=1, source_target_pairs={{0,1},{1,0},{2,3},{3,2},{4,5},{5,4},{6,7},{7,6},{8,9},{9,8},{10,11... | collective-permute-start | bytes 786440 | tf_op jit(solution)/shard_map/ppermute | solution.py:99
  443.0 93.2 %all-to-all-start.5 = ((bf16[4,128,2304]{2,1,0:T(8,128)(2,1)}), bf16[4,128,2304]{2,1,0:T(8,128)(2,1)}, u32[]{:S(2)}, u32[]{:S(2)}) async-start(bf16[4,128,2304]{2,1,0:T(8,128)(2,1)} %bitcast.294), calls=%async_computation.7 | async-start | bytes 4718592 | tf_op jit(solution)/shard_map/all_to_all | solution.py:105
  447.6 134.0 %reduce-scatter.7.cloned.1.call-start = ((), (), s32[]{:S(2)}) async-start(), calls=%async_computation.16 | async-start | bytes 2621440 | tf_op jit(solution)/shard_map/reduce_scatter | solution.py:111
  449.3 165.8 %reduce-scatter.9.cloned.1.call-start = ((), (), s32[]{:S(2)}) async-start(), calls=%async_computation.17 | async-start | bytes 2621440 | tf_op jit(solution)/shard_map/reduce_scatter | solution.py:111
  456.3 14.6 %collective-permute-start.22 = (bf16[1024,256]{1,0:T(8,128)(2,1)}, bf16[1024,256]{1,0:T(8,128)(2,1)}, u32[]{:S(2)}, u32[]{:S(2)}) collective-permute-start(bf16[1024,256]{1,0:T(8,128)(2,1)} %pad_maximum_fusion.8), channel_id=1, source_target_pairs={{0,4},{1,5},{2,6},{3,7},{4,0},{5,1},{6,2},{7,3},{8,12},{9,13},{10,... | collective-permute-start | bytes 1572872 | tf_op jit(solution)/shard_map/ppermute | solution.py:99
  559.7 53.4 %all-to-all-start.6 = ((bf16[4,128,2048]{2,1,0:T(8,128)(2,1)}), bf16[4,128,2048]{2,1,0:T(8,128)(2,1)}, u32[]{:S(2)}, u32[]{:S(2)}) async-start(bf16[4,128,2048]{2,1,0:T(8,128)(2,1)} %bitcast.72), calls=%async_computation.8 | async-start | bytes 4194304 | tf_op jit(solution)/shard_map/all_to_all | solution.py:105
  564.1 61.3 %reduce-scatter.11.cloned.1.call-start = ((), (), s32[]{:S(2)}) async-start(), calls=%async_computation.18 | async-start | bytes 2359296 | tf_op jit(solution)/shard_map/reduce_scatter | solution.py:111
  589.9 28.8 %collective-permute-start.30 = (f32[136]{0:T(256)S(1)}, f32[136]{0:T(256)S(1)}, u32[]{:S(2)}, u32[]{:S(2)}) collective-permute-start(f32[136]{0:T(256)S(1)} %bitcast.318), channel_id=1, source_target_pairs={{0,8},{1,9},{2,10},{3,11},{4,12},{5,13},{6,14},{7,15},{8,0},{9,1},... | collective-permute-start | bytes 1640 | tf_op jit(solution)/shard_map/ppermute | solution.py:99
  591.6 27.0 %collective-permute-start.31 = (f32[136]{0:T(256)S(1)}, f32[136]{0:T(256)S(1)}, u32[]{:S(2)}, u32[]{:S(2)}) collective-permute-start(f32[136]{0:T(256)S(1)} %bitcast.317), channel_id=1, source_target_pairs={{0,16},{1,17},{2,18},{3,19},{4,20},{5,21},{6,22},{7,23},{8,24},{9,... | collective-permute-start | bytes 1640 | tf_op jit(solution)/shard_map/ppermute | solution.py:99
  594.0 24.7 %collective-permute-start.32 = (f32[136]{0:T(256)S(1)}, f32[136]{0:T(256)S(1)}, u32[]{:S(2)}, u32[]{:S(2)}) collective-permute-start(f32[136]{0:T(256)S(1)} %bitcast.316), channel_id=1, source_target_pairs={{0,24},{1,25},{2,26},{3,27},{4,28},{5,29},{6,30},{7,31},{8,16},{9,... | collective-permute-start | bytes 1640 | tf_op jit(solution)/shard_map/ppermute | solution.py:99
  615.2 17.7 %all-to-all-start.7 = ((bf16[4,128,512]{2,1,0:T(8,128)(2,1)}), bf16[4,128,512]{2,1,0:T(8,128)(2,1)S(1)}, u32[]{:S(2)}, u32[]{:S(2)}) async-start(bf16[4,128,512]{2,1,0:T(8,128)(2,1)} %bitcast.302), calls=%async_computation.10 | async-start | bytes 1048576 | tf_op jit(solution)/shard_map/all_to_all | solution.py:105
  (137 other events, 1641.8 us)
Sparse Core Ops, SparseCore 0:
  10.9 117.0 all-gather.3
  138.9 73.0 all-gather.5
  222.9 43.2 all-gather.7
  334.3 96.3 reduce-scatter.4
  450.5 78.5 reduce-scatter.6
  547.5 33.3 reduce-scatter.8
  584.1 41.2 reduce-scatter.10

commit v4 on v3

--- a/solution.py
+++ b/solution.py
@@ -691,7 +691,7 @@
         dealt = jnp.swapaxes(dealt, 0, 1)
     dealt = g.exchange_a(dealt).reshape(group_rows, -1)
     d_att, rows_of_part = dealt[:, : 2 * q_cols], dealt[:, 2 * q_cols :]
-    out_mine = g.scatter("a", after([out_part], mlp_total, d_att)[0])
+    wo_total = g.scatter("byc", dot_tn(rows_of_part, att_heads).astype(bf16))
     mlp_dealt = g.exchange_a(after([part_rows(mlp_total)], d_att)[0])
     mine_half, other_half = g.by_core(d_att[:, :q_cols], d_att[:, q_cols:])
     d_att = [mine_half, g.swap(other_half)]
@@ -719,7 +719,7 @@
     for i in range(1, R):
         block = jnp.concatenate([of_sequence(back[1], i) for back in backs], axis=0)
         d_kv = d_kv + g.move(block.astype(bf16), b=-i).astype(f32)
-    (d_kv,) = after([d_kv], mlp_dealt)
+    out_mine = g.scatter("a", after([out_part], mlp_dealt, wo_total, d_kv)[0])
     e_q = unrotate(d_query, cosine3, sine3)
     e_k = unrotate(d_kv[:, :HEAD_SIZE], cosine, sine)
     d_q_pre = norm_back(q_pre, q_root, query_gain, e_q).reshape(2 * group_rows, q_cols)
@@ -729,11 +729,10 @@
     )
     d_qkv = jnp.concatenate([d_q_pre, d_k_pre, d_kv[:, HEAD_SIZE:]], axis=1).astype(bf16)
     d_qkv = [of_sequence(d_qkv, 0), of_sequence(d_qkv, 1)]
+    d_qkv = after(d_qkv, mlp_dealt)
     qkv_grad = over_tokens((normed, d_qkv, True))
     d_qkv = after(d_qkv, qkv_grad)
     d_normed = of_both([[v] for v in d_qkv], qkv_w)
-    (out_sum,) = permute([after([out_mine], d_normed)[0].astype(f32)], True)
-    result = (middle_own + out_sum).astype(bf16)
     qkv_total = g.scatter("by", qkv_grad)
     attn_gain_grad = jnp.sum(d_normed * inputs * x_root, axis=0)
     e1 = g.to_rows_owner(d_normed)
@@ -741,6 +740,8 @@
         x_own.astype(f32), inv_rms(x_own.astype(f32)), first_gain, e1
     )
 
+    (out_sum,) = permute([out_mine.astype(f32)], True)
+    result = (middle_own + out_sum).astype(bf16)
     (qkv_total,) = after([qkv_total], e1)
     dealt = core_rows(g.exchange_a(part_rows(qkv_total)))
     grad_wq, grad_wk, grad_wv = to_owner(dealt, [q_cols, HEAD_SIZE, HEAD_SIZE])
@@ -768,8 +769,7 @@
         sums[2 * rows_own :].reshape(2, -1),
     ]
 
-    (rows_of_part,) = after([rows_of_part], d_kv)
-    grad_wo = g.scatter("byc", dot_tn(rows_of_part, att_heads).astype(bf16)).astype(f32)
+    grad_wo = wo_total.astype(f32)
     grad_wg, grad_wu, grad_wd = to_owner(core_rows(mlp_dealt), [ff_cols] * 3)
     return (
         result[None],

time: 653 us -> 632 us (0.968)
  waiting for transfers between devices: 293 us -> 271 us
    all_to_all x8, waiting for transfers between devices: 171 us -> 122 us  [exchange_a(): lax.all_to_all(array, BOTH, 0, 0, axis_index_groups=self.groups('a'), til...]
    ppermute x33, waiting for transfers between devices: 115 us -> 146 us  [move(): return lax.ppermute(array, BOTH, route)]
    unnamed x248 -> x234, local copies, waits for them, and re-layouts: 23.8 us -> 24.7 us
  transfers between devices with their start and end apart: 48 -> 48, of which waited for: 19 -> 22; matrix products, arithmetic and copies ran while one was open for 21% -> 21% of each run, Pallas kernels for 9% -> 9%
where the time goes in v4:
time: 632 us; the launch traced here: 624 us
  waiting for transfers between devices  271 us (43%)
  Pallas kernels  101 us (16%)
  starting transfers between devices  67.7 us (11%)
  other arithmetic  55.3 us (9%)
  local copies, waits for them, and re-layouts  53.6 us (8%)
  matrix products  47.8 us (8%)
  between operations  27.2 us (4%)
    ppermute x33, waiting for transfers between devices, move(): return lax.ppermute(array, BOTH, route)  146 us
    all_to_all x8, waiting for transfers between devices, exchange_a(): lax.all_to_all(array, BOTH, 0, 0, axis_index_groups=self.groups('a'), til...  122 us
    all_to_all x8, starting transfers between devices, exchange_a(): lax.all_to_all(array, BOTH, 0, 0, axis_index_groups=self.groups('a'), til...  35.7 us
    ppermute x33, starting transfers between devices, move(): return lax.ppermute(array, BOTH, route)  31.7 us
    pallas_call x6, Pallas kernels, product_t(): pl.pallas_call(body, grid=(width // rows,), in_specs=[pl.BlockSpec(left.s...  29.3 us
    unnamed x234, local copies, waits for them, and re-layouts  24.7 us
    pallas_call x2, Pallas kernels, token_products(): pl.pallas_call(body, grid_spec=pltpu.PrefetchScalarGridSpec(num_scalar_pr...  23.7 us
    pallas_call x2, Pallas kernels, feed_forward(): pl.pallas_call(body, grid=(steps,), in_specs=[rows, pl.BlockSpec((width,...  20.6 us
  transfers between devices with their start and end apart: 48, of which 22 were waited for; matrix products, arithmetic and copies ran while one was open for 21% of the time, Pallas kernels for 9%

profile of v4, /device:TPU:0, one launch (start us, length us, event | category | flops | bytes accessed | tf_op | source)
XLA Modules:
  0.0 623.7 jit_solution(8910919614030657925)
XLA Ops:
  31.8 4.7 shard_map.242
  44.0 24.3 %all-to-all-done = bf16[4,160,512]{2,1,0:T(8,128)(2,1)S(1)} async-done(((bf16[4,160,512]{2,1,0:T(8,128)(2,1)}), bf16[4,160,512]{2,1,0:T(8,128)(2,1)S(1)}, u32[]{:S(2)}, u32[]{:S(2)}) %all-to-all-start) | async-done | bytes 655392 | tf_op jit(solution)/shard_map/all_to_all | solution.py:105
  68.3 4.4 all-to-all-start.1
  85.7 46.7 %collective-permute-done.2.refs_3_ = bf16[128,2048]{1,0:T(8,128)(2,1)S(1)} collective-permute-done((bf16[128,2048]{1,0:T(8,128)(2,1)S(1)}, bf16[128,2048]{1,0:T(8,128)(2,1)S(1)}, u32[]{:S(2)}, u32[]{:S(2)}) %collective-permute-start.2) | collective-permute-done | bytes 524320 | tf_op jit(solution)/shard_map/ppermute | solution.py:99
  173.7 5.8 collective-permute-done.8
  198.7 21.3 %collective-permute-done.11.refs_1_ = bf16[512,512]{1,0:T(8,128)(2,1)S(1)} collective-permute-done((bf16[512,512]{1,0:T(8,128)(2,1)S(1)}, bf16[512,512]{1,0:T(8,128)(2,1)S(1)}, u32[]{:S(2)}, u32[]{:S(2)}) %collective-permute-start.11) | collective-permute-done | bytes 524320 | tf_op jit(solution)/shard_map/ppermute | solution.py:99
  223.1 11.8 %collective-permute-done.13.refs_3_ = bf16[512,512]{1,0:T(8,128)(2,1)} collective-permute-done((bf16[512,512]{1,0:T(8,128)(2,1)}, bf16[512,512]{1,0:T(8,128)(2,1)}, u32[]{:S(2)}, u32[]{:S(2)}) %collective-permute-start.13) | collective-permute-done | bytes 524320 | tf_op jit(solution)/shard_map/ppermute | solution.py:99
  242.3 7.9 %multiply_reduce_fusion = (f32[512]{0:T(512)S(1)}, f32[512,2048]{1,0:T(8,128)S(1)}) fusion(bf16[512,2048]{1,0:T(8,128)(2,1)S(1)} %shard_map.244, bf16[2048,2048]{1,0:T(8,128)(2,1)} %all-gather.4.cloned.1.call-done, bf16[512,2048]{1,0:T(8,128)(2,1)S(1)} %shard_map.238), kind=kOutput, calls=%fused_computation.20 | convolution fusion | flops 4299161088 | bytes 16779264 | tf_op jit(solution)/shard_map/dot_general | solution.py:35
  250.2 9.3 %collective-permute-done.15.refs_2_ = bf16[128,2048]{1,0:T(8,128)(2,1)S(1)} collective-permute-done((bf16[128,2048]{1,0:T(8,128)(2,1)S(1)}, bf16[128,2048]{1,0:T(8,128)(2,1)S(1)}, u32[]{:S(2)}, u32[]{:S(2)}) %collective-permute-start.15) | collective-permute-done | bytes 524320 | tf_op jit(solution)/shard_map/ppermute | solution.py:99
  261.1 11.1 %collective-permute-done.16.refs_3_ = bf16[128,2048]{1,0:T(8,128)(2,1)S(1)} collective-permute-done((bf16[128,2048]{1,0:T(8,128)(2,1)S(1)}, bf16[128,2048]{1,0:T(8,128)(2,1)S(1)}, u32[]{:S(2)}, u32[]{:S(2)}) %collective-permute-start.16) | collective-permute-done | bytes 524320 | tf_op jit(solution)/shard_map/ppermute | solution.py:99
  277.3 10.3 %shard_map.249 = (bf16[512,768]{1,0:T(8,128)(2,1)}, bf16[512,768]{1,0:T(8,128)(2,1)}, bf16[512,768]{1,0:T(8,128)(2,1)}) custom-call(bf16[512,2048]{1,0:T(8,128)(2,1)} %copy-done.38, bf16[2048,1536]{1,0:T(8,128)(2,1)} %all-gather.6.cloned.1.call-done.gate_ref.up_ref.refs_2_, bf16[2048,1536]{1,0:T(8,128)(2,1)} %all-gather.6.cloned.1.call-done.gate_ref.up_ref.refs_2_, ...), custom_call_target="tpu_custom_call" | custom-call | tf_op jit(solution)/shard_map/pallas_call | solution.py:460
  290.0 6.0 shard_map.250
  296.2 10.3 %shard_map.248 = (bf16[512,768]{1,0:T(8,128)(2,1)}, bf16[512,768]{1,0:T(8,128)(2,1)}, bf16[512,768]{1,0:T(8,128)(2,1)}) custom-call(bf16[512,2048]{1,0:T(8,128)(2,1)} %copy-done.1, bf16[2048,1536]{1,0:T(8,128)(2,1)} %all-gather.6.cloned.1.call-done.gate_ref.up_ref.refs_2_, bf16[2048,1536]{1,0:T(8,128)(2,1)} %all-gather.6.cloned.1.call-done.gate_ref.up_ref.refs_2_, ...), custom_call_target="tpu_custom_call" | custom-call | tf_op jit(solution)/shard_map/pallas_call | solution.py:460
  308.8 7.4 %shard_map.251 = bf16[512,2048]{1,0:T(8,128)(2,1)} custom-call(bf16[512,768]{1,0:T(8,128)(2,1)S(1)} %copy-done.17, bf16[512,768]{1,0:T(8,128)(2,1)S(1)} %copy-done.19, bf16[2048,1536]{1,0:T(8,128)(2,1)} %all-gather.6.cloned.1.call-done.gate_ref.up_ref.refs_2_, bf16[512,2048]{1,0:T(8,128)(2,1)} %collective-permute-done.19.refs_3_), custom_call_target="tpu_custom_call" | custom-call | tf_op jit(solution)/shard_map/pallas_call | solution.py:430
  316.3 17.7 %shard_map.254 = bf16[2048,2304]{1,0:T(8,128)(2,1)} custom-call(s32[48]{0:T(128)S(1)} %copy-done.34, bf16[512,2048]{1,0:T(8,128)(2,1)} %copy-done.1, bf16[512,2048]{1,0:T(8,128)(2,1)} %copy-done.38, bf16[512,768]{1,0:T(8,128)(2,1)S(1)} %copy-done.18, bf16[512,768]{1,0:T(8,128)(2,1)S(1)} %copy-done.14, bf16[512,2048]{1,0:T(8,128)(2,1)} %copy-done.1, ...), custom_call_target="tpu_custom_call" | custom-call | tf_op jit(solution)/shard_map/pallas_call | solution.py:399
  334.0 6.1 all-to-all-start.4
  340.1 48.6 %all-to-all-done.4 = bf16[4,128,2048]{2,1,0:T(8,128)(2,1)S(1)} async-done(((bf16[4,128,2048]{2,1,0:T(8,128)(2,1)}), bf16[4,128,2048]{2,1,0:T(8,128)(2,1)S(1)}, u32[]{:S(2)}, u32[]{:S(2)}) %all-to-all-start.4) | async-done | bytes 2097184 | tf_op jit(solution)/shard_map/all_to_all | solution.py:105
  393.3 4.8 convolution_convert_fusion.1.refs_0_
  399.2 4.5 all-to-all-start.5
  409.0 19.9 %all-to-all-done.5 = bf16[4,128,1024]{2,1,0:T(8,128)(2,1)} async-done(((bf16[4,128,1024]{2,1,0:T(8,128)(2,1)}), bf16[4,128,1024]{2,1,0:T(8,128)(2,1)}, u32[]{:S(2)}, u32[]{:S(2)}) %all-to-all-start.5) | async-done | bytes 1048608 | tf_op jit(solution)/shard_map/all_to_all | solution.py:105
  432.1 4.5 convolution_convert_fusion
  436.6 4.7 all-to-all-start.3
  461.3 5.6 shard_map.253
  469.2 6.5 %collective-permute-done.22 = bf16[1024,256]{1,0:T(8,128)(2,1)} collective-permute-done((bf16[1024,256]{1,0:T(8,128)(2,1)}, bf16[1024,256]{1,0:T(8,128)(2,1)}, u32[]{:S(2)}, u32[]{:S(2)}) %collective-permute-start.22) | collective-permute-done | bytes 524320 | tf_op jit(solution)/shard_map/ppermute | solution.py:99
  478.9 17.2 %all-to-all-done.3 = bf16[4,128,2304]{2,1,0:T(8,128)(2,1)} async-done(((bf16[4,128,2304]{2,1,0:T(8,128)(2,1)}), bf16[4,128,2304]{2,1,0:T(8,128)(2,1)}, u32[]{:S(2)}, u32[]{:S(2)}) %all-to-all-start.3) | async-done | bytes 2359328 | tf_op jit(solution)/shard_map/all_to_all | solution.py:105
  513.2 6.1 shard_map.258
  523.7 4.5 collective-permute-done.23.refs_2_
  533.1 4.9 all-to-all-start.6
  559.3 6.3 %shard_map.262 = (f32[64,6144]{1,0:T(8,128)}, f32[64,6144]{1,0:T(8,128)}, f32[64,6144]{1,0:T(8,128)}) custom-call(s32[2]{0:T(128)S(1)} %copy-done.33, bf16[4,64,2304]{2,1,0:T(8,128)(2,1)S(1)} %get-tuple-element.114.keep_ref, bf16[4,64,2304]{2,1,0:T(8,128)(2,1)} %collective-permute-done.25.got_ref), custom_call_target="tpu_custom_call" | custom-call | tf_op jit(solution)/shard_map/pallas_call | solution.py:355
  565.7 7.0 %collective-permute-done.30 = f32[136]{0:T(256)S(1)} collective-permute-done((f32[136]{0:T(256)S(1)}, f32[136]{0:T(256)S(1)}, u32[]{:S(2)}, u32[]{:S(2)}) %collective-permute-start.30) | collective-permute-done | bytes 576 | tf_op jit(solution)/shard_map/ppermute | solution.py:99
  572.6 14.3 %collective-permute-done.31 = f32[136]{0:T(256)S(1)} collective-permute-done((f32[136]{0:T(256)S(1)}, f32[136]{0:T(256)S(1)}, u32[]{:S(2)}, u32[]{:S(2)}) %collective-permute-start.31) | collective-permute-done | bytes 576 | tf_op jit(solution)/shard_map/ppermute | solution.py:99
  598.2 12.0 %all-to-all-done.7 = bf16[4,128,512]{2,1,0:T(8,128)(2,1)S(1)} async-done(((bf16[4,128,512]{2,1,0:T(8,128)(2,1)}), bf16[4,128,512]{2,1,0:T(8,128)(2,1)S(1)}, u32[]{:S(2)}, u32[]{:S(2)}) %all-to-all-start.7) | async-done | bytes 524320 | tf_op jit(solution)/shard_map/all_to_all | solution.py:105
  (505 shorter events, 220.1 us)
Async XLA Ops:
  7.2 131.6 %all-gather.4.cloned.1.call-start = ((), (), s32[]{:S(2)}) async-start(), calls=%async_computation.12 | async-start | bytes 8650752 | tf_op jit(solution)/shard_map/all_gather | solution.py:525
  7.9 68.2 %collective-permute-start.1 = (bf16[128,2048]{1,0:T(8,128)(2,1)}, bf16[128,2048]{1,0:T(8,128)(2,1)S(1)}, u32[]{:S(2)}, u32[]{:S(2)}) collective-permute-start(bf16[128,2048]{1,0:T(8,128)(2,1)} %bitcast.280), channel_id=1, source_target_pairs={{0,16},{1,17},{2,18},{3,19},{4,20},{5,21},{6,22},{7,23},{8,24},{9,... | collective-permute-start | bytes 1572872 | tf_op jit(solution)/shard_map/ppermute | solution.py:99
  12.0 73.7 %collective-permute-start = (bf16[128,2048]{1,0:T(8,128)(2,1)}, bf16[128,2048]{1,0:T(8,128)(2,1)}, u32[]{:S(2)}, u32[]{:S(2)}) collective-permute-start(bf16[128,2048]{1,0:T(8,128)(2,1)} %bitcast.281), channel_id=1, source_target_pairs={{0,8},{1,9},{2,10},{3,11},{4,12},{5,13},{6,14},{7,15},{8,0},{9,1},... | collective-permute-start | bytes 1572872 | tf_op jit(solution)/shard_map/ppermute | solution.py:99
  37.0 31.3 %all-to-all-start = ((bf16[4,160,512]{2,1,0:T(8,128)(2,1)}), bf16[4,160,512]{2,1,0:T(8,128)(2,1)S(1)}, u32[]{:S(2)}, u32[]{:S(2)}) async-start(bf16[4,160,512]{2,1,0:T(8,128)(2,1)} %shard_map.240), calls=%async_computation | async-start | bytes 1310720 | tf_op jit(solution)/shard_map/all_to_all | solution.py:105
  68.3 70.5 %all-to-all-start.1 = ((bf16[4,128,1536]{2,1,0:T(8,128)(2,1)}), bf16[4,128,1536]{2,1,0:T(8,128)(2,1)}, u32[]{:S(2)}, u32[]{:S(2)}) async-start(bf16[4,128,1536]{2,1,0:T(8,128)(2,1)} %get-tuple-element.64), calls=%async_computation.1 | async-start | bytes 3145728 | tf_op jit(solution)/shard_map/all_to_all | solution.py:105
  72.7 150.2 %all-gather.6.cloned.1.call-start = ((), (), s32[]{:S(2)}) async-start(), calls=%async_computation.13 | async-start | bytes 7864320 | tf_op jit(solution)/shard_map/all_gather | solution.py:108
  76.1 56.3 %collective-permute-start.2 = (bf16[128,2048]{1,0:T(8,128)(2,1)S(1)}, bf16[128,2048]{1,0:T(8,128)(2,1)S(1)}, u32[]{:S(2)}, u32[]{:S(2)}) collective-permute-start(bf16[128,2048]{1,0:T(8,128)(2,1)S(1)} %collective-permute-done.1.refs_2_), channel_id=1, source_target_pairs={{0,8},{1,9},{2,10},{3,11},{4,12},{5,13},{6,14},{7,15},{8,0},{9,1},... | collective-permute-start | bytes 1572872 | tf_op jit(solution)/shard_map/ppermute | solution.py:99
  78.9 56.8 %collective-permute-start.4 = (bf16[640,512]{1,0:T(8,128)(2,1)S(1)}, bf16[640,512]{1,0:T(8,128)(2,1)S(1)}, u32[]{:S(2)}, u32[]{:S(2)}) collective-permute-start(bf16[640,512]{1,0:T(8,128)(2,1)S(1)} %bitcast.283), channel_id=1, source_target_pairs={{0,2},{1,3},{2,0},{3,1},{4,6},{5,7},{6,4},{7,5},{8,10},{9,11},{10,... | collective-permute-start | bytes 1966088 | tf_op jit(solution)/shard_map/ppermute | solution.py:99
  80.5 55.2 %collective-permute-start.5 = (bf16[640,512]{1,0:T(8,128)(2,1)S(1)}, bf16[640,512]{1,0:T(8,128)(2,1)S(1)}, u32[]{:S(2)}, u32[]{:S(2)}) collective-permute-start(bf16[640,512]{1,0:T(8,128)(2,1)S(1)} %bitcast.284), channel_id=1, source_target_pairs={{0,4},{1,5},{2,6},{3,7},{4,0},{5,1},{6,2},{7,3},{8,12},{9,13},{10,... | collective-permute-start | bytes 1966088 | tf_op jit(solution)/shard_map/ppermute | solution.py:99
  82.0 53.7 %collective-permute-start.6 = (bf16[640,512]{1,0:T(8,128)(2,1)S(1)}, bf16[640,512]{1,0:T(8,128)(2,1)S(1)}, u32[]{:S(2)}, u32[]{:S(2)}) collective-permute-start(bf16[640,512]{1,0:T(8,128)(2,1)S(1)} %bitcast.285), channel_id=1, source_target_pairs={{0,6},{1,7},{2,4},{3,5},{4,2},{5,3},{6,0},{7,1},{8,14},{9,15},{10,... | collective-permute-start | bytes 1966088 | tf_op jit(solution)/shard_map/ppermute | solution.py:99
  147.4 47.2 %all-to-all-start.2 = ((bf16[4,128,768]{2,1,0:T(8,128)(2,1)}), bf16[4,128,768]{2,1,0:T(8,128)(2,1)}, u32[]{:S(2)}, u32[]{:S(2)}) async-start(bf16[4,128,768]{2,1,0:T(8,128)(2,1)} %get-tuple-element.65), calls=%async_computation.2 | async-start | bytes 1572864 | tf_op jit(solution)/shard_map/all_to_all | solution.py:105
  151.7 125.7 %all-gather.8.cloned.1.call-start = ((), (), s32[]{:S(2)}) async-start(), calls=%async_computation.14 | async-start | bytes 3932160 | tf_op jit(solution)/shard_map/all_gather | solution.py:108
  161.5 18.1 %collective-permute-start.8 = (bf16[1024,256]{1,0:T(8,128)(2,1)}, bf16[1024,256]{1,0:T(8,128)(2,1)}, u32[]{:S(2)}, u32[]{:S(2)}) collective-permute-start(bf16[1024,256]{1,0:T(8,128)(2,1)} %pad_maximum_fusion.6), channel_id=1, source_target_pairs={{0,4},{1,5},{2,6},{3,7},{4,0},{5,1},{6,2},{7,3},{8,12},{9,13},{10,... | collective-permute-start | bytes 1572872 | tf_op jit(solution)/shard_map/ppermute | solution.py:99
  194.6 25.4 %collective-permute-start.11 = (bf16[512,512]{1,0:T(8,128)(2,1)S(1)}, bf16[512,512]{1,0:T(8,128)(2,1)S(1)}, u32[]{:S(2)}, u32[]{:S(2)}) collective-permute-start(bf16[512,512]{1,0:T(8,128)(2,1)S(1)} %pad_maximum_fusion.7.refs_0_), channel_id=1, source_target_pairs={{0,8},{1,9},{2,10},{3,11},{4,12},{5,13},{6,14},{7,15},{8,0},{9,1},... | collective-permute-start | bytes 1572872 | tf_op jit(solution)/shard_map/ppermute | solution.py:99
  196.3 26.3 %collective-permute-start.12 = (bf16[512,512]{1,0:T(8,128)(2,1)S(1)}, bf16[512,512]{1,0:T(8,128)(2,1)}, u32[]{:S(2)}, u32[]{:S(2)}) collective-permute-start(bf16[512,512]{1,0:T(8,128)(2,1)S(1)} %pad_maximum_fusion.7.refs_0_), channel_id=1, source_target_pairs={{0,16},{1,17},{2,18},{3,19},{4,20},{5,21},{6,22},{7,23},{8,24},{9,... | collective-permute-start | bytes 1572872 | tf_op jit(solution)/shard_map/ppermute | solution.py:99
  222.9 213.7 %reduce-scatter.5.cloned.1.call-start = ((), (), s32[]{:S(2)}) async-start(), calls=%async_computation.15 | async-start | bytes 11796480 | tf_op jit(solution)/shard_map/reduce_scatter | solution.py:111
  235.0 24.5 %collective-permute-start.15 = (bf16[128,2048]{1,0:T(8,128)(2,1)S(1)}, bf16[128,2048]{1,0:T(8,128)(2,1)S(1)}, u32[]{:S(2)}, u32[]{:S(2)}) collective-permute-start(bf16[128,2048]{1,0:T(8,128)(2,1)S(1)} %shard_map.246.refs_0_), channel_id=1, source_target_pairs={{0,16},{1,17},{2,18},{3,19},{4,20},{5,21},{6,22},{7,23},{8,24},{9,... | collective-permute-start | bytes 1572872 | tf_op jit(solution)/shard_map/ppermute | solution.py:99
  237.4 23.7 %collective-permute-start.14 = (bf16[128,2048]{1,0:T(8,128)(2,1)S(1)}, bf16[128,2048]{1,0:T(8,128)(2,1)S(1)}, u32[]{:S(2)}, u32[]{:S(2)}) collective-permute-start(bf16[128,2048]{1,0:T(8,128)(2,1)S(1)} %shard_map.246.refs_0_), channel_id=1, source_target_pairs={{0,8},{1,9},{2,10},{3,11},{4,12},{5,13},{6,14},{7,15},{8,0},{9,1},... | collective-permute-start | bytes 1572872 | tf_op jit(solution)/shard_map/ppermute | solution.py:99
  334.0 54.8 %all-to-all-start.4 = ((bf16[4,128,2048]{2,1,0:T(8,128)(2,1)}), bf16[4,128,2048]{2,1,0:T(8,128)(2,1)S(1)}, u32[]{:S(2)}, u32[]{:S(2)}) async-start(bf16[4,128,2048]{2,1,0:T(8,128)(2,1)} %bitcast.49), calls=%async_computation.5 | async-start | bytes 4194304 | tf_op jit(solution)/shard_map/all_to_all | solution.py:105
  399.2 29.8 %all-to-all-start.5 = ((bf16[4,128,1024]{2,1,0:T(8,128)(2,1)}), bf16[4,128,1024]{2,1,0:T(8,128)(2,1)}, u32[]{:S(2)}, u32[]{:S(2)}) async-start(bf16[4,128,1024]{2,1,0:T(8,128)(2,1)} %copy-done.12), calls=%async_computation.6 | async-start | bytes 2097152 | tf_op jit(solution)/shard_map/all_to_all | solution.py:105
  403.7 75.3 %reduce-scatter.7.cloned.1.call-start = ((), (), s32[]{:S(2)}) async-start(), calls=%async_computation.16 | async-start | bytes 2359296 | tf_op jit(solution)/shard_map/reduce_scatter | solution.py:111
  409.0 52.3 %collective-permute-start.20 = (bf16[512,2048]{1,0:T(8,128)(2,1)}, bf16[512,2048]{1,0:T(8,128)(2,1)S(1)}, u32[]{:S(2)}, u32[]{:S(2)}) collective-permute-start(bf16[512,2048]{1,0:T(8,128)(2,1)} %shard_map.252), channel_id=1, source_target_pairs={{0,1},{1,0},{2,3},{3,2},{4,5},{5,4},{6,7},{7,6},{8,9},{9,8},{10,11... | collective-permute-start | bytes 6291464 | tf_op jit(solution)/shard_map/ppermute | solution.py:99
  430.9 18.3 %collective-permute-start.21 = (bf16[512,256]{1,0:T(8,128)(2,1)}, bf16[512,256]{1,0:T(8,128)(2,1)}, u32[]{:S(2)}, u32[]{:S(2)}) collective-permute-start(bf16[512,256]{1,0:T(8,128)(2,1)} %get-tuple-element.126), channel_id=1, source_target_pairs={{0,1},{1,0},{2,3},{3,2},{4,5},{5,4},{6,7},{7,6},{8,9},{9,8},{10,11... | collective-permute-start | bytes 786440 | tf_op jit(solution)/shard_map/ppermute | solution.py:99
  436.6 59.5 %all-to-all-start.3 = ((bf16[4,128,2304]{2,1,0:T(8,128)(2,1)}), bf16[4,128,2304]{2,1,0:T(8,128)(2,1)}, u32[]{:S(2)}, u32[]{:S(2)}) async-start(bf16[4,128,2304]{2,1,0:T(8,128)(2,1)} %bitcast.293), calls=%async_computation.4 | async-start | bytes 4718592 | tf_op jit(solution)/shard_map/all_to_all | solution.py:105
  441.3 146.9 %reduce-scatter.9.cloned.1.call-start = ((), (), s32[]{:S(2)}) async-start(), calls=%async_computation.17 | async-start | bytes 2621440 | tf_op jit(solution)/shard_map/reduce_scatter | solution.py:111
  458.2 17.5 %collective-permute-start.22 = (bf16[1024,256]{1,0:T(8,128)(2,1)}, bf16[1024,256]{1,0:T(8,128)(2,1)}, u32[]{:S(2)}, u32[]{:S(2)}) collective-permute-start(bf16[1024,256]{1,0:T(8,128)(2,1)} %pad_maximum_fusion.8), channel_id=1, source_target_pairs={{0,4},{1,5},{2,6},{3,7},{4,0},{5,1},{6,2},{7,3},{8,12},{9,13},{10,... | collective-permute-start | bytes 1572872 | tf_op jit(solution)/shard_map/ppermute | solution.py:99
  496.1 96.5 %reduce-scatter.11.cloned.1.call-start = ((), (), s32[]{:S(2)}) async-start(), calls=%async_computation.18 | async-start | bytes 2621440 | tf_op jit(solution)/shard_map/reduce_scatter | solution.py:111
  533.1 56.3 %all-to-all-start.6 = ((bf16[4,128,2048]{2,1,0:T(8,128)(2,1)}), bf16[4,128,2048]{2,1,0:T(8,128)(2,1)}, u32[]{:S(2)}, u32[]{:S(2)}) async-start(bf16[4,128,2048]{2,1,0:T(8,128)(2,1)} %bitcast.279), calls=%async_computation.9 | async-start | bytes 4194304 | tf_op jit(solution)/shard_map/all_to_all | solution.py:105
  554.0 18.6 %collective-permute-start.30 = (f32[136]{0:T(256)S(1)}, f32[136]{0:T(256)S(1)}, u32[]{:S(2)}, u32[]{:S(2)}) collective-permute-start(f32[136]{0:T(256)S(1)} %bitcast.317), channel_id=1, source_target_pairs={{0,8},{1,9},{2,10},{3,11},{4,12},{5,13},{6,14},{7,15},{8,0},{9,1},... | collective-permute-start | bytes 1640 | tf_op jit(solution)/shard_map/ppermute | solution.py:99
  556.0 30.9 %collective-permute-start.31 = (f32[136]{0:T(256)S(1)}, f32[136]{0:T(256)S(1)}, u32[]{:S(2)}, u32[]{:S(2)}) collective-permute-start(f32[136]{0:T(256)S(1)} %bitcast.316), channel_id=1, source_target_pairs={{0,16},{1,17},{2,18},{3,19},{4,20},{5,21},{6,22},{7,23},{8,24},{9,... | collective-permute-start | bytes 1640 | tf_op jit(solution)/shard_map/ppermute | solution.py:99
  558.4 28.5 %collective-permute-start.32 = (f32[136]{0:T(256)S(1)}, f32[136]{0:T(256)S(1)}, u32[]{:S(2)}, u32[]{:S(2)}) collective-permute-start(f32[136]{0:T(256)S(1)} %bitcast.315), channel_id=1, source_target_pairs={{0,24},{1,25},{2,26},{3,27},{4,28},{5,29},{6,30},{7,31},{8,16},{9,... | collective-permute-start | bytes 1640 | tf_op jit(solution)/shard_map/ppermute | solution.py:99
  592.6 17.7 %all-to-all-start.7 = ((bf16[4,128,512]{2,1,0:T(8,128)(2,1)}), bf16[4,128,512]{2,1,0:T(8,128)(2,1)S(1)}, u32[]{:S(2)}, u32[]{:S(2)}) async-start(bf16[4,128,512]{2,1,0:T(8,128)(2,1)} %bitcast.301), calls=%async_computation.11 | async-start | bytes 1048576 | tf_op jit(solution)/shard_map/all_to_all | solution.py:105
  (130 other events, 1059.1 us)
Sparse Core Ops, SparseCore 0:
  10.9 117.0 all-gather.3
  139.0 73.0 all-gather.5
  223.1 43.2 all-gather.7
  334.1 96.2 reduce-scatter.4
  436.7 42.1 reduce-scatter.6
  496.3 41.9 reduce-scatter.8
  541.2 34.7 reduce-scatter.10

commit v5 on v4

--- a/solution.py
+++ b/solution.py
@@ -405,7 +405,7 @@
             out_specs=pl.BlockSpec((per_step * unit, sum(widths)), lambda i, s: (i, 0)),
         ),
         out_shape=like((width, sum(widths))),
-        compiler_params=pltpu.CompilerParams(vmem_limit_bytes=VMEM_BYTES),
+        compiler_params=pltpu.CompilerParams(vmem_limit_bytes=ALL_VMEM_BYTES),
     )(jnp.asarray(np.concatenate(orders), jnp.int32), *flat)
 
 
@@ -435,7 +435,7 @@
         + ([] if add is None else [block]),
         out_specs=block,
         out_shape=like((tokens, width)),
-        compiler_params=pltpu.CompilerParams(vmem_limit_bytes=VMEM_BYTES),
+        compiler_params=pltpu.CompilerParams(vmem_limit_bytes=ALL_VMEM_BYTES),
     )(*lefts, right, *([] if add is None else [add]))
 
 

time: 632 us -> 636 us (level)
  Pallas kernels: 101 us -> 113 us
  waiting for transfers between devices: 271 us -> 261 us
    pallas_call x6, Pallas kernels: 29.3 us -> 37.4 us  [product_t(): pl.pallas_call(body, grid=(width // rows,), in_specs=[pl.BlockSpec(left.s...]
    unnamed x234 -> x206, local copies, waits for them, and re-layouts: 24.7 us -> 21.6 us
  transfers between devices with their start and end apart: 48 -> 48, of which waited for: 22 -> 22; matrix products, arithmetic and copies ran while one was open for 21% -> 22% of each run, Pallas kernels for 9% -> 10%
where the time goes in v5:
time: 636 us; the launch traced here: 628 us
  waiting for transfers between devices  261 us (41%)
  Pallas kernels  113 us (18%)
  starting transfers between devices  66.2 us (10%)
  other arithmetic  57.8 us (9%)
  local copies, waits for them, and re-layouts  55.8 us (9%)
  matrix products  46.8 us (7%)
  between operations  26.9 us (4%)
    ppermute x33, waiting for transfers between devices, move(): return lax.ppermute(array, BOTH, route)  140 us
    all_to_all x8, waiting for transfers between devices, exchange_a(): lax.all_to_all(array, BOTH, 0, 0, axis_index_groups=self.groups('a'), til...  118 us
    pallas_call x6, Pallas kernels, product_t(): pl.pallas_call(body, grid=(width // rows,), in_specs=[pl.BlockSpec(left.s...  37.4 us
    all_to_all x8, starting transfers between devices, exchange_a(): lax.all_to_all(array, BOTH, 0, 0, axis_index_groups=self.groups('a'), til...  33.9 us
    ppermute x33, starting transfers between devices, move(): return lax.ppermute(array, BOTH, route)  32 us
    pallas_call x2, Pallas kernels, token_products(): pl.pallas_call(body, grid_spec=pltpu.PrefetchScalarGridSpec(num_scalar_pr...  26.3 us
    unnamed x206, local copies, waits for them, and re-layouts  21.6 us
    pallas_call x2, Pallas kernels, feed_forward(): pl.pallas_call(body, grid=(steps,), in_specs=[rows, pl.BlockSpec((width,...  20.6 us
  transfers between devices with their start and end apart: 48, of which 22 were waited for; matrix products, arithmetic and copies ran while one was open for 22% of the time, Pallas kernels for 10%

profile of v5, /device:TPU:0, one launch (start us, length us, event | category | flops | bytes accessed | tf_op | source)
XLA Modules:
  0.0 627.9 jit_solution(1964139951255138759)
XLA Ops:
  31.7 4.7 shard_map.242
  43.9 24.3 %all-to-all-done = bf16[4,160,512]{2,1,0:T(8,128)(2,1)S(1)} async-done(((bf16[4,160,512]{2,1,0:T(8,128)(2,1)}), bf16[4,160,512]{2,1,0:T(8,128)(2,1)S(1)}, u32[]{:S(2)}, u32[]{:S(2)}) %all-to-all-start) | async-done | bytes 655392 | tf_op jit(solution)/shard_map/all_to_all | solution.py:105
  68.2 4.4 all-to-all-start.1
  85.6 46.6 %collective-permute-done.2.refs_3_ = bf16[128,2048]{1,0:T(8,128)(2,1)S(1)} collective-permute-done((bf16[128,2048]{1,0:T(8,128)(2,1)S(1)}, bf16[128,2048]{1,0:T(8,128)(2,1)S(1)}, u32[]{:S(2)}, u32[]{:S(2)}) %collective-permute-start.2) | collective-permute-done | bytes 524320 | tf_op jit(solution)/shard_map/ppermute | solution.py:99
  173.6 5.9 collective-permute-done.8
  199.6 21.3 %collective-permute-done.11.refs_1_ = bf16[512,512]{1,0:T(8,128)(2,1)S(1)} collective-permute-done((bf16[512,512]{1,0:T(8,128)(2,1)S(1)}, bf16[512,512]{1,0:T(8,128)(2,1)S(1)}, u32[]{:S(2)}, u32[]{:S(2)}) %collective-permute-start.11) | collective-permute-done | bytes 524320 | tf_op jit(solution)/shard_map/ppermute | solution.py:99
  226.8 9.1 %collective-permute-done.13.refs_3_ = bf16[512,512]{1,0:T(8,128)(2,1)} collective-permute-done((bf16[512,512]{1,0:T(8,128)(2,1)}, bf16[512,512]{1,0:T(8,128)(2,1)}, u32[]{:S(2)}, u32[]{:S(2)}) %collective-permute-start.13) | collective-permute-done | bytes 524320 | tf_op jit(solution)/shard_map/ppermute | solution.py:99
  243.2 7.9 %multiply_reduce_fusion = (f32[512]{0:T(512)S(1)}, f32[512,2048]{1,0:T(8,128)S(1)}) fusion(bf16[512,2048]{1,0:T(8,128)(2,1)S(1)} %shard_map.244, bf16[2048,2048]{1,0:T(8,128)(2,1)} %all-gather.4.cloned.1.call-done, bf16[512,2048]{1,0:T(8,128)(2,1)S(1)} %shard_map.238), kind=kOutput, calls=%fused_computation.20 | convolution fusion | flops 4299161088 | bytes 16779264 | tf_op jit(solution)/shard_map/dot_general | solution.py:35
  251.1 9.3 %collective-permute-done.15.refs_2_ = bf16[128,2048]{1,0:T(8,128)(2,1)S(1)} collective-permute-done((bf16[128,2048]{1,0:T(8,128)(2,1)S(1)}, bf16[128,2048]{1,0:T(8,128)(2,1)S(1)}, u32[]{:S(2)}, u32[]{:S(2)}) %collective-permute-start.15) | collective-permute-done | bytes 524320 | tf_op jit(solution)/shard_map/ppermute | solution.py:99
  262.7 10.6 %collective-permute-done.16.refs_3_ = bf16[128,2048]{1,0:T(8,128)(2,1)S(1)} collective-permute-done((bf16[128,2048]{1,0:T(8,128)(2,1)S(1)}, bf16[128,2048]{1,0:T(8,128)(2,1)S(1)}, u32[]{:S(2)}, u32[]{:S(2)}) %collective-permute-start.16) | collective-permute-done | bytes 524320 | tf_op jit(solution)/shard_map/ppermute | solution.py:99
  278.3 10.3 %shard_map.249 = (bf16[512,768]{1,0:T(8,128)(2,1)}, bf16[512,768]{1,0:T(8,128)(2,1)}, bf16[512,768]{1,0:T(8,128)(2,1)}) custom-call(bf16[512,2048]{1,0:T(8,128)(2,1)} %copy-done.20, bf16[2048,1536]{1,0:T(8,128)(2,1)} %all-gather.6.cloned.1.call-done.gate_ref.up_ref.refs_2_, bf16[2048,1536]{1,0:T(8,128)(2,1)} %all-gather.6.cloned.1.call-done.gate_ref.up_ref.refs_2_, ...), custom_call_target="tpu_custom_call" | custom-call | tf_op jit(solution)/shard_map/pallas_call | solution.py:460
  288.6 7.5 %shard_map.250 = bf16[512,2048]{1,0:T(8,128)(2,1)} custom-call(bf16[512,768]{1,0:T(8,128)(2,1)} %get-tuple-element.80.refs_0_.refs_3_, bf16[512,768]{1,0:T(8,128)(2,1)} %get-tuple-element.81.refs_1_.refs_7_, bf16[2048,1536]{1,0:T(8,128)(2,1)} %all-gather.6.cloned.1.call-done.gate_ref.up_ref.refs_2_), custom_call_target="tpu_custom_call" | custom-call | tf_op jit(solution)/shard_map/pallas_call | solution.py:430
  296.2 10.3 %shard_map.248 = (bf16[512,768]{1,0:T(8,128)(2,1)}, bf16[512,768]{1,0:T(8,128)(2,1)}, bf16[512,768]{1,0:T(8,128)(2,1)}) custom-call(bf16[512,2048]{1,0:T(8,128)(2,1)} %copy-done, bf16[2048,1536]{1,0:T(8,128)(2,1)} %all-gather.6.cloned.1.call-done.gate_ref.up_ref.refs_2_, bf16[2048,1536]{1,0:T(8,128)(2,1)} %all-gather.6.cloned.1.call-done.gate_ref.up_ref.refs_2_, ...), custom_call_target="tpu_custom_call" | custom-call | tf_op jit(solution)/shard_map/pallas_call | solution.py:460
  307.9 7.8 %shard_map.251 = bf16[512,2048]{1,0:T(8,128)(2,1)} custom-call(bf16[512,768]{1,0:T(8,128)(2,1)} %get-tuple-element.78.refs_0_.refs_2_, bf16[512,768]{1,0:T(8,128)(2,1)} %get-tuple-element.79.refs_1_.refs_6_, bf16[2048,1536]{1,0:T(8,128)(2,1)} %all-gather.6.cloned.1.call-done.gate_ref.up_ref.refs_2_, bf16[512,2048]{1,0:T(8,128)(2,1)} %copy-done.61), custom_call_target="tpu_custom_call" | custom-call | tf_op jit(solution)/shard_map/pallas_call | solution.py:430
  315.6 19.0 %shard_map.254 = bf16[2048,2304]{1,0:T(8,128)(2,1)} custom-call(s32[48]{0:T(128)} %constant.279.clone.order_ref, bf16[512,2048]{1,0:T(8,128)(2,1)} %copy-done, bf16[512,2048]{1,0:T(8,128)(2,1)} %copy-done.20, bf16[512,768]{1,0:T(8,128)(2,1)} %get-tuple-element.78.refs_0_.refs_2_, bf16[512,768]{1,0:T(8,128)(2,1)} %get-tuple-element.80.refs_0_.refs_3_, ...), custom_call_target="tpu_custom_call" | custom-call | tf_op jit(solution)/shard_map/pallas_call | solution.py:399
  334.7 6.1 all-to-all-start.4
  341.6 47.9 %all-to-all-done.4 = bf16[4,128,2048]{2,1,0:T(8,128)(2,1)S(1)} async-done(((bf16[4,128,2048]{2,1,0:T(8,128)(2,1)}), bf16[4,128,2048]{2,1,0:T(8,128)(2,1)S(1)}, u32[]{:S(2)}, u32[]{:S(2)}) %all-to-all-start.4) | async-done | bytes 2097184 | tf_op jit(solution)/shard_map/all_to_all | solution.py:105
  394.0 4.8 convolution_convert_fusion.1.refs_0_
  404.8 5.6 shard_map.252
  410.4 18.3 %all-to-all-done.5 = bf16[4,128,1024]{2,1,0:T(8,128)(2,1)S(1)} async-done(((bf16[4,128,1024]{2,1,0:T(8,128)(2,1)}), bf16[4,128,1024]{2,1,0:T(8,128)(2,1)S(1)}, u32[]{:S(2)}, u32[]{:S(2)}) %all-to-all-start.5) | async-done | bytes 1048608 | tf_op jit(solution)/shard_map/all_to_all | solution.py:105
  461.4 6.3 %shard_map.253 = bf16[512,2048]{1,0:T(8,128)(2,1)} custom-call(bf16[512,768]{1,0:T(8,128)(2,1)} %get-tuple-element.82.refs_0_.refs_10_, bf16[2048,768]{1,0:T(8,128)(2,1)} %all-gather.8.cloned.1.call-done.down_ref.refs_1_, bf16[512,2048]{1,0:T(8,128)(2,1)} %collective-permute-done.20.refs_2_), custom_call_target="tpu_custom_call" | custom-call | tf_op jit(solution)/shard_map/pallas_call | solution.py:430
  469.8 4.6 collective-permute-done.22
  478.5 15.8 %all-to-all-done.3 = bf16[4,128,2304]{2,1,0:T(8,128)(2,1)S(1)} async-done(((bf16[4,128,2304]{2,1,0:T(8,128)(2,1)}), bf16[4,128,2304]{2,1,0:T(8,128)(2,1)S(1)}, u32[]{:S(2)}, u32[]{:S(2)}) %all-to-all-start.3) | async-done | bytes 2359328 | tf_op jit(solution)/shard_map/all_to_all | solution.py:105
  514.2 7.2 %shard_map.258 = bf16[2048,512]{1,0:T(8,128)(2,1)} custom-call(s32[16]{0:T(128)} %constant.280.clone.order_ref, bf16[512,2048]{1,0:T(8,128)(2,1)} %fusion.2.refs_0_, bf16[512,2048]{1,0:T(8,128)(2,1)} %collective-permute-done.7.refs_1_, bf16[512,512]{1,0:T(8,128)(2,1)} %get-tuple-element.89.refs_2_.refs_0_, bf16[512,512]{1,0:T(8,128)(2,1)} %get-tuple-element.90.refs_3_.refs_0_), custom_call_target="tpu_custom_call" | custom-call | tf_op jit(solution)/shard_map/pallas_call | solution.py:399
  521.4 5.0 shard_map.259
  526.4 4.3 collective-permute-done.23.refs_2_
  532.1 5.3 shard_map.260
  537.4 4.9 all-to-all-start.6
  563.6 6.3 %shard_map.262 = (f32[64,6144]{1,0:T(8,128)}, f32[64,6144]{1,0:T(8,128)}, f32[64,6144]{1,0:T(8,128)}) custom-call(s32[2]{0:T(128)S(1)} %copy-done.17, bf16[4,64,2304]{2,1,0:T(8,128)(2,1)S(1)} %get-tuple-element.114.keep_ref, bf16[4,64,2304]{2,1,0:T(8,128)(2,1)} %collective-permute-done.25.got_ref), custom_call_target="tpu_custom_call" | custom-call | tf_op jit(solution)/shard_map/pallas_call | solution.py:355
  569.9 7.0 %collective-permute-done.30 = f32[136]{0:T(256)S(1)} collective-permute-done((f32[136]{0:T(256)S(1)}, f32[136]{0:T(256)S(1)}, u32[]{:S(2)}, u32[]{:S(2)}) %collective-permute-start.30) | collective-permute-done | bytes 576 | tf_op jit(solution)/shard_map/ppermute | solution.py:99
  576.9 14.3 %collective-permute-done.31 = f32[136]{0:T(256)S(1)} collective-permute-done((f32[136]{0:T(256)S(1)}, f32[136]{0:T(256)S(1)}, u32[]{:S(2)}, u32[]{:S(2)}) %collective-permute-start.31) | collective-permute-done | bytes 576 | tf_op jit(solution)/shard_map/ppermute | solution.py:99
  602.4 12.1 %all-to-all-done.7 = bf16[4,128,512]{2,1,0:T(8,128)(2,1)S(1)} async-done(((bf16[4,128,512]{2,1,0:T(8,128)(2,1)}), bf16[4,128,512]{2,1,0:T(8,128)(2,1)S(1)}, u32[]{:S(2)}, u32[]{:S(2)}) %all-to-all-start.7) | async-done | bytes 524320 | tf_op jit(solution)/shard_map/all_to_all | solution.py:105
  (477 shorter events, 226.2 us)
Async XLA Ops:
  7.2 131.4 %all-gather.4.cloned.1.call-start = ((), (), s32[]{:S(2)}) async-start(), calls=%async_computation.12 | async-start | bytes 8650752 | tf_op jit(solution)/shard_map/all_gather | solution.py:525
  7.9 68.1 %collective-permute-start.1 = (bf16[128,2048]{1,0:T(8,128)(2,1)}, bf16[128,2048]{1,0:T(8,128)(2,1)S(1)}, u32[]{:S(2)}, u32[]{:S(2)}) collective-permute-start(bf16[128,2048]{1,0:T(8,128)(2,1)} %bitcast.279), channel_id=1, source_target_pairs={{0,16},{1,17},{2,18},{3,19},{4,20},{5,21},{6,22},{7,23},{8,24},{9,... | collective-permute-start | bytes 1572872 | tf_op jit(solution)/shard_map/ppermute | solution.py:99
  12.0 73.6 %collective-permute-start = (bf16[128,2048]{1,0:T(8,128)(2,1)}, bf16[128,2048]{1,0:T(8,128)(2,1)}, u32[]{:S(2)}, u32[]{:S(2)}) collective-permute-start(bf16[128,2048]{1,0:T(8,128)(2,1)} %bitcast.280), channel_id=1, source_target_pairs={{0,8},{1,9},{2,10},{3,11},{4,12},{5,13},{6,14},{7,15},{8,0},{9,1},... | collective-permute-start | bytes 1572872 | tf_op jit(solution)/shard_map/ppermute | solution.py:99
  36.9 31.3 %all-to-all-start = ((bf16[4,160,512]{2,1,0:T(8,128)(2,1)}), bf16[4,160,512]{2,1,0:T(8,128)(2,1)S(1)}, u32[]{:S(2)}, u32[]{:S(2)}) async-start(bf16[4,160,512]{2,1,0:T(8,128)(2,1)} %shard_map.240), calls=%async_computation | async-start | bytes 1310720 | tf_op jit(solution)/shard_map/all_to_all | solution.py:105
  68.2 70.4 %all-to-all-start.1 = ((bf16[4,128,1536]{2,1,0:T(8,128)(2,1)}), bf16[4,128,1536]{2,1,0:T(8,128)(2,1)}, u32[]{:S(2)}, u32[]{:S(2)}) async-start(bf16[4,128,1536]{2,1,0:T(8,128)(2,1)} %get-tuple-element.64), calls=%async_computation.1 | async-start | bytes 3145728 | tf_op jit(solution)/shard_map/all_to_all | solution.py:105
  72.6 151.3 %all-gather.6.cloned.1.call-start = ((), (), s32[]{:S(2)}) async-start(), calls=%async_computation.13 | async-start | bytes 7864320 | tf_op jit(solution)/shard_map/all_gather | solution.py:108
  76.0 56.1 %collective-permute-start.2 = (bf16[128,2048]{1,0:T(8,128)(2,1)S(1)}, bf16[128,2048]{1,0:T(8,128)(2,1)S(1)}, u32[]{:S(2)}, u32[]{:S(2)}) collective-permute-start(bf16[128,2048]{1,0:T(8,128)(2,1)S(1)} %collective-permute-done.1.refs_2_), channel_id=1, source_target_pairs={{0,8},{1,9},{2,10},{3,11},{4,12},{5,13},{6,14},{7,15},{8,0},{9,1},... | collective-permute-start | bytes 1572872 | tf_op jit(solution)/shard_map/ppermute | solution.py:99
  78.9 56.6 %collective-permute-start.4 = (bf16[640,512]{1,0:T(8,128)(2,1)S(1)}, bf16[640,512]{1,0:T(8,128)(2,1)S(1)}, u32[]{:S(2)}, u32[]{:S(2)}) collective-permute-start(bf16[640,512]{1,0:T(8,128)(2,1)S(1)} %bitcast.282), channel_id=1, source_target_pairs={{0,2},{1,3},{2,0},{3,1},{4,6},{5,7},{6,4},{7,5},{8,10},{9,11},{10,... | collective-permute-start | bytes 1966088 | tf_op jit(solution)/shard_map/ppermute | solution.py:99
  80.4 55.0 %collective-permute-start.5 = (bf16[640,512]{1,0:T(8,128)(2,1)S(1)}, bf16[640,512]{1,0:T(8,128)(2,1)S(1)}, u32[]{:S(2)}, u32[]{:S(2)}) collective-permute-start(bf16[640,512]{1,0:T(8,128)(2,1)S(1)} %bitcast.283), channel_id=1, source_target_pairs={{0,4},{1,5},{2,6},{3,7},{4,0},{5,1},{6,2},{7,3},{8,12},{9,13},{10,... | collective-permute-start | bytes 1966088 | tf_op jit(solution)/shard_map/ppermute | solution.py:99
  81.9 53.6 %collective-permute-start.6 = (bf16[640,512]{1,0:T(8,128)(2,1)S(1)}, bf16[640,512]{1,0:T(8,128)(2,1)S(1)}, u32[]{:S(2)}, u32[]{:S(2)}) collective-permute-start(bf16[640,512]{1,0:T(8,128)(2,1)S(1)} %bitcast.284), channel_id=1, source_target_pairs={{0,6},{1,7},{2,4},{3,5},{4,2},{5,3},{6,0},{7,1},{8,14},{9,15},{10,... | collective-permute-start | bytes 1966088 | tf_op jit(solution)/shard_map/ppermute | solution.py:99
  147.1 48.4 %all-to-all-start.2 = ((bf16[4,128,768]{2,1,0:T(8,128)(2,1)}), bf16[4,128,768]{2,1,0:T(8,128)(2,1)}, u32[]{:S(2)}, u32[]{:S(2)}) async-start(bf16[4,128,768]{2,1,0:T(8,128)(2,1)} %get-tuple-element.65), calls=%async_computation.2 | async-start | bytes 1572864 | tf_op jit(solution)/shard_map/all_to_all | solution.py:105
  151.4 126.9 %all-gather.8.cloned.1.call-start = ((), (), s32[]{:S(2)}) async-start(), calls=%async_computation.14 | async-start | bytes 3932160 | tf_op jit(solution)/shard_map/all_gather | solution.py:108
  161.2 18.3 %collective-permute-start.8 = (bf16[1024,256]{1,0:T(8,128)(2,1)}, bf16[1024,256]{1,0:T(8,128)(2,1)}, u32[]{:S(2)}, u32[]{:S(2)}) collective-permute-start(bf16[1024,256]{1,0:T(8,128)(2,1)} %pad_maximum_fusion.6), channel_id=1, source_target_pairs={{0,4},{1,5},{2,6},{3,7},{4,0},{5,1},{6,2},{7,3},{8,12},{9,13},{10,... | collective-permute-start | bytes 1572872 | tf_op jit(solution)/shard_map/ppermute | solution.py:99
  195.6 25.4 %collective-permute-start.11 = (bf16[512,512]{1,0:T(8,128)(2,1)S(1)}, bf16[512,512]{1,0:T(8,128)(2,1)S(1)}, u32[]{:S(2)}, u32[]{:S(2)}) collective-permute-start(bf16[512,512]{1,0:T(8,128)(2,1)S(1)} %pad_maximum_fusion.7.refs_0_), channel_id=1, source_target_pairs={{0,8},{1,9},{2,10},{3,11},{4,12},{5,13},{6,14},{7,15},{8,0},{9,1},... | collective-permute-start | bytes 1572872 | tf_op jit(solution)/shard_map/ppermute | solution.py:99
  197.2 26.3 %collective-permute-start.12 = (bf16[512,512]{1,0:T(8,128)(2,1)S(1)}, bf16[512,512]{1,0:T(8,128)(2,1)}, u32[]{:S(2)}, u32[]{:S(2)}) collective-permute-start(bf16[512,512]{1,0:T(8,128)(2,1)S(1)} %pad_maximum_fusion.7.refs_0_), channel_id=1, source_target_pairs={{0,16},{1,17},{2,18},{3,19},{4,20},{5,21},{6,22},{7,23},{8,24},{9,... | collective-permute-start | bytes 1572872 | tf_op jit(solution)/shard_map/ppermute | solution.py:99
  223.9 211.9 %reduce-scatter.5.cloned.1.call-start = ((), (), s32[]{:S(2)}) async-start(), calls=%async_computation.15 | async-start | bytes 11796480 | tf_op jit(solution)/shard_map/reduce_scatter | solution.py:111
  236.0 24.4 %collective-permute-start.15 = (bf16[128,2048]{1,0:T(8,128)(2,1)S(1)}, bf16[128,2048]{1,0:T(8,128)(2,1)S(1)}, u32[]{:S(2)}, u32[]{:S(2)}) collective-permute-start(bf16[128,2048]{1,0:T(8,128)(2,1)S(1)} %shard_map.246.refs_0_), channel_id=1, source_target_pairs={{0,16},{1,17},{2,18},{3,19},{4,20},{5,21},{6,22},{7,23},{8,24},{9,... | collective-permute-start | bytes 1572872 | tf_op jit(solution)/shard_map/ppermute | solution.py:99
  238.4 24.3 %collective-permute-start.14 = (bf16[128,2048]{1,0:T(8,128)(2,1)S(1)}, bf16[128,2048]{1,0:T(8,128)(2,1)S(1)}, u32[]{:S(2)}, u32[]{:S(2)}) collective-permute-start(bf16[128,2048]{1,0:T(8,128)(2,1)S(1)} %shard_map.246.refs_0_), channel_id=1, source_target_pairs={{0,8},{1,9},{2,10},{3,11},{4,12},{5,13},{6,14},{7,15},{8,0},{9,1},... | collective-permute-start | bytes 1572872 | tf_op jit(solution)/shard_map/ppermute | solution.py:99
  334.7 54.8 %all-to-all-start.4 = ((bf16[4,128,2048]{2,1,0:T(8,128)(2,1)}), bf16[4,128,2048]{2,1,0:T(8,128)(2,1)S(1)}, u32[]{:S(2)}, u32[]{:S(2)}) async-start(bf16[4,128,2048]{2,1,0:T(8,128)(2,1)} %bitcast.291), calls=%async_computation.5 | async-start | bytes 4194304 | tf_op jit(solution)/shard_map/all_to_all | solution.py:105
  399.9 28.8 %all-to-all-start.5 = ((bf16[4,128,1024]{2,1,0:T(8,128)(2,1)}), bf16[4,128,1024]{2,1,0:T(8,128)(2,1)S(1)}, u32[]{:S(2)}, u32[]{:S(2)}) async-start(bf16[4,128,1024]{2,1,0:T(8,128)(2,1)} %shard_map.256), calls=%async_computation.6 | async-start | bytes 2097152 | tf_op jit(solution)/shard_map/all_to_all | solution.py:105
  403.5 75.0 %reduce-scatter.7.cloned.1.call-start = ((), (), s32[]{:S(2)}) async-start(), calls=%async_computation.16 | async-start | bytes 2359296 | tf_op jit(solution)/shard_map/reduce_scatter | solution.py:111
  410.4 51.0 %collective-permute-start.20 = (bf16[512,2048]{1,0:T(8,128)(2,1)}, bf16[512,2048]{1,0:T(8,128)(2,1)}, u32[]{:S(2)}, u32[]{:S(2)}) collective-permute-start(bf16[512,2048]{1,0:T(8,128)(2,1)} %shard_map.252), channel_id=1, source_target_pairs={{0,1},{1,0},{2,3},{3,2},{4,5},{5,4},{6,7},{7,6},{8,9},{9,8},{10,11... | collective-permute-start | bytes 6291464 | tf_op jit(solution)/shard_map/ppermute | solution.py:99
  435.8 58.5 %all-to-all-start.3 = ((bf16[4,128,2304]{2,1,0:T(8,128)(2,1)}), bf16[4,128,2304]{2,1,0:T(8,128)(2,1)S(1)}, u32[]{:S(2)}, u32[]{:S(2)}) async-start(bf16[4,128,2304]{2,1,0:T(8,128)(2,1)} %bitcast.295), calls=%async_computation.4 | async-start | bytes 4718592 | tf_op jit(solution)/shard_map/all_to_all | solution.py:105
  439.6 152.8 %reduce-scatter.9.cloned.1.call-start = ((), (), s32[]{:S(2)}) async-start(), calls=%async_computation.17 | async-start | bytes 2621440 | tf_op jit(solution)/shard_map/reduce_scatter | solution.py:111
  456.7 17.7 %collective-permute-start.22 = (bf16[1024,256]{1,0:T(8,128)(2,1)}, bf16[1024,256]{1,0:T(8,128)(2,1)}, u32[]{:S(2)}, u32[]{:S(2)}) collective-permute-start(bf16[1024,256]{1,0:T(8,128)(2,1)} %pad_maximum_fusion.8), channel_id=1, source_target_pairs={{0,4},{1,5},{2,6},{3,7},{4,0},{5,1},{6,2},{7,3},{8,12},{9,13},{10,... | collective-permute-start | bytes 1572872 | tf_op jit(solution)/shard_map/ppermute | solution.py:99
  494.3 102.5 %reduce-scatter.11.cloned.1.call-start = ((), (), s32[]{:S(2)}) async-start(), calls=%async_computation.18 | async-start | bytes 2621440 | tf_op jit(solution)/shard_map/reduce_scatter | solution.py:111
  537.4 56.3 %all-to-all-start.6 = ((bf16[4,128,2048]{2,1,0:T(8,128)(2,1)}), bf16[4,128,2048]{2,1,0:T(8,128)(2,1)}, u32[]{:S(2)}, u32[]{:S(2)}) async-start(bf16[4,128,2048]{2,1,0:T(8,128)(2,1)} %bitcast.289), calls=%async_computation.9 | async-start | bytes 4194304 | tf_op jit(solution)/shard_map/all_to_all | solution.py:105
  547.3 16.3 %collective-permute-start.25 = (bf16[4,64,2304]{2,1,0:T(8,128)(2,1)}, bf16[4,64,2304]{2,1,0:T(8,128)(2,1)}, u32[]{:S(2)}, u32[]{:S(2)}) collective-permute-start(bf16[4,64,2304]{2,1,0:T(8,128)(2,1)} %get-tuple-element.113), channel_id=1, source_target_pairs={{0,1},{1,0},{2,3},{3,2},{4,5},{5,4},{6,7},{7,6},{8,9},{9,8},{10,11... | collective-permute-start | bytes 3538952 | tf_op jit(solution)/shard_map/ppermute | solution.py:99
  558.2 18.7 %collective-permute-start.30 = (f32[136]{0:T(256)S(1)}, f32[136]{0:T(256)S(1)}, u32[]{:S(2)}, u32[]{:S(2)}) collective-permute-start(f32[136]{0:T(256)S(1)} %bitcast.321), channel_id=1, source_target_pairs={{0,8},{1,9},{2,10},{3,11},{4,12},{5,13},{6,14},{7,15},{8,0},{9,1},... | collective-permute-start | bytes 1640 | tf_op jit(solution)/shard_map/ppermute | solution.py:99
  560.2 30.9 %collective-permute-start.31 = (f32[136]{0:T(256)S(1)}, f32[136]{0:T(256)S(1)}, u32[]{:S(2)}, u32[]{:S(2)}) collective-permute-start(f32[136]{0:T(256)S(1)} %bitcast.320), channel_id=1, source_target_pairs={{0,16},{1,17},{2,18},{3,19},{4,20},{5,21},{6,22},{7,23},{8,24},{9,... | collective-permute-start | bytes 1640 | tf_op jit(solution)/shard_map/ppermute | solution.py:99
  562.6 28.6 %collective-permute-start.32 = (f32[136]{0:T(256)S(1)}, f32[136]{0:T(256)S(1)}, u32[]{:S(2)}, u32[]{:S(2)}) collective-permute-start(f32[136]{0:T(256)S(1)} %bitcast.319), channel_id=1, source_target_pairs={{0,24},{1,25},{2,26},{3,27},{4,28},{5,29},{6,30},{7,31},{8,16},{9,... | collective-permute-start | bytes 1640 | tf_op jit(solution)/shard_map/ppermute | solution.py:99
  596.8 17.7 %all-to-all-start.7 = ((bf16[4,128,512]{2,1,0:T(8,128)(2,1)}), bf16[4,128,512]{2,1,0:T(8,128)(2,1)S(1)}, u32[]{:S(2)}, u32[]{:S(2)}) async-start(bf16[4,128,512]{2,1,0:T(8,128)(2,1)} %bitcast.305), calls=%async_computation.11 | async-start | bytes 1048576 | tf_op jit(solution)/shard_map/all_to_all | solution.py:105
  (116 other events, 1039.0 us)
Sparse Core Ops, SparseCore 0:
  10.9 116.6 all-gather.3
  138.7 73.2 all-gather.5
  224.0 43.2 all-gather.7
  334.8 96.2 reduce-scatter.4
  435.9 42.5 reduce-scatter.6
  494.5 41.9 reduce-scatter.8
  539.4 34.6 reduce-scatter.10
